TPU v7x, 32 devices: a whole 2x2x4 slice. The times are simulated.
32 devices in a mesh: grp: 4 (over x, core), wide: 8 (over z, y).
Axes of the slice: x: 2, y: 2, z: 4, core: 2. Of those that a mesh axis runs over, the one named last changes fastest.
Arguments:
- tokens: bfloat16 [8192, 2048], P(('grp', 'wide')), may hold values from -6 to 6
- lengths: int32 [32], P(('grp', 'wide')), may hold values from 1 to 256, 6144 in all
- cotangent: bfloat16 [8192, 2048], P(('grp', 'wide')), may hold values from -6 to 6
- norm_gain: float32 [2048], P(('grp', 'wide')), may hold values from 0.25 to 1.75
- conv_weight: float32 [2048, 3], P(('grp', 'wide')), may hold values from -3.5 to 3.5
- w_query: float32 [2048, 256], P(('grp', 'wide')), may hold values from -0.125 to 0.125
- w_key: float32 [2048, 256], P(('grp', 'wide')), may hold values from -0.125 to 0.125
- w_value: float32 [2048, 2048], P(('grp', 'wide')), may hold values from -0.125 to 0.125
- w_query_window: float32 [2048, 2048], P(('grp', 'wide')), may hold values from -0.125 to 0.125
- w_key_window: float32 [2048, 2048], P(('grp', 'wide')), may hold values from -0.125 to 0.125
- w_out: float32 [2048, 2048], P(('grp', 'wide')), may hold values from -0.375 to 0.375
- ffn_gain: float32 [2048], P(('grp', 'wide')), may hold values from 0.25 to 1.75
- w_gate: float32 [2048, 5504], P(('grp', 'wide')), may hold values from -0.125 to 0.125
- w_up: float32 [2048, 5504], P(('grp', 'wide')), may hold values from -0.125 to 0.125
- w_down: float32 [5504, 2048], P(('grp', 'wide')), may hold values from -0.078125 to 0.078125
Outputs:
- block_out: bfloat16 [8192, 2048], P(('grp', 'wide'))
- grad_tokens: bfloat16 [8192, 2048], P(('grp', 'wide'))
- grad_norm_gain: float32 [2048], P(('grp', 'wide'))
- grad_conv: float32 [2048, 3], P(('grp', 'wide'))
- grad_query: float32 [2048, 256], P(('grp', 'wide'))
- grad_key: float32 [2048, 256], P(('grp', 'wide'))
- grad_value: float32 [2048, 2048], P(('grp', 'wide'))
- grad_query_window: float32 [2048, 2048], P(('grp', 'wide'))
- grad_key_window: float32 [2048, 2048], P(('grp', 'wide'))
- grad_out: float32 [2048, 2048], P(('grp', 'wide'))
- grad_ffn_gain: float32 [2048], P(('grp', 'wide'))
- grad_gate: float32 [2048, 5504], P(('grp', 'wide'))
- grad_up: float32 [2048, 5504], P(('grp', 'wide'))
- grad_down: float32 [5504, 2048], P(('grp', 'wide'))
Inputs may be any that keep to these rules, and one draw needn't show every extreme that they name: lengths[b] is the number of real tokens in slot b; at least one slot is full with 256.
All inputs are finite; a program needn't handle non-finite values. No bound on the sum of `lengths` on one device may be relied on, other than what follows from the above.
Results may differ from a plain program's by a relative error of at most 0.017.
The roundings to bfloat16 on the way count: a program that leaves them out, or rounds other values in their place, can miss the bound.
Values may be sent and summed in bfloat16 or wider, within the bound.
No kernel may reach another device: no remote copies, remote signals or barrier semaphores. Data moves between devices by JAX's collectives and lax.ppermute only.
A program may use at most 384 MiB of HBM per device.

v0:
```python
import jax
import jax.numpy as jnp
from jax import lax
from jax.sharding import PartitionSpec as P

D = 2048
HEADS = 16
FEAT = 16
WINDOW = 64
CONV_K = 3
VHEAD = 128


def product(left, right):
    return jnp.dot(left, right, preferred_element_type=jnp.float32)


def product_tn(left, right):
    return lax.dot_general(
        left, right, (((0,), (0,)), ((), ())), preferred_element_type=jnp.float32
    )


def product_nt(left, right):
    return lax.dot_general(
        left, right, (((1,), (1,)), ((), ())), preferred_element_type=jnp.float32
    )


def rms_norm(values, gain_vec):
    return values * lax.rsqrt(jnp.mean(values * values, axis=-1, keepdims=True) + 1e-06) * gain_vec


def short_conv(values, taps):
    total = values * taps[:, 0]
    for shift in range(1, CONV_K):
        moved = jnp.concatenate(
            [jnp.zeros((shift, values.shape[1]), jnp.float32), values[:-shift]], axis=0
        )
        total = total + moved * taps[:, shift]
    return total


def taylor(values):
    count = values.shape[0]
    scaled = values.reshape(count, HEADS, FEAT).transpose(1, 0, 2) * FEAT ** (-0.25)
    outer = (scaled[:, :, :, None] * scaled[:, :, None, :]).reshape(
        HEADS, count, FEAT * FEAT
    ) * 0.5**0.5
    return jnp.concatenate([jnp.ones((HEADS, count, 1), jnp.float32), scaled, outer], axis=2)


def front_part(inputs, g_one, taps):
    return short_conv(rms_norm(inputs, g_one), taps)


def shards(
    tokens,
    lengths,
    cotangent,
    norm_gain,
    conv_weight,
    w_query,
    w_key,
    w_value,
    w_query_window,
    w_key_window,
    w_out,
    ffn_gain,
    w_gate,
    w_up,
    w_down,
):
    low_type = jnp.bfloat16
    mixer_full = (
        lax.all_gather(norm_gain.astype(low_type), ("grp", "wide"), axis=0, tiled=True),
        lax.all_gather(conv_weight.astype(low_type), ("grp", "wide"), axis=0, tiled=True),
        lax.all_gather(w_query.astype(low_type), ("grp", "wide"), axis=0, tiled=True),
        lax.all_gather(w_key.astype(low_type), ("grp", "wide"), axis=0, tiled=True),
        lax.all_gather(w_value.astype(low_type), ("grp", "wide"), axis=0, tiled=True),
        lax.all_gather(w_query_window.astype(low_type), ("grp", "wide"), axis=0, tiled=True),
        lax.all_gather(w_key_window.astype(low_type), ("grp", "wide"), axis=0, tiled=True),
        lax.all_gather(w_out.astype(low_type), ("grp", "wide"), axis=0, tiled=True),
    )
    ffn_full = (
        lax.all_gather(ffn_gain.astype(low_type), ("grp", "wide"), axis=0, tiled=True),
        lax.all_gather(w_gate.astype(low_type), ("grp", "wide"), axis=0, tiled=True),
        lax.all_gather(w_up.astype(low_type), ("grp", "wide"), axis=0, tiled=True),
        lax.all_gather(w_down.astype(low_type), ("grp", "wide"), axis=0, tiled=True),
    )
    g_one_b, taps_b, wq, wk, wv, wq_win, wk_win, wo = mixer_full
    g_two_b, wg, wu, wd = ffn_full
    inputs = tokens.astype(jnp.float32)
    count = inputs.shape[0]
    length = lengths[0]
    place = jnp.arange(count, dtype=jnp.int32)
    is_valid = (place < length).astype(jnp.float32)
    causal_bool = place[:, None] >= place[None, :]
    causal = causal_bool.astype(jnp.float32)[None]
    in_window = (
        causal_bool & (place[:, None] - place[None, :] < WINDOW) & (place[None, :] < length)
    )[None]
    scale = VHEAD ** (-0.5)
    conv_out, front_pull = jax.vjp(
        front_part, inputs, g_one_b.astype(jnp.float32), taps_b.astype(jnp.float32)
    )
    conv_low = conv_out.astype(low_type)
    query = product(conv_low, wq)
    key_lin = product(conv_low, wk)
    value = product(conv_low, wv).astype(low_type).reshape(count, HEADS, VHEAD)
    query_win = product(conv_low, wq_win).astype(low_type).reshape(count, HEADS, VHEAD)
    key_win = product(conv_low, wk_win).astype(low_type).reshape(count, HEADS, VHEAD)

    def key_features(values):
        return taylor(values) * is_valid[None, :, None]

    feat_query_f, query_pull = jax.vjp(taylor, query)
    feat_key_f, key_pull = jax.vjp(key_features, key_lin)
    feat_query = feat_query_f.astype(low_type)
    feat_key = feat_key_f.astype(low_type)
    kernel = (
        jnp.einsum("htf,hsf->hts", feat_query, feat_key, preferred_element_type=jnp.float32)
        * causal
    )
    denom = jnp.sum(kernel, axis=2, keepdims=True)
    share_f = kernel / denom
    share = share_f.astype(low_type)
    linear_out = jnp.einsum("hts,she->the", share, value, preferred_element_type=jnp.float32)
    raw_scores = jnp.einsum("the,she->hts", query_win, key_win, preferred_element_type=jnp.float32)
    logits = jnp.where(in_window, raw_scores * scale, -1e30)
    probs = jax.nn.softmax(logits, axis=2)
    probs_low = probs.astype(low_type)
    window_out = jnp.einsum("hts,she->the", probs_low, value, preferred_element_type=jnp.float32)
    mixed = (linear_out + window_out).reshape(count, D).astype(low_type)
    resid = inputs + product(mixed, wo)
    normed_f, middle_pull = jax.vjp(rms_norm, resid, g_two_b.astype(jnp.float32))
    normed = normed_f.astype(low_type)
    gate_pre = product(normed, wg)
    up_pre = product(normed, wu)
    sigma = jax.nn.sigmoid(gate_pre)
    silu_gate = gate_pre * sigma
    hidden = (silu_gate * up_pre).astype(low_type)
    block_out = ((resid + product(hidden, wd)) * is_valid[:, None]).astype(low_type)
    ffn_back = (
        lax.all_gather(ffn_gain.astype(low_type), ("grp", "wide"), axis=0, tiled=True),
        lax.all_gather(w_gate.astype(low_type), ("grp", "wide"), axis=0, tiled=True),
        lax.all_gather(w_up.astype(low_type), ("grp", "wide"), axis=0, tiled=True),
        lax.all_gather(w_down.astype(low_type), ("grp", "wide"), axis=0, tiled=True),
    )
    wg, wu, wd = (ffn_back[1], ffn_back[2], ffn_back[3])
    grad_outer = cotangent.astype(jnp.float32) * is_valid[:, None]
    down_in = grad_outer.astype(low_type)
    grad_down = product_tn(hidden, down_in)
    grad_hidden = product_nt(down_in, wd).astype(low_type).astype(jnp.float32)
    grad_gate_pre = (grad_hidden * up_pre * sigma * (1.0 + gate_pre * (1.0 - sigma))).astype(
        low_type
    )
    grad_up_pre = (grad_hidden * silu_gate).astype(low_type)
    grad_gate = product_tn(normed, grad_gate_pre)
    grad_up = product_tn(normed, grad_up_pre)
    grad_normed = (
        (product_nt(grad_gate_pre, wg) + product_nt(grad_up_pre, wu))
        .astype(low_type)
        .astype(jnp.float32)
    )
    grad_resid_norm, grad_ffn_gain = middle_pull(grad_normed)
    grad_resid = grad_outer + grad_resid_norm
    ffn_sums = (
        lax.psum_scatter(grad_ffn_gain, ("grp", "wide"), scatter_dimension=0, tiled=True),
        lax.psum_scatter(grad_gate, ("grp", "wide"), scatter_dimension=0, tiled=True),
        lax.psum_scatter(grad_up, ("grp", "wide"), scatter_dimension=0, tiled=True),
        lax.psum_scatter(grad_down, ("grp", "wide"), scatter_dimension=0, tiled=True),
    )
    mixer_back = (
        lax.all_gather(norm_gain.astype(low_type), ("grp", "wide"), axis=0, tiled=True),
        lax.all_gather(conv_weight.astype(low_type), ("grp", "wide"), axis=0, tiled=True),
        lax.all_gather(w_query.astype(low_type), ("grp", "wide"), axis=0, tiled=True),
        lax.all_gather(w_key.astype(low_type), ("grp", "wide"), axis=0, tiled=True),
        lax.all_gather(w_value.astype(low_type), ("grp", "wide"), axis=0, tiled=True),
        lax.all_gather(w_query_window.astype(low_type), ("grp", "wide"), axis=0, tiled=True),
        lax.all_gather(w_key_window.astype(low_type), ("grp", "wide"), axis=0, tiled=True),
        lax.all_gather(w_out.astype(low_type), ("grp", "wide"), axis=0, tiled=True),
    )
    wq, wk, wv, wq_win, wk_win, wo = (
        mixer_back[2],
        mixer_back[3],
        mixer_back[4],
        mixer_back[5],
        mixer_back[6],
        mixer_back[7],
    )
    branch_in = grad_resid.astype(low_type)
    grad_out = product_tn(mixed, branch_in)
    grad_mixed = product_nt(branch_in, wo).astype(low_type).reshape(count, HEADS, VHEAD)
    grad_weights = jnp.einsum("the,she->hts", grad_mixed, value, preferred_element_type=jnp.float32)
    grad_value_heads = jnp.einsum(
        "hts,the->she", probs_low, grad_mixed, preferred_element_type=jnp.float32
    )
    grad_value_heads = grad_value_heads + jnp.einsum(
        "hts,the->she", share, grad_mixed, preferred_element_type=jnp.float32
    )
    grad_logits = probs * (grad_weights - jnp.sum(grad_weights * probs, axis=2, keepdims=True))
    grad_raw = jnp.where(in_window, grad_logits * scale, 0.0).astype(low_type)
    grad_query_win = (
        jnp.einsum("hts,she->the", grad_raw, key_win, preferred_element_type=jnp.float32)
        .reshape(count, D)
        .astype(low_type)
    )
    grad_key_win = (
        jnp.einsum("hts,the->she", grad_raw, query_win, preferred_element_type=jnp.float32)
        .reshape(count, D)
        .astype(low_type)
    )
    grad_kernel = (
        (grad_weights - jnp.sum(grad_weights * share_f, axis=2, keepdims=True)) / denom * causal
    ).astype(low_type)
    grad_feat_query = jnp.einsum(
        "hts,hsf->htf", grad_kernel, feat_key, preferred_element_type=jnp.float32
    )
    grad_feat_key = jnp.einsum(
        "hts,htf->hsf", grad_kernel, feat_query, preferred_element_type=jnp.float32
    )
    grad_query_pre = query_pull(grad_feat_query)[0].astype(low_type)
    grad_key_pre = key_pull(grad_feat_key)[0].astype(low_type)
    grad_value_pre = grad_value_heads.reshape(count, D).astype(low_type)
    grad_query = product_tn(conv_low, grad_query_pre)
    grad_key = product_tn(conv_low, grad_key_pre)
    grad_value = product_tn(conv_low, grad_value_pre)
    grad_query_window = product_tn(conv_low, grad_query_win)
    grad_key_window = product_tn(conv_low, grad_key_win)
    grad_conv_low = (
        product_nt(grad_query_pre, wq)
        + product_nt(grad_key_pre, wk)
        + product_nt(grad_value_pre, wv)
    )
    grad_conv_low = (
        grad_conv_low + product_nt(grad_query_win, wq_win) + product_nt(grad_key_win, wk_win)
    )
    grad_front, grad_norm_gain, grad_conv = front_pull(
        grad_conv_low.astype(low_type).astype(jnp.float32)
    )
    grad_tokens = (grad_resid + grad_front).astype(low_type)
    mixer_sums = (
        lax.psum_scatter(grad_norm_gain, ("grp", "wide"), scatter_dimension=0, tiled=True),
        lax.psum_scatter(grad_conv, ("grp", "wide"), scatter_dimension=0, tiled=True),
        lax.psum_scatter(grad_query, ("grp", "wide"), scatter_dimension=0, tiled=True),
        lax.psum_scatter(grad_key, ("grp", "wide"), scatter_dimension=0, tiled=True),
        lax.psum_scatter(grad_value, ("grp", "wide"), scatter_dimension=0, tiled=True),
        lax.psum_scatter(grad_query_window, ("grp", "wide"), scatter_dimension=0, tiled=True),
        lax.psum_scatter(grad_key_window, ("grp", "wide"), scatter_dimension=0, tiled=True),
        lax.psum_scatter(grad_out, ("grp", "wide"), scatter_dimension=0, tiled=True),
    )
    return (
        block_out,
        grad_tokens,
        mixer_sums[0],
        mixer_sums[1],
        mixer_sums[2],
        mixer_sums[3],
        mixer_sums[4],
        mixer_sums[5],
        mixer_sums[6],
        mixer_sums[7],
        ffn_sums[0],
        ffn_sums[1],
        ffn_sums[2],
        ffn_sums[3],
    )


def solution(mesh):
    placed = (
        P(("grp", "wide"), None),
        P(("grp", "wide")),
        P(("grp", "wide"), None),
        P(("grp", "wide")),
        P(("grp", "wide"), None),
        P(("grp", "wide"), None),
        P(("grp", "wide"), None),
        P(("grp", "wide"), None),
        P(("grp", "wide"), None),
        P(("grp", "wide"), None),
        P(("grp", "wide"), None),
        P(("grp", "wide")),
        P(("grp", "wide"), None),
        P(("grp", "wide"), None),
        P(("grp", "wide"), None),
    )
    return jax.shard_map(
        shards,
        mesh=mesh,
        in_specs=placed,
        out_specs=(
            P(("grp", "wide"), None),
            P(("grp", "wide"), None),
            P(("grp", "wide")),
            P(("grp", "wide"), None),
            P(("grp", "wide"), None),
            P(("grp", "wide"), None),
            P(("grp", "wide"), None),
            P(("grp", "wide"), None),
            P(("grp", "wide"), None),
            P(("grp", "wide"), None),
            P(("grp", "wide")),
            P(("grp", "wide"), None),
            P(("grp", "wide"), None),
            P(("grp", "wide"), None),
        ),
        check_vma=False,
    )
```

profile of v0, /device:TPU:0, one launch (start us, length us, event | category | flops | bytes accessed | tf_op | source)
XLA Modules:
  0.0 5533.0 jit_solution(5764992241881015207)
XLA Ops:
  23.6 42.1 all-reduce.14
  65.7 65.9 %all-gather = bf16[32,64,3]{1,2,0:T(4,128)(2,1)S(1)} all-gather(bf16[1,64,3]{1,2,0:T(4,128)(2,1)S(1)} %convert_bitcast_fusion.1), channel_id=1, replica_groups=mesh['grp'=4,'wide'=8] {'grp','wide'}, dimensions={0}, use_global_device_ids=true | all-gather | bytes 12672 | tf_op jit(solution)/shard_map/all_gather | solution.py:77
  147.6 56.9 %all-gather.20.cloned.1.call-done = bf16[2048,2048]{1,0:T(8,128)(2,1)} async-done(((bf16[64,2048]{1,0:T(8,128)(2,1)}), bf16[2048,2048]{1,0:T(8,128)(2,1)}) %all-gather.20.cloned.1.call-update) | async-done | bytes 8388624 | tf_op jit(solution)/shard_map/all_gather | solution.py:82
  212.7 71.3 %all-gather.18.cloned.1.call-done = bf16[2048,2048]{1,0:T(8,128)(2,1)} async-done(((bf16[64,2048]{1,0:T(8,128)(2,1)}), bf16[2048,2048]{1,0:T(8,128)(2,1)}) %all-gather.18.cloned.1.call-update) | async-done | bytes 8388624 | tf_op jit(solution)/shard_map/all_gather | solution.py:81
  297.7 65.7 %all-gather.12.cloned.1.call-done = bf16[2048,2048]{1,0:T(8,128)(2,1)} async-done(((bf16[64,2048]{1,0:T(8,128)(2,1)}), bf16[2048,2048]{1,0:T(8,128)(2,1)}) %all-gather.12.cloned.1.call-update) | async-done | bytes 8388624 | tf_op jit(solution)/shard_map/all_gather | solution.py:80
  373.5 69.2 %all-gather.22.cloned.1.call-done = bf16[2048,2048]{1,0:T(8,128)(2,1)} async-done(((bf16[64,2048]{1,0:T(8,128)(2,1)}), bf16[2048,2048]{1,0:T(8,128)(2,1)}) %all-gather.22.cloned.1.call-update) | async-done | bytes 8388624 | tf_op jit(solution)/shard_map/all_gather | solution.py:83
  449.2 140.3 %all-gather.28.cloned.1.call-done = bf16[32,172,2048]{2,1,0:T(8,128)(2,1)} async-done(((bf16[1,172,2048]{2,1,0:T(8,128)(2,1)}), bf16[32,172,2048]{2,1,0:T(8,128)(2,1)}) %all-gather.28.cloned.1.call-update) | async-done | bytes 22544400 | tf_op jit(solution)/shard_map/all_gather | solution.py:89
  589.4 33.0 reshape.232
  622.5 110.1 %all-gather.26.cloned.1.call-done = bf16[2048,5504]{1,0:T(8,128)(2,1)} async-done(((bf16[64,5504]{1,0:T(8,128)(2,1)}), bf16[2048,5504]{1,0:T(8,128)(2,1)}) %all-gather.26.cloned.1.call-update) | async-done | bytes 22544400 | tf_op jit(solution)/shard_map/all_gather | solution.py:88
  732.6 13.0 fusion.109
  745.6 130.1 %all-gather.24.cloned.1.call-done = bf16[2048,5504]{1,0:T(8,128)(2,1)} async-done(((bf16[64,5504]{1,0:T(8,128)(2,1)}), bf16[2048,5504]{1,0:T(8,128)(2,1)}) %all-gather.24.cloned.1.call-update) | async-done | bytes 22544400 | tf_op jit(solution)/shard_map/all_gather | solution.py:87
  875.7 13.1 fusion.108
  888.8 24.6 multiply_convert_fusion
  913.4 13.1 fusion.110
  926.5 13.5 fusion.28
  957.2 8.4 fusion.51
  965.7 8.5 fusion.54
  974.2 10.4 fusion.49
  984.5 9.2 broadcast_multiply_fusion
  1031.0 9.7 fusion.74
  1051.3 8.2 fusion.119
  1070.1 19.3 fusion.121
  1089.5 19.4 fusion.120
  1110.1 19.3 fusion.77
  1129.4 1527.7 %fusion = f32[176,2048]{1,0:T(8,128)S(1)} fusion(f32[5504,2048]{1,0:T(8,128)} %fusion.77), kind=kCustom, calls=%all-reduce-scatter | all-reduce-scatter fusion | flops 11534337 | bytes 46530560
  2662.4 12.8 fusion.17
  2675.2 85.0 %all-reduce.13 = (f32[2048]{0:T(1024)S(1)}, f32[2048]{0:T(1024)S(1)}) all-reduce(f32[2048]{0:T(1024)S(1)} %get-tuple-element.22, f32[2048]{0:T(1024)S(1)} %copy-done.55), channel_id=2, replica_groups=mesh['grp'=4,'wide'=8] {'grp','wide'}, use_global_device_ids=true, to_apply=%region_14.15.clone | all-reduce | flops 4096 | bytes 32768
  2773.5 135.5 %reduce-scatter.20.cloned.1.call-done = f32[64,2048]{1,0:T(8,128)} async-done(((f32[2048,2048]{1,0:T(8,128)}), f32[64,2048]{1,0:T(8,128)}) %reduce-scatter.20.cloned.1.call-update) | async-done | bytes 524304 | tf_op jit(solution)/shard_map/reduce_scatter | solution.py:249
  2909.0 360.6 %reduce-scatter.22.cloned.1.call-done = f32[64,2048]{1,0:T(8,128)} async-done(((f32[2048,2048]{1,0:T(8,128)}), f32[64,2048]{1,0:T(8,128)}) %reduce-scatter.22.cloned.1.call-update) | async-done | bytes 524304 | tf_op jit(solution)/shard_map/reduce_scatter | solution.py:250
  3269.6 360.2 %reduce-scatter.18.cloned.1.call-done = f32[64,2048]{1,0:T(8,128)} async-done(((f32[2048,2048]{1,0:T(8,128)}), f32[64,2048]{1,0:T(8,128)}) %reduce-scatter.18.cloned.1.call-update) | async-done | bytes 524304 | tf_op jit(solution)/shard_map/reduce_scatter | solution.py:248
  3629.8 947.7 %reduce-scatter.28.cloned.1.call-done = f32[64,5504]{1,0:T(8,128)} async-done(((f32[2048,5504]{1,0:T(8,128)}), f32[64,5504]{1,0:T(8,128)}) %reduce-scatter.28.cloned.1.call-update) | async-done | bytes 1409040 | tf_op jit(solution)/shard_map/reduce_scatter | solution.py:171
  4577.5 948.4 %reduce-scatter.26.cloned.1.call-done = f32[64,5504]{1,0:T(8,128)} async-done(((f32[2048,5504]{1,0:T(8,128)}), f32[64,5504]{1,0:T(8,128)}) %reduce-scatter.26.cloned.1.call-update) | async-done | bytes 1409040 | tf_op jit(solution)/shard_map/reduce_scatter | solution.py:170
  (268 shorter events, 164.6 us)
Async XLA Ops:
  7.2 128.3 %all-gather.16.cloned.1.call-start = ((), (), s32[]{:S(2)}) async-start(), calls=%async_computation.11 | async-start | bytes 1081344 | tf_op jit(solution)/shard_map/all_gather | solution.py:79
  8.8 128.8 %all-gather.14.cloned.1.call-start = ((), (), s32[]{:S(2)}) async-start(), calls=%async_computation.10 | async-start | bytes 1081344 | tf_op jit(solution)/shard_map/all_gather | solution.py:78
  10.4 194.2 %all-gather.20.cloned.1.call-start = ((), (), s32[]{:S(2)}) async-start(), calls=%async_computation.13 | async-start | bytes 8650752 | tf_op jit(solution)/shard_map/all_gather | solution.py:82
  12.2 271.8 %all-gather.18.cloned.1.call-start = ((), (), s32[]{:S(2)}) async-start(), calls=%async_computation.12 | async-start | bytes 8650752 | tf_op jit(solution)/shard_map/all_gather | solution.py:81
  14.1 349.4 %all-gather.12.cloned.1.call-start = ((), (), s32[]{:S(2)}) async-start(), calls=%async_computation.9 | async-start | bytes 8650752 | tf_op jit(solution)/shard_map/all_gather | solution.py:80
  15.9 426.8 %all-gather.22.cloned.1.call-start = ((), (), s32[]{:S(2)}) async-start(), calls=%async_computation.14 | async-start | bytes 8650752 | tf_op jit(solution)/shard_map/all_gather | solution.py:83
  17.8 47.9 copy-start.56
  17.8 114.0 %copy-start.4 = (bf16[256,2048]{1,0:T(8,128)(2,1)S(1)}, bf16[256,2048]{1,0:T(8,128)(2,1)}, u32[]{:S(2)}) copy-start(bf16[256,2048]{1,0:T(8,128)(2,1)} %param.15) | copy-start | bytes 3145732
  17.8 571.6 %all-gather.28.cloned.1.call-start = ((), (), s32[]{:S(2)}) async-start(), calls=%async_computation.25 | async-start | bytes 23789568 | tf_op jit(solution)/shard_map/all_gather | solution.py:89
  18.8 713.7 %all-gather.26.cloned.1.call-start = ((), (), s32[]{:S(2)}) async-start(), calls=%async_computation.16 | async-start | bytes 23248896 | tf_op jit(solution)/shard_map/all_gather | solution.py:88
  21.3 854.4 %all-gather.24.cloned.1.call-start = ((), (), s32[]{:S(2)}) async-start(), calls=%async_computation.15 | async-start | bytes 23248896 | tf_op jit(solution)/shard_map/all_gather | solution.py:87
  22.3 2742.2 %reduce-scatter.30.cloned.1.call-start = ((), (), s32[]{:S(2)}) async-start(), calls=%async_computation.26 | async-start | bytes 1081344
  65.7 69.7 %copy-start.41 = (f32[2048]{0:T(1024)}, f32[2048]{0:T(1024)S(1)}, u32[]{:S(2)}) copy-start(f32[2048]{0:T(1024)S(1)} %convert_element_type.209) | copy-start | bytes 24580
  131.8 237.5 %copy-start.40 = (f32[256,256]{0,1:T(8,128)}, f32[256,256]{0,1:T(8,128)S(1)}, u32[]{:S(2)}) copy-start(f32[256,256]{0,1:T(8,128)S(1)} %fusion.87) | copy-start | bytes 786436
  135.5 228.0 %copy-start = (bf16[256,2048]{1,0:T(8,128)(2,1)}, bf16[256,2048]{1,0:T(8,128)(2,1)S(1)}, u32[]{:S(2)}) copy-start(bf16[256,2048]{1,0:T(8,128)(2,1)S(1)} %add_convert_fusion.2) | copy-start | bytes 3145732
  147.6 221.7 %copy-start.65 = (f32[16,256]{1,0:T(8,128)}, f32[16,256]{1,0:T(8,128)S(1)}, u32[]{:S(2)}) copy-start(f32[16,256]{1,0:T(8,128)S(1)} %get-tuple-element.40) | copy-start | bytes 49156
  212.7 80.2 %copy-start.35 = (bf16[256,2048]{0,1:T(8,128)(2,1)}, bf16[256,2048]{0,1:T(8,128)(2,1)S(1)}, u32[]{:S(2)}) copy-start(bf16[256,2048]{0,1:T(8,128)(2,1)S(1)} %copy.115) | copy-start | bytes 3145732
  448.9 491.2 %copy-start.8 = (f32[256,2048]{1,0:T(8,128)}, f32[256,2048]{1,0:T(8,128)S(1)}, u32[]{:S(2)}) copy-start(f32[256,2048]{1,0:T(8,128)S(1)} %get-tuple-element.45) | copy-start | bytes 6291460
  449.1 426.5 %copy-start.10 = (bf16[256,2048]{1,0:T(8,128)(2,1)}, bf16[256,2048]{1,0:T(8,128)(2,1)S(1)}, u32[]{:S(2)}) copy-start(bf16[256,2048]{1,0:T(8,128)(2,1)S(1)} %multiply_convert_fusion.5) | copy-start | bytes 3145732
  926.5 13.6 copy-start.19
  1027.2 1746.3 %reduce-scatter.16.cloned.1.call-start = ((), (), s32[]{:S(2)}) async-start(), calls=%async_computation.18 | async-start | bytes 2162688 | tf_op jit(solution)/shard_map/reduce_scatter | solution.py:247
  1029.1 1744.4 %reduce-scatter.14.cloned.1.call-start = ((), (), s32[]{:S(2)}) async-start(), calls=%async_computation.17 | async-start | bytes 2162688 | tf_op jit(solution)/shard_map/reduce_scatter | solution.py:246
  1031.0 1742.6 %reduce-scatter.24.cloned.1.call-start = ((), (), s32[]{:S(2)}) async-start(), calls=%async_computation.22 | async-start | bytes 17301504 | tf_op jit(solution)/shard_map/reduce_scatter | solution.py:251
  1040.8 1868.3 %reduce-scatter.20.cloned.1.call-start = ((), (), s32[]{:S(2)}) async-start(), calls=%async_computation.20 | async-start | bytes 17301504 | tf_op jit(solution)/shard_map/reduce_scatter | solution.py:249
  1050.1 2219.5 %reduce-scatter.22.cloned.1.call-start = ((), (), s32[]{:S(2)}) async-start(), calls=%async_computation.21 | async-start | bytes 17301504 | tf_op jit(solution)/shard_map/reduce_scatter | solution.py:250
  1059.5 2570.2 %reduce-scatter.18.cloned.1.call-start = ((), (), s32[]{:S(2)}) async-start(), calls=%async_computation.19 | async-start | bytes 17301504 | tf_op jit(solution)/shard_map/reduce_scatter | solution.py:248
  1068.9 3508.6 %reduce-scatter.28.cloned.1.call-start = ((), (), s32[]{:S(2)}) async-start(), calls=%async_computation.24 | async-start | bytes 46497792 | tf_op jit(solution)/shard_map/reduce_scatter | solution.py:171
  1089.4 4436.5 %reduce-scatter.26.cloned.1.call-start = ((), (), s32[]{:S(2)}) async-start(), calls=%async_computation.23 | async-start | bytes 46497792 | tf_op jit(solution)/shard_map/reduce_scatter | solution.py:170
  2659.3 15.9 copy-start.55
  2659.3 102.0 %copy-start.54 = (f32[256]{0:T(256)S(1)}, f32[256]{0:T(256)}, u32[]{:S(2)}) copy-start(f32[256]{0:T(256)} %copy-done.53) | copy-start | bytes 3076
  2659.3 102.1 %copy-start.7 = (f32[256,2048]{1,0:T(8,128)S(1)}, f32[256,2048]{1,0:T(8,128)}, u32[]{:S(2)}) copy-start(f32[256,2048]{1,0:T(8,128)} %copy-done.6) | copy-start | bytes 6291460
  2659.3 106.7 %collective-permute-start = (f32[124,2048]{1,0:T(8,128)}, f32[124,2048]{1,0:T(8,128)}, u32[]{:S(2)}, u32[]{:S(2)}) collective-permute-start(f32[124,2048]{1,0:T(8,128)} %slice.25), channel_id=1, source_target_pairs={{0,1},{1,2},{2,3},{3,4},{4,5},{5,6},{6,7},{7,8},{8,9},{9,10},{10,1... | collective-permute-start | bytes 3047432
  (57 other events, 249.3 us)
Sparse Core Ops, SparseCore 0:
  11.7 56.4 all-gather.15
  71.8 52.7 all-gather.13
  128.1 76.3 all-gather.19
  207.9 75.9 all-gather.17
  287.4 75.9 all-gather.11
  366.8 75.8 all-gather.21
  446.2 143.1 all-gather.27
  592.3 140.2 all-gather.25
  735.4 140.2 all-gather.23
  1027.3 165.8 reduce-scatter.29
  1196.2 244.8 reduce-scatter.15
  1443.8 235.0 reduce-scatter.13
  1681.9 734.7 reduce-scatter.23
  2419.5 489.4 reduce-scatter.19
  2911.9 357.6 reduce-scatter.21
  3272.4 357.2 reduce-scatter.17
  3632.6 944.8 reduce-scatter.27
  4580.3 945.5 reduce-scatter.25
where the time goes:
time: 5540 us; the launch traced here: 5530 us
  waiting for transfers between devices  3400 us (61%)
  blocking collectives  1720 us (31%)
  matrix products  295 us (5%)
  local copies, waits for them, and re-layouts  66.9 us (1%)
    unnamed x3, blocking collectives  1650 us
    reduce_scatter x1, waiting for transfers between devices, shards(): lax.psum_scatter(grad_gate, ('grp', 'wide'), scatter_dimension=0, tiled=T...  948 us
    reduce_scatter x1, waiting for transfers between devices, shards(): lax.psum_scatter(grad_up, ('grp', 'wide'), scatter_dimension=0, tiled=True)  948 us
    reduce_scatter x1, waiting for transfers between devices, shards(): lax.psum_scatter(grad_key_window, ('grp', 'wide'), scatter_dimension=0, t...  361 us
    reduce_scatter x1, waiting for transfers between devices, shards(): lax.psum_scatter(grad_value, ('grp', 'wide'), scatter_dimension=0, tiled=...  360 us
    all_gather x1, waiting for transfers between devices, shards(): lax.all_gather(w_down.astype(low_type), ('grp', 'wide'), axis=0, tiled=True)  140 us
    reduce_scatter x1, waiting for transfers between devices, shards(): lax.psum_scatter(grad_query_window, ('grp', 'wide'), scatter_dimension=0,...  136 us
    all_gather x1, waiting for transfers between devices, shards(): lax.all_gather(w_gate.astype(low_type), ('grp', 'wide'), axis=0, tiled=True)  130 us
  transfers between devices with their start and end apart: 19, of which 12 were waited for; matrix products, arithmetic and copies ran while one was open for 32% of the time, Pallas kernels for 0%

commit v1 on v0

v1 whole, which is shorter than its diff:
```python
import functools

import jax
import jax.numpy as jnp
from jax import lax
from jax.experimental import pallas as pl
from jax.experimental.pallas import tpu as pltpu
from jax.sharding import PartitionSpec as P

D = 2048
HEADS = 16
FEAT = 16
WINDOW = 64
CONV_K = 3
VHEAD = 128
GROUP = 4
HEADS_G = HEADS // GROUP
LIN_G = HEADS_G * FEAT
WIN_G = HEADS_G * VHEAD
PACK = 2 * LIN_G + 3 * WIN_G

low = jnp.bfloat16
f32 = jnp.float32

CYCLES = {8: (0, 2, 4, 6, 7, 5, 3, 1)}


def dot(left, right, over_left, over_right):
    return lax.dot_general(
        left, right, (((over_left,), (over_right,)), ((), ())), preferred_element_type=f32
    )


def product(left, right):
    return dot(left, right, 1, 0)


def product_tn(left, right):
    return dot(left, right, 0, 0)


def product_nt(left, right):
    return dot(left, right, 1, 1)


def rms_norm(values, gain_vec):
    return values * lax.rsqrt(jnp.mean(values * values, axis=-1, keepdims=True) + 1e-06) * gain_vec


def short_conv(values, taps):
    total = values * taps[0]
    for shift in range(1, CONV_K):
        moved = jnp.concatenate(
            [jnp.zeros((shift, values.shape[1]), f32), values[:-shift]], axis=0
        )
        total = total + moved * taps[shift]
    return total


def front_part(inputs, g_one, taps):
    return short_conv(rms_norm(inputs, g_one), taps)


def head_parts(pack_ref, head, keep, in_window):
    query = pack_ref[:, FEAT * head : FEAT * (head + 1)].astype(low)
    key = pack_ref[:, LIN_G + FEAT * head : LIN_G + FEAT * (head + 1)].astype(low)
    start = 2 * LIN_G + VHEAD * head
    value = pack_ref[:, start : start + VHEAD].astype(low)
    start += WIN_G
    query_win = pack_ref[:, start : start + VHEAD].astype(low)
    start += WIN_G
    key_win = pack_ref[:, start : start + VHEAD].astype(low)
    scores = product_nt(query, key) * FEAT**-0.5
    kernel = jnp.where(keep, 1.0 + scores + 0.5 * scores * scores, 0.0)
    over = 1.0 / jnp.sum(kernel, axis=1, keepdims=True)
    share = kernel * over
    logits = jnp.where(in_window, product_nt(query_win, key_win) * VHEAD**-0.5, -1e30)
    raised = jnp.exp(logits - jnp.max(logits, axis=1, keepdims=True))
    probs = raised * (1.0 / jnp.sum(raised, axis=1, keepdims=True))
    return query, key, value, query_win, key_win, scores, over, share, probs


def masks(length, count):
    row = lax.broadcasted_iota(jnp.int32, (count, count), 0)
    col = lax.broadcasted_iota(jnp.int32, (count, count), 1)
    keep = (row >= col) & (col < length)
    return keep, keep & (row - col < WINDOW)


def mix_kernel(lens_ref, pack_ref, mixed_ref):
    keep, in_window = masks(lens_ref[pl.program_id(0)], pack_ref.shape[0])
    for head in range(HEADS_G):
        parts = head_parts(pack_ref, head, keep, in_window)
        value, share, probs = parts[2], parts[7], parts[8]
        out = product((share + probs).astype(low), value)
        mixed_ref[:, VHEAD * head : VHEAD * (head + 1)] = out.astype(low)


def mix_back_kernel(lens_ref, pack_ref, grad_ref, out_ref):
    keep, in_window = masks(lens_ref[pl.program_id(0)], pack_ref.shape[0])
    grad_query, grad_key = [], []
    for head in range(HEADS_G):
        query, key, value, query_win, key_win, scores, over, share, probs = head_parts(
            pack_ref, head, keep, in_window
        )
        grad = grad_ref[:, VHEAD * head : VHEAD * (head + 1)]
        weights = product_nt(grad, value)
        grad_raw = probs * (weights - jnp.sum(weights * probs, axis=1, keepdims=True))
        grad_raw = (grad_raw * VHEAD**-0.5).astype(low)
        centred = weights - jnp.sum(weights * share, axis=1, keepdims=True)
        grad_scores = jnp.where(keep, centred * (over * FEAT**-0.5) * (1.0 + scores), 0.0)
        grad_scores = grad_scores.astype(low)
        start = 2 * LIN_G + VHEAD * head
        out_ref[:, start : start + VHEAD] = product_tn((share + probs).astype(low), grad).astype(low)
        start += WIN_G
        out_ref[:, start : start + VHEAD] = product(grad_raw, key_win).astype(low)
        start += WIN_G
        out_ref[:, start : start + VHEAD] = product_tn(grad_raw, query_win).astype(low)
        grad_query.append(product(grad_scores, key).astype(low))
        grad_key.append(product_tn(grad_scores, query).astype(low))
    out_ref[:, : 2 * LIN_G] = jnp.concatenate(grad_query + grad_key, axis=1)


def per_sequence(body, name, count, widths, out_width, out_type, lens, *arrays):
    return pl.pallas_call(
        body,
        grid=(GROUP,),
        in_specs=[pl.BlockSpec(memory_space=pltpu.SMEM)]
        + [pl.BlockSpec((count, width), lambda i: (i, 0)) for width in widths],
        out_specs=pl.BlockSpec((count, out_width), lambda i: (i, 0)),
        out_shape=jax.ShapeDtypeStruct((GROUP * count, out_width), out_type),
        compiler_params=pltpu.CompilerParams(vmem_limit_bytes=32 * 1024 * 1024),
        cost_estimate=pl.CostEstimate(
            flops=2_000_000_000, bytes_accessed=10_000_000, transcendentals=1_000_000
        ),
        name=name,
    )(lens, *arrays)


def swap(value, over):
    return lax.ppermute(value, "grp", [(i, i ^ over) for i in range(GROUP)])


def group_gather(own):
    peer = swap(own, 1)
    across = swap(own, 2)
    return own, peer, across, swap(across, 1)


def group_sum(parts):
    across = (parts[2].astype(f32) + swap(parts[3], 1).astype(f32)).astype(low)
    return parts[0].astype(f32) + swap(parts[1], 1).astype(f32) + swap(across, 2).astype(f32)


def group_exchange(blocks, me):
    def pick(r):
        return lax.dynamic_index_in_dim(blocks, me ^ r, 0, keepdims=False)

    got = jnp.stack([pick(0)] + [swap(pick(r), r) for r in range(1, GROUP)])
    return [lax.dynamic_index_in_dim(got, me ^ j, 0, keepdims=False) for j in range(GROUP)]


def steps_of(axis, size):
    step = 1
    while step < size:
        yield axis, size, step
        step *= 2


def everywhere(value, wide_size):
    stack = value[None]
    for axis, size, step in list(steps_of("wide", wide_size)) + list(steps_of("grp", GROUP)):
        other = lax.ppermute(stack, axis, [(i, i ^ step) for i in range(size)])
        upper = (lax.axis_index(axis) & step) > 0
        stack = jnp.where(
            upper, jnp.concatenate([other, stack], 0), jnp.concatenate([stack, other], 0)
        )
    return stack


def sum_everywhere(value, wide_size):
    for axis, size, step in list(steps_of("grp", GROUP)) + list(steps_of("wide", wide_size)):
        value = value + lax.ppermute(value, axis, [(i, i ^ step) for i in range(size)])
    return value


def wide_gather(block, at, size):
    if size not in CYCLES:
        return jnp.moveaxis(lax.all_gather(block, "wide"), 0, at)
    cycle = CYCLES[size]
    order = jnp.array(cycle, jnp.int32)
    place = jnp.array([cycle.index(i) for i in range(size)], jnp.int32)[lax.axis_index("wide")]
    split = 0 if at == 1 else 2
    halves = jnp.split(block, 2, axis=split)
    whole = jnp.zeros(block.shape[:at] + (size,) + block.shape[at:], block.dtype)
    for step in range(size):
        for d in (0, 1):
            index = [jnp.int32(0)] * 4
            index[at] = order[(place - step if d == 0 else place + step) % size]
            index[split if at == 1 else 3] = jnp.int32(d * halves[0].shape[split])
            whole = lax.dynamic_update_slice(whole, jnp.expand_dims(halves[d], at), index)
            if step < size - 1:
                way = [(cycle[i], cycle[(i + 1) % size]) for i in range(size)]
                if d == 1:
                    way = [(to, of) for of, to in way]
                halves[d] = lax.ppermute(halves[d], "wide", way)
    return whole


def wide_sum(terms, at, size):
    split = 0 if at == 1 else 3
    if size not in CYCLES:
        full = lax.psum_scatter(terms.astype(f32), "wide", scatter_dimension=at, tiled=True)
        return jnp.split(jnp.squeeze(full, at), 2, axis=0 if at == 1 else 2)
    cycle = CYCLES[size]
    order = jnp.array(cycle, jnp.int32)
    place = jnp.array([cycle.index(i) for i in range(size)], jnp.int32)[lax.axis_index("wide")]
    extent = list(terms.shape)
    extent[at] = 1
    extent[split] //= 2
    sums = [None, None]
    for step in range(size):
        for d in (0, 1):
            index = [jnp.int32(0)] * 4
            index[at] = order[(place - step - 1 if d == 0 else place + step + 1) % size]
            index[split] = jnp.int32(d * extent[split])
            mine = jnp.squeeze(lax.dynamic_slice(terms, index, extent), at)
            if step == 0:
                sums[d] = mine
            else:
                sums[d] = sums[d].astype(f32) + mine.astype(f32)
            if step < size - 1:
                way = [(cycle[i], cycle[(i + 1) % size]) for i in range(size)]
                if d == 1:
                    way = [(to, of) for of, to in way]
                sums[d] = lax.ppermute(sums[d].astype(low), "wide", way)
    return sums


def shards(
    tokens,
    lengths,
    cotangent,
    norm_gain,
    conv_weight,
    w_query,
    w_key,
    w_value,
    w_query_window,
    w_key_window,
    w_out,
    ffn_gain,
    w_gate,
    w_up,
    w_down,
    *,
    wide_size,
):
    me = lax.axis_index("grp")
    spot = me * wide_size + lax.axis_index("wide")
    count = tokens.shape[0]
    rows = w_query.shape[0]
    hid_rows = w_down.shape[0]
    hid_g = w_gate.shape[1] // GROUP
    length = lengths[0]
    is_valid = (jnp.arange(count, dtype=jnp.int32) < length).astype(f32)

    def by_columns(weight):
        width = weight.shape[1] // GROUP
        return weight.astype(low).reshape(rows, GROUP, width).transpose(1, 0, 2)

    mixer_blocks = jnp.concatenate(
        [by_columns(x) for x in (w_query, w_key, w_value, w_query_window, w_key_window)], axis=2
    )
    mixer_shard = jnp.stack(group_exchange(mixer_blocks, me))
    w_mix = wide_gather(mixer_shard, 1, wide_size).reshape(D, PACK)
    wo = wide_gather(w_out.astype(low)[None].reshape(rows, 1, D), 0, wide_size).reshape(WIN_G, D)
    gate_shard = jnp.stack(group_exchange(by_columns(w_gate), me))
    up_shard = jnp.stack(group_exchange(by_columns(w_up), me))
    wg = wide_gather(gate_shard, 1, wide_size).reshape(D, hid_g)
    wu = wide_gather(up_shard, 1, wide_size).reshape(D, hid_g)
    wd = wide_gather(w_down.astype(low).reshape(hid_rows, 1, D), 0, wide_size).reshape(hid_g, D)

    small = jnp.concatenate(
        [
            norm_gain[None],
            conv_weight.T,
            ffn_gain[None],
            jnp.broadcast_to(length.astype(f32), (1, rows)),
            jnp.zeros((2, rows), f32),
        ],
        axis=0,
    ).astype(low)
    small_all = everywhere(small, wide_size)
    g_one, tap_0, tap_1, tap_2, g_two = [
        small_all[:, i].reshape(D).astype(f32) for i in range(5)
    ]
    taps = jnp.stack([tap_0, tap_1, tap_2])
    group_lens = small_all[:, 5, 0].reshape(GROUP, wide_size)
    group_lens = lax.dynamic_index_in_dim(group_lens, lax.axis_index("wide"), 1, keepdims=False)
    group_lens = group_lens.astype(jnp.int32)[me ^ jnp.arange(GROUP, dtype=jnp.int32)]

    inputs = tokens.astype(f32)
    conv_out, front_pull = jax.vjp(front_part, inputs, g_one, taps)
    conv_low = jnp.concatenate(group_gather(conv_out.astype(low)), axis=0)
    grad_outer = cotangent.astype(f32) * is_valid[:, None]
    down_in = jnp.concatenate(group_gather(grad_outer.astype(low)), axis=0)

    pack = product(conv_low, w_mix)
    mixed = per_sequence(
        mix_kernel, "mix", count, (PACK,), WIN_G, low, group_lens, pack
    )

    def partial_sum(make):
        far = make(slice(2 * count, 4 * count)).astype(low)
        near = make(slice(0, 2 * count)).astype(low)
        return group_sum([near[:count], near[count:], far[:count], far[count:]])

    resid = inputs + partial_sum(lambda part: product(mixed[part], wo))
    normed_f, middle_pull = jax.vjp(rms_norm, resid, g_two)
    normed = jnp.concatenate(group_gather(normed_f.astype(low)), axis=0)
    gate_pre = product(normed, wg)
    up_pre = product(normed, wu)
    sigma = jax.nn.sigmoid(gate_pre)
    silu_gate = gate_pre * sigma
    hidden = (silu_gate * up_pre).astype(low)
    down = partial_sum(lambda part: product(hidden[part], wd))
    block_out = ((resid + down) * is_valid[:, None]).astype(low)

    grad_down = product_tn(hidden, down_in).astype(low)
    grad_hidden = product_nt(down_in, wd).astype(low).astype(f32)
    grad_gate_pre = (grad_hidden * up_pre * sigma * (1.0 + gate_pre * (1.0 - sigma))).astype(low)
    grad_up_pre = (grad_hidden * silu_gate).astype(low)
    grad_normed = partial_sum(
        lambda part: product_nt(grad_gate_pre[part], wg) + product_nt(grad_up_pre[part], wu)
    )
    grad_gate = product_tn(normed, grad_gate_pre).astype(low)
    grad_up = product_tn(normed, grad_up_pre).astype(low)
    grad_resid_norm, grad_ffn_gain = middle_pull(grad_normed.astype(low).astype(f32))
    grad_resid = grad_outer + grad_resid_norm
    branch_in = jnp.concatenate(group_gather(grad_resid.astype(low)), axis=0)

    down_sums = wide_sum(grad_down.reshape(wide_size, hid_rows, 1, D), 0, wide_size)
    gate_sums = wide_sum(grad_gate.reshape(GROUP, wide_size, rows, hid_g), 1, wide_size)
    up_sums = wide_sum(grad_up.reshape(GROUP, wide_size, rows, hid_g), 1, wide_size)

    grad_mixed = product_nt(branch_in, wo).astype(low)
    grad_out = product_tn(mixed, branch_in).astype(low)
    grad_pack = per_sequence(
        mix_back_kernel, "mix_back", count, (PACK, WIN_G), PACK, low, group_lens, pack, grad_mixed
    )
    grad_mix = product_tn(conv_low, grad_pack).astype(low)
    grad_conv_low = partial_sum(lambda part: product_nt(grad_pack[part], w_mix))
    grad_front, grad_norm_gain, grad_taps = front_pull(grad_conv_low.astype(low).astype(f32))
    grad_tokens = (grad_resid + grad_front).astype(low)

    out_sums = wide_sum(grad_out.reshape(wide_size, rows, 1, D), 0, wide_size)
    mix_sums = wide_sum(grad_mix.reshape(GROUP, wide_size, rows, PACK), 1, wide_size)

    def to_owner(halves):
        return group_exchange(jnp.concatenate(halves, axis=0).astype(low), me)

    def widen(pieces):
        return jnp.concatenate([piece.astype(f32) for piece in pieces], axis=1)

    mix_pieces = to_owner(mix_sums)
    edges = [0, LIN_G, 2 * LIN_G, 2 * LIN_G + WIN_G, 2 * LIN_G + 2 * WIN_G, PACK]
    grad_query, grad_key, grad_value, grad_query_window, grad_key_window = [
        widen([piece[:, a:b] for piece in mix_pieces]) for a, b in zip(edges, edges[1:])
    ]
    gains = jnp.concatenate(
        [grad_norm_gain[None], grad_taps, grad_ffn_gain[None], jnp.zeros((3, D), f32)], axis=0
    )
    gains = sum_everywhere(gains, wide_size).reshape(8, GROUP * wide_size, rows)
    gains = lax.dynamic_index_in_dim(gains, spot, 1, keepdims=False)
    return (
        block_out,
        grad_tokens,
        gains[0],
        gains[1 : 1 + CONV_K].T,
        grad_query,
        grad_key,
        grad_value,
        grad_query_window,
        grad_key_window,
        jnp.concatenate(out_sums, axis=2).reshape(rows, D),
        gains[1 + CONV_K],
        widen(to_owner(gate_sums)),
        widen(to_owner(up_sums)),
        jnp.concatenate(down_sums, axis=2).reshape(hid_rows, D),
    )


def solution(mesh):
    rows = P(("grp", "wide"), None)
    flat = P(("grp", "wide"))
    return jax.shard_map(
        functools.partial(shards, wide_size=mesh.shape["wide"]),
        mesh=mesh,
        in_specs=(rows, flat, rows, flat, rows, rows, rows, rows, rows, rows, rows, flat, rows, rows, rows),
        out_specs=(rows, rows, flat, rows, rows, rows, rows, rows, rows, rows, flat, rows, rows, rows),
        check_vma=False,
    )
```

time: 5540 us -> 1060 us (0.19)
  waiting for transfers between devices: 3400 us -> 444 us
  blocking collectives: 1720 us -> 0 us
  starting transfers between devices: 4.29 us -> 175 us
  matrix products: 295 us -> 140 us
  between operations: 16.1 us -> 84 us
    reduce_scatter x8 -> x0, waiting for transfers between devices: 2750 us -> none  [the longest x1 948 us: shards(): lax.psum_scatter(grad_gate, ('grp', 'wide'), scatter_dimension=0, tiled=T...]
    unnamed x3 -> x0, blocking collectives: 1650 us -> none
    all_gather x9 -> x0, waiting for transfers between devices: 644 us -> none  [the longest x1 140 us: shards(): lax.all_gather(w_down.astype(low_type), ('grp', 'wide'), axis=0, tiled=True)]
    ppermute x0 -> x192, waiting for transfers between devices: none -> 444 us  [the longest x70 234 us: wide_gather(): halves[d] = lax.ppermute(halves[d], 'wide', way)]
    ppermute x0 -> x192, starting transfers between devices: none -> 175 us  [the longest x70 71.7 us: wide_gather(): halves[d] = lax.ppermute(halves[d], 'wide', way)]
    dot_general x37 -> x20, matrix products: 291 us -> 140 us  [dot(): lax.dot_general(left, right, (((over_left,), (over_right,)), ((), ())), p...]
    all_gather x1 -> x0, blocking collectives: 65.9 us -> none  [shards(): lax.all_gather(conv_weight.astype(low_type), ('grp', 'wide'), axis=0, til...]
  transfers between devices with their start and end apart: 19 -> 192, of which waited for: 12 -> 105; matrix products, arithmetic and copies ran while one was open for 32% -> 24% of each run, Pallas kernels for 0% -> 2%
where the time goes in v1:
time: 1060 us; the launch traced here: 1050 us
  waiting for transfers between devices  444 us (42%)
  starting transfers between devices  175 us (17%)
  matrix products  140 us (13%)
  local copies, waits for them, and re-layouts  119 us (11%)
  between operations  84 us (8%)
  other arithmetic  68 us (6%)
  Pallas kernels  21.8 us (2%)
    ppermute x70, waiting for transfers between devices, wide_gather(): halves[d] = lax.ppermute(halves[d], 'wide', way)  234 us
    ppermute x70, waiting for transfers between devices, wide_sum(): sums[d] = lax.ppermute(sums[d].astype(low), 'wide', way)  145 us
    dot_general x20, matrix products, dot(): lax.dot_general(left, right, (((over_left,), (over_right,)), ((), ())), p...  140 us
    ppermute x70, starting transfers between devices, wide_gather(): halves[d] = lax.ppermute(halves[d], 'wide', way)  71.7 us
    ppermute x70, starting transfers between devices, wide_sum(): sums[d] = lax.ppermute(sums[d].astype(low), 'wide', way)  66.5 us
    ppermute x42, waiting for transfers between devices, swap(): return lax.ppermute(value, 'grp', [(i, i ^ over) for i in range(GROUP)])  50 us
    dynamic_update_slice x76, local copies, waits for them, and re-layouts, wide_gather(): lax.dynamic_update_slice(whole, jnp.expand_dims(halves[d], at), index)  25.4 us
    ppermute x42, starting transfers between devices, swap(): return lax.ppermute(value, 'grp', [(i, i ^ over) for i in range(GROUP)])  25.4 us
  transfers between devices with their start and end apart: 192, of which 105 were waited for; matrix products, arithmetic and copies ran while one was open for 24% of the time, Pallas kernels for 2%

profile of v1, /device:TPU:0, one launch (start us, length us, event | category | flops | bytes accessed | tf_op | source)
XLA Modules:
  0.0 1052.5 jit_solution(16542306921319450352)
XLA Ops:
  193.9 8.5 collective-permute-done.29
  228.8 7.6 collective-permute-done.49
  366.8 6.8 collective-permute-done.54
  378.0 6.9 collective-permute-done.87
  426.7 9.0 collective-permute-done.19
  437.6 12.1 %collective-permute-done.21 = bf16[2,64,1664]{2,0,1:T(2,128)(2,1)S(1)} collective-permute-done((bf16[2,64,1664]{2,0,1:T(2,128)(2,1)S(1)}, bf16[2,64,1664]{2,0,1:T(2,128)(2,1)S(1)}, u32[]{:S(2)}, u32[]{:S(2)}) %collective-permute-start.21) | collective-permute-done | bytes 426016 | tf_op jit(solution)/shard_map/ppermute | solution.py:206
  449.8 11.1 %collective-permute-done.22 = bf16[2,64,1664]{2,0,1:T(2,128)(2,1)S(1)} collective-permute-done((bf16[2,64,1664]{2,0,1:T(2,128)(2,1)S(1)}, bf16[2,64,1664]{2,0,1:T(2,128)(2,1)S(1)}, u32[]{:S(2)}, u32[]{:S(2)}) %collective-permute-start.22) | collective-permute-done | bytes 426016 | tf_op jit(solution)/shard_map/ppermute | solution.py:206
  461.6 11.3 %collective-permute-done.23 = bf16[2,64,1664]{2,0,1:T(2,128)(2,1)S(1)} collective-permute-done((bf16[2,64,1664]{2,0,1:T(2,128)(2,1)S(1)}, bf16[2,64,1664]{2,0,1:T(2,128)(2,1)S(1)}, u32[]{:S(2)}, u32[]{:S(2)}) %collective-permute-start.23) | collective-permute-done | bytes 426016 | tf_op jit(solution)/shard_map/ppermute | solution.py:206
  472.9 8.1 collective-permute-done.24
  484.6 9.3 fusion.82.pack_ref
  493.9 7.4 mix.1
  539.9 9.8 convolution_convert_fusion.4
  551.4 11.1 %collective-permute-done.43 = bf16[256,2048]{1,0:T(8,128)(2,1)S(1)} collective-permute-done((bf16[256,2048]{1,0:T(8,128)(2,1)S(1)}, bf16[256,2048]{1,0:T(8,128)(2,1)S(1)}, u32[]{:S(2)}, u32[]{:S(2)}) %collective-permute-start.43) | collective-permute-done | bytes 1048608 | tf_op jit(solution)/shard_map/ppermute | solution.py:141
  565.2 9.8 fusion.137
  575.1 16.2 %fusion.2 = (bf16[1024,1376]{0,1:T(8,128)(2,1)}, bf16[1024,1376]{0,1:T(8,128)(2,1)}, bf16[1024,1376]{0,1:T(8,128)(2,1)}) fusion(bf16[1024,1376]{0,1:T(8,128)(2,1)} %convolution_convert_fusion.4, f32[1024,1376]{0,1:T(8,128)} %fusion.137, bf16[2048,1376]{1,0:T(8,128)(2,1)} %bitcast.837, bf16[256,2048]{1,0:T(8,128)(2,1)} %copy-done.77, ...), kind=kOutput, calls=%fused_computation.9 | convolution fusion | flops 5810683904 | bytes 26738688 | tf_op jit(solution)/shard_map/dot_general | solution.py:29
  591.4 8.6 fusion.20
  629.7 9.8 convolution_convert_fusion.1
  639.4 8.3 copy.350
  651.8 10.2 convolution_convert_fusion
  662.0 8.3 copy.364
  674.4 10.3 convolution_convert_fusion.2
  703.9 7.4 collective-permute-done.152
  713.2 12.1 %collective-permute-done.179 = bf16[172,1,1024]{2,0,1:T(8,128)(2,1)S(1)} collective-permute-done((bf16[172,1,1024]{2,0,1:T(8,128)(2,1)S(1)}, bf16[172,1,1024]{2,0,1:T(8,128)(2,1)S(1)}, u32[]{:S(2)}, u32[]{:S(2)}) %collective-permute-start.179) | collective-permute-done | bytes 352288 | tf_op jit(solution)/shard_map/ppermute | solution.py:236
  746.9 7.1 collective-permute-done.180
  770.0 7.2 collective-permute-done.181
  820.3 7.1 collective-permute-done.183
  837.3 10.6 %collective-permute-done.184 = bf16[172,1,1024]{2,0,1:T(8,128)(2,1)S(1)} collective-permute-done((bf16[172,1,1024]{2,0,1:T(8,128)(2,1)S(1)}, bf16[172,1,1024]{2,0,1:T(8,128)(2,1)S(1)}, u32[]{:S(2)}, u32[]{:S(2)}) %collective-permute-start.184) | collective-permute-done | bytes 352288 | tf_op jit(solution)/shard_map/ppermute | solution.py:236
  890.9 14.4 %mix_back.1 = bf16[1024,1664]{1,0:T(8,128)(2,1)S(1)} custom-call(s32[4]{0:T(128)S(1)} %copy-done.4, f32[1024,1664]{1,0:T(8,128)S(1)} %bitcast.792, bf16[1024,512]{1,0:T(8,128)(2,1)S(1)} %convolution_convert_fusion.12.grad_ref), custom_call_target="tpu_custom_call" | custom-call | flops 2000000000 | bytes 10000000 | tf_op jit(solution)/shard_map/mix_back/pallas_call | solution.py:125
  915.1 9.6 convolution_convert_fusion.3
  976.8 8.9 collective-permute-done.107
  995.1 8.5 collective-permute-done.124
  1009.8 8.5 collective-permute-done.110
  (850 shorter events, 666.6 us)
Async XLA Ops:
  2.7 50.8 %collective-permute-start = (bf16[1,8,64]{2,1,0:T(8,128)(2,1)S(1)}, bf16[1,8,64]{2,1,0:T(8,128)(2,1)S(1)}, u32[]{:S(2)}, u32[]{:S(2)}) collective-permute-start(bf16[1,8,64]{2,1,0:T(8,128)(2,1)S(1)} %concatenate.140), channel_id=1, source_target_pairs={{0,1},{1,0},{2,3},{3,2},{4,5},{5,4},{6,7},{7,6},{8,9},{9,8},{10,11... | collective-permute-start | bytes 3080 | tf_op jit(solution)/shard_map/ppermute | solution.py:173
  15.7 152.4 %collective-permute-start.10 = (bf16[64,1664]{1,0:T(8,128)(2,1)}, bf16[64,1664]{1,0:T(8,128)(2,1)}, u32[]{:S(2)}, u32[]{:S(2)}) collective-permute-start(bf16[64,1664]{1,0:T(8,128)(2,1)} %bitcast.775), channel_id=1, source_target_pairs={{0,24},{8,16},{16,8},{24,0},{1,25},{9,17},{17,9},{25,1},{2,26},{10... | collective-permute-start | bytes 638984 | tf_op jit(solution)/shard_map/ppermute | solution.py:141
  17.0 153.5 %collective-permute-start.9 = (bf16[64,1664]{1,0:T(8,128)(2,1)}, bf16[64,1664]{1,0:T(8,128)(2,1)}, u32[]{:S(2)}, u32[]{:S(2)}) collective-permute-start(bf16[64,1664]{1,0:T(8,128)(2,1)} %bitcast.776), channel_id=1, source_target_pairs={{0,16},{8,24},{16,0},{24,8},{1,17},{9,25},{17,1},{25,9},{2,18},{10... | collective-permute-start | bytes 638984 | tf_op jit(solution)/shard_map/ppermute | solution.py:141
  18.7 130.3 %collective-permute-start.25 = (bf16[64,1,1024]{2,0,1:T(8,128)(2,1)}, bf16[64,1,1024]{2,0,1:T(8,128)(2,1)}, u32[]{:S(2)}, u32[]{:S(2)}) collective-permute-start(bf16[64,1,1024]{2,0,1:T(8,128)(2,1)} %get-tuple-element.166), channel_id=1, source_target_pairs={{0,2},{2,4},{4,6},{6,7},{7,5},{5,3},{3,1},{1,0},{8,10},{10,12},{12... | collective-permute-start | bytes 393224 | tf_op jit(solution)/shard_map/ppermute | solution.py:206
  20.2 130.9 %collective-permute-start.26 = (bf16[64,1,1024]{2,0,1:T(8,128)(2,1)}, bf16[64,1,1024]{2,0,1:T(8,128)(2,1)}, u32[]{:S(2)}, u32[]{:S(2)}) collective-permute-start(bf16[64,1,1024]{2,0,1:T(8,128)(2,1)} %get-tuple-element.165), channel_id=1, source_target_pairs={{2,0},{4,2},{6,4},{7,6},{5,7},{3,5},{1,3},{0,1},{10,8},{12,10},{14... | collective-permute-start | bytes 393224 | tf_op jit(solution)/shard_map/ppermute | solution.py:206
  78.8 62.2 %collective-permute-start.4 = (bf16[16,8,64]{2,1,0:T(8,128)(2,1)S(1)}, bf16[16,8,64]{2,1,0:T(8,128)(2,1)S(1)}, u32[]{:S(2)}, u32[]{:S(2)}) collective-permute-start(bf16[16,8,64]{2,1,0:T(8,128)(2,1)S(1)} %maximum_select_fusion.1), channel_id=1, source_target_pairs={{0,16},{8,24},{16,0},{24,8},{1,17},{9,25},{17,1},{25,9},{2,18},{10... | collective-permute-start | bytes 49160 | tf_op jit(solution)/shard_map/ppermute | solution.py:173
  165.3 25.8 %collective-permute-start.80 = (bf16[172,1,1024]{2,0,1:T(8,128)(2,1)}, bf16[172,1,1024]{2,0,1:T(8,128)(2,1)S(1)}, u32[]{:S(2)}, u32[]{:S(2)}) collective-permute-start(bf16[172,1,1024]{2,0,1:T(8,128)(2,1)} %get-tuple-element.163), channel_id=1, source_target_pairs={{2,0},{4,2},{6,4},{7,6},{5,7},{3,5},{1,3},{0,1},{10,8},{12,10},{14... | collective-permute-start | bytes 1056776 | tf_op jit(solution)/shard_map/ppermute | solution.py:206
  168.1 345.1 %collective-permute-start.97 = (bf16[256,2048]{1,0:T(8,128)(2,1)}, bf16[256,2048]{1,0:T(8,128)(2,1)}, u32[]{:S(2)}, u32[]{:S(2)}) collective-permute-start(bf16[256,2048]{1,0:T(8,128)(2,1)} %fusion.17), channel_id=1, source_target_pairs={{0,16},{8,24},{16,0},{24,8},{1,17},{9,25},{17,1},{25,9},{2,18},{10... | collective-permute-start | bytes 3145736 | tf_op jit(solution)/shard_map/ppermute | solution.py:141
  170.6 175.0 %collective-permute-start.6 = (bf16[256,2048]{1,0:T(8,128)(2,1)S(1)}, bf16[256,2048]{1,0:T(8,128)(2,1)S(1)}, u32[]{:S(2)}, u32[]{:S(2)}) collective-permute-start(bf16[256,2048]{1,0:T(8,128)(2,1)S(1)} %copy-done.46), channel_id=1, source_target_pairs={{0,16},{8,24},{16,0},{24,8},{1,17},{9,25},{17,1},{25,9},{2,18},{10... | collective-permute-start | bytes 3145736 | tf_op jit(solution)/shard_map/ppermute | solution.py:141
  188.6 292.4 %collective-permute-start.5 = (bf16[256,2048]{1,0:T(8,128)(2,1)S(1)}, bf16[256,2048]{1,0:T(8,128)(2,1)S(1)}, u32[]{:S(2)}, u32[]{:S(2)}) collective-permute-start(bf16[256,2048]{1,0:T(8,128)(2,1)S(1)} %copy-done.46), channel_id=1, source_target_pairs={{0,8},{8,0},{16,24},{24,16},{1,9},{9,1},{17,25},{25,17},{2,10},{10... | collective-permute-start | bytes 3145736 | tf_op jit(solution)/shard_map/ppermute | solution.py:141
  188.7 29.5 %collective-permute-start.65 = (bf16[2,64,1376]{2,1,0:T(8,128)(2,1)S(1)}, bf16[2,64,1376]{2,1,0:T(8,128)(2,1)S(1)}, u32[]{:S(2)}, u32[]{:S(2)}) collective-permute-start(bf16[2,64,1376]{2,1,0:T(8,128)(2,1)S(1)} %pad_maximum_fusion.20), channel_id=1, source_target_pairs={{0,2},{2,4},{4,6},{6,7},{7,5},{5,3},{3,1},{1,0},{8,10},{10,12},{12... | collective-permute-start | bytes 1056776 | tf_op jit(solution)/shard_map/ppermute | solution.py:206
  346.5 136.7 %collective-permute-start.7 = (bf16[256,2048]{1,0:T(8,128)(2,1)S(1)}, bf16[256,2048]{1,0:T(8,128)(2,1)S(1)}, u32[]{:S(2)}, u32[]{:S(2)}) collective-permute-start(bf16[256,2048]{1,0:T(8,128)(2,1)S(1)} %collective-permute-done.6), channel_id=1, source_target_pairs={{0,8},{8,0},{16,24},{24,16},{1,9},{9,1},{17,25},{25,17},{2,10},{10... | collective-permute-start | bytes 3145736 | tf_op jit(solution)/shard_map/ppermute | solution.py:141
  435.7 67.0 %collective-permute-start.75 = (bf16[2,64,1376]{2,1,0:T(8,128)(2,1)S(1)}, bf16[2,64,1376]{2,1,0:T(8,128)(2,1)S(1)}, u32[]{:S(2)}, u32[]{:S(2)}) collective-permute-start(bf16[2,64,1376]{2,1,0:T(8,128)(2,1)S(1)} %collective-permute-done.73), channel_id=1, source_target_pairs={{0,2},{2,4},{4,6},{6,7},{7,5},{5,3},{3,1},{1,0},{8,10},{10,12},{12... | collective-permute-start | bytes 1056776 | tf_op jit(solution)/shard_map/ppermute | solution.py:206
  481.1 26.6 %collective-permute-start.58 = (bf16[2,64,1376]{2,1,0:T(8,128)(2,1)}, bf16[2,64,1376]{2,1,0:T(8,128)(2,1)}, u32[]{:S(2)}, u32[]{:S(2)}) collective-permute-start(bf16[2,64,1376]{2,1,0:T(8,128)(2,1)} %collective-permute-done.56), channel_id=1, source_target_pairs={{0,2},{2,4},{4,6},{6,7},{7,5},{5,3},{3,1},{1,0},{8,10},{10,12},{12... | collective-permute-start | bytes 1056776 | tf_op jit(solution)/shard_map/ppermute | solution.py:206
  483.2 27.7 %collective-permute-start.59 = (bf16[2,64,1376]{2,1,0:T(8,128)(2,1)}, bf16[2,64,1376]{2,1,0:T(8,128)(2,1)}, u32[]{:S(2)}, u32[]{:S(2)}) collective-permute-start(bf16[2,64,1376]{2,1,0:T(8,128)(2,1)} %collective-permute-done.57), channel_id=1, source_target_pairs={{2,0},{4,2},{6,4},{7,6},{5,7},{3,5},{1,3},{0,1},{10,8},{12,10},{14... | collective-permute-start | bytes 1056776 | tf_op jit(solution)/shard_map/ppermute | solution.py:206
  507.7 25.5 %collective-permute-start.41 = (bf16[256,2048]{1,0:T(8,128)(2,1)S(1)}, bf16[256,2048]{1,0:T(8,128)(2,1)}, u32[]{:S(2)}, u32[]{:S(2)}) collective-permute-start(bf16[256,2048]{1,0:T(8,128)(2,1)S(1)} %add_convert_fusion.7), channel_id=1, source_target_pairs={{0,16},{8,24},{16,0},{24,8},{1,17},{9,25},{17,1},{25,9},{2,18},{10... | collective-permute-start | bytes 3145736 | tf_op jit(solution)/shard_map/ppermute | solution.py:141
  521.2 28.5 %collective-permute-start.77 = (bf16[2,64,1376]{2,1,0:T(8,128)(2,1)S(1)}, bf16[2,64,1376]{2,1,0:T(8,128)(2,1)}, u32[]{:S(2)}, u32[]{:S(2)}) collective-permute-start(bf16[2,64,1376]{2,1,0:T(8,128)(2,1)S(1)} %collective-permute-done.75), channel_id=1, source_target_pairs={{0,2},{2,4},{4,6},{6,7},{7,5},{5,3},{3,1},{1,0},{8,10},{10,12},{12... | collective-permute-start | bytes 1056776 | tf_op jit(solution)/shard_map/ppermute | solution.py:206
  528.7 33.9 %collective-permute-start.78 = (bf16[2,64,1376]{2,1,0:T(8,128)(2,1)}, bf16[2,64,1376]{2,1,0:T(8,128)(2,1)S(1)}, u32[]{:S(2)}, u32[]{:S(2)}) collective-permute-start(bf16[2,64,1376]{2,1,0:T(8,128)(2,1)} %copy-done.54), channel_id=1, source_target_pairs={{2,0},{4,2},{6,4},{7,6},{5,7},{3,5},{1,3},{0,1},{10,8},{12,10},{14... | collective-permute-start | bytes 1056776 | tf_op jit(solution)/shard_map/ppermute | solution.py:206
  533.2 30.2 %collective-permute-start.60 = (bf16[2,64,1376]{2,1,0:T(8,128)(2,1)}, bf16[2,64,1376]{2,1,0:T(8,128)(2,1)S(1)}, u32[]{:S(2)}, u32[]{:S(2)}) collective-permute-start(bf16[2,64,1376]{2,1,0:T(8,128)(2,1)} %collective-permute-done.58), channel_id=1, source_target_pairs={{0,2},{2,4},{4,6},{6,7},{7,5},{5,3},{3,1},{1,0},{8,10},{10,12},{12... | collective-permute-start | bytes 1056776 | tf_op jit(solution)/shard_map/ppermute | solution.py:206
  536.7 26.8 %collective-permute-start.61 = (bf16[2,64,1376]{2,1,0:T(8,128)(2,1)}, bf16[2,64,1376]{2,1,0:T(8,128)(2,1)S(1)}, u32[]{:S(2)}, u32[]{:S(2)}) collective-permute-start(bf16[2,64,1376]{2,1,0:T(8,128)(2,1)} %collective-permute-done.59), channel_id=1, source_target_pairs={{2,0},{4,2},{6,4},{7,6},{5,7},{3,5},{1,3},{0,1},{10,8},{12,10},{14... | collective-permute-start | bytes 1056776 | tf_op jit(solution)/shard_map/ppermute | solution.py:206
  620.4 108.6 %collective-permute-start.100 = (bf16[256,2048]{1,0:T(8,128)(2,1)}, bf16[256,2048]{1,0:T(8,128)(2,1)S(1)}, u32[]{:S(2)}, u32[]{:S(2)}) collective-permute-start(bf16[256,2048]{1,0:T(8,128)(2,1)} %slice.269), channel_id=1, source_target_pairs={{0,8},{8,0},{16,24},{24,16},{1,9},{9,1},{17,25},{25,17},{2,10},{10... | collective-permute-start | bytes 3145736 | tf_op jit(solution)/shard_map/ppermute | solution.py:141
  649.7 42.1 %collective-permute-start.151 = (bf16[2,64,1376]{2,1,0:T(8,128)(2,1)}, bf16[2,64,1376]{2,1,0:T(8,128)(2,1)}, u32[]{:S(2)}, u32[]{:S(2)}) collective-permute-start(bf16[2,64,1376]{2,1,0:T(8,128)(2,1)} %get-tuple-element.95), channel_id=1, source_target_pairs={{2,0},{4,2},{6,4},{7,6},{5,7},{3,5},{1,3},{0,1},{10,8},{12,10},{14... | collective-permute-start | bytes 1056776 | tf_op jit(solution)/shard_map/ppermute | solution.py:236
  650.3 41.9 %collective-permute-start.144 = (bf16[2,64,1376]{2,1,0:T(8,128)(2,1)}, bf16[2,64,1376]{2,1,0:T(8,128)(2,1)}, u32[]{:S(2)}, u32[]{:S(2)}) collective-permute-start(bf16[2,64,1376]{2,1,0:T(8,128)(2,1)} %get-tuple-element.96), channel_id=1, source_target_pairs={{0,2},{2,4},{4,6},{6,7},{7,5},{5,3},{3,1},{1,0},{8,10},{10,12},{12... | collective-permute-start | bytes 1056776 | tf_op jit(solution)/shard_map/ppermute | solution.py:236
  713.1 90.7 %collective-permute-start.99 = (bf16[256,2048]{1,0:T(8,128)(2,1)S(1)}, bf16[256,2048]{1,0:T(8,128)(2,1)S(1)}, u32[]{:S(2)}, u32[]{:S(2)}) collective-permute-start(bf16[256,2048]{1,0:T(8,128)(2,1)S(1)} %copy-done.43), channel_id=1, source_target_pairs={{0,8},{8,0},{16,24},{24,16},{1,9},{9,1},{17,25},{25,17},{2,10},{10... | collective-permute-start | bytes 3145736 | tf_op jit(solution)/shard_map/ppermute | solution.py:141
  777.2 27.0 %collective-permute-start.101 = (bf16[256,2048]{1,0:T(8,128)(2,1)S(1)}, bf16[256,2048]{1,0:T(8,128)(2,1)S(1)}, u32[]{:S(2)}, u32[]{:S(2)}) collective-permute-start(bf16[256,2048]{1,0:T(8,128)(2,1)S(1)} %add_convert_fusion.5), channel_id=1, source_target_pairs={{0,16},{8,24},{16,0},{24,8},{1,17},{9,25},{17,1},{25,9},{2,18},{10... | collective-permute-start | bytes 3145736 | tf_op jit(solution)/shard_map/ppermute | solution.py:141
  811.9 48.7 %collective-permute-start.103 = (bf16[256,2048]{1,0:T(8,128)(2,1)}, bf16[256,2048]{1,0:T(8,128)(2,1)}, u32[]{:S(2)}, u32[]{:S(2)}) collective-permute-start(bf16[256,2048]{1,0:T(8,128)(2,1)} %fusion.135), channel_id=1, source_target_pairs={{0,16},{8,24},{16,0},{24,8},{1,17},{9,25},{17,1},{25,9},{2,18},{10... | collective-permute-start | bytes 3145736 | tf_op jit(solution)/shard_map/ppermute | solution.py:141
  847.9 30.7 %collective-permute-start.102 = (bf16[256,2048]{1,0:T(8,128)(2,1)}, bf16[256,2048]{1,0:T(8,128)(2,1)}, u32[]{:S(2)}, u32[]{:S(2)}) collective-permute-start(bf16[256,2048]{1,0:T(8,128)(2,1)} %fusion.135), channel_id=1, source_target_pairs={{0,8},{8,0},{16,24},{24,16},{1,9},{9,1},{17,25},{25,17},{2,10},{10... | collective-permute-start | bytes 3145736 | tf_op jit(solution)/shard_map/ppermute | solution.py:141
  912.7 38.2 %collective-permute-start.106 = (bf16[256,2048]{1,0:T(8,128)(2,1)}, bf16[256,2048]{1,0:T(8,128)(2,1)S(1)}, u32[]{:S(2)}, u32[]{:S(2)}) collective-permute-start(bf16[256,2048]{1,0:T(8,128)(2,1)} %slice.275), channel_id=1, source_target_pairs={{0,8},{8,0},{16,24},{24,16},{1,9},{9,1},{17,25},{25,17},{2,10},{10... | collective-permute-start | bytes 3145736 | tf_op jit(solution)/shard_map/ppermute | solution.py:141
  943.6 31.2 %collective-permute-start.105 = (bf16[256,2048]{1,0:T(8,128)(2,1)S(1)}, bf16[256,2048]{1,0:T(8,128)(2,1)S(1)}, u32[]{:S(2)}, u32[]{:S(2)}) collective-permute-start(bf16[256,2048]{1,0:T(8,128)(2,1)S(1)} %slice.272), channel_id=1, source_target_pairs={{0,8},{8,0},{16,24},{24,16},{1,9},{9,1},{17,25},{25,17},{2,10},{10... | collective-permute-start | bytes 3145736 | tf_op jit(solution)/shard_map/ppermute | solution.py:141
  959.6 26.1 %collective-permute-start.107 = (bf16[256,2048]{1,0:T(8,128)(2,1)S(1)}, bf16[256,2048]{1,0:T(8,128)(2,1)S(1)}, u32[]{:S(2)}, u32[]{:S(2)}) collective-permute-start(bf16[256,2048]{1,0:T(8,128)(2,1)S(1)} %add_convert_fusion.3), channel_id=1, source_target_pairs={{0,16},{8,24},{16,0},{24,8},{1,17},{9,25},{17,1},{25,9},{2,18},{10... | collective-permute-start | bytes 3145736 | tf_op jit(solution)/shard_map/ppermute | solution.py:141
  965.9 59.8 %collective-permute-start.93 = (bf16[256,2048]{1,0:T(8,128)(2,1)S(1)}, bf16[256,2048]{1,0:T(8,128)(2,1)S(1)}, u32[]{:S(2)}, u32[]{:S(2)}) collective-permute-start(bf16[256,2048]{1,0:T(8,128)(2,1)S(1)} %copy-done.42), channel_id=1, source_target_pairs={{0,8},{8,0},{16,24},{24,16},{1,9},{9,1},{17,25},{25,17},{2,10},{10... | collective-permute-start | bytes 3145736 | tf_op jit(solution)/shard_map/ppermute | solution.py:141
  971.9 53.8 %collective-permute-start.95 = (bf16[256,2048]{1,0:T(8,128)(2,1)S(1)}, bf16[256,2048]{1,0:T(8,128)(2,1)S(1)}, u32[]{:S(2)}, u32[]{:S(2)}) collective-permute-start(bf16[256,2048]{1,0:T(8,128)(2,1)S(1)} %copy-done.41), channel_id=1, source_target_pairs={{0,16},{8,24},{16,0},{24,8},{1,17},{9,25},{17,1},{25,9},{2,18},{10... | collective-permute-start | bytes 3145736 | tf_op jit(solution)/shard_map/ppermute | solution.py:141
  (257 other events, 4135.1 us)

commit v2 on v1

v2 whole, which is shorter than its diff:
```python
import functools

import jax
import jax.numpy as jnp
from jax import lax
from jax.experimental import pallas as pl
from jax.experimental.pallas import tpu as pltpu
from jax.sharding import PartitionSpec as P

D = 2048
HEADS = 16
FEAT = 16
WINDOW = 64
CONV_K = 3
VHEAD = 128
GROUP = 4
HEADS_G = HEADS // GROUP
LIN_G = HEADS_G * FEAT
WIN_G = HEADS_G * VHEAD
PACK = 2 * LIN_G + 3 * WIN_G

low = jnp.bfloat16
f32 = jnp.float32

CYCLES = {8: (0, 2, 4, 6, 7, 5, 3, 1)}


def dot(left, right, over_left, over_right):
    return lax.dot_general(
        left, right, (((over_left,), (over_right,)), ((), ())), preferred_element_type=f32
    )


def product(left, right):
    return dot(left, right, 1, 0)


def product_tn(left, right):
    return dot(left, right, 0, 0)


def product_nt(left, right):
    return dot(left, right, 1, 1)


def rms_norm(values, gain_vec):
    return values * lax.rsqrt(jnp.mean(values * values, axis=-1, keepdims=True) + 1e-06) * gain_vec


def short_conv(values, taps):
    total = values * taps[0]
    for shift in range(1, CONV_K):
        moved = jnp.concatenate(
            [jnp.zeros((shift, values.shape[1]), f32), values[:-shift]], axis=0
        )
        total = total + moved * taps[shift]
    return total


def front_part(inputs, g_one, taps):
    return short_conv(rms_norm(inputs, g_one), taps)


def head_parts(pack_ref, head, keep, in_window):
    query = pack_ref[:, FEAT * head : FEAT * (head + 1)].astype(low)
    key = pack_ref[:, LIN_G + FEAT * head : LIN_G + FEAT * (head + 1)].astype(low)
    start = 2 * LIN_G + VHEAD * head
    value = pack_ref[:, start : start + VHEAD].astype(low)
    start += WIN_G
    query_win = pack_ref[:, start : start + VHEAD].astype(low)
    start += WIN_G
    key_win = pack_ref[:, start : start + VHEAD].astype(low)
    scores = product_nt(query, key) * FEAT**-0.5
    kernel = jnp.where(keep, 1.0 + scores + 0.5 * scores * scores, 0.0)
    over = 1.0 / jnp.sum(kernel, axis=1, keepdims=True)
    share = kernel * over
    logits = jnp.where(in_window, product_nt(query_win, key_win) * VHEAD**-0.5, -1e30)
    raised = jnp.exp(logits - jnp.max(logits, axis=1, keepdims=True))
    probs = raised * (1.0 / jnp.sum(raised, axis=1, keepdims=True))
    return query, key, value, query_win, key_win, scores, over, share, probs


def masks(length, count):
    row = lax.broadcasted_iota(jnp.int32, (count, count), 0)
    col = lax.broadcasted_iota(jnp.int32, (count, count), 1)
    keep = (row >= col) & (col < length)
    return keep, keep & (row - col < WINDOW)


def mix_kernel(lens_ref, pack_ref, mixed_ref):
    keep, in_window = masks(lens_ref[pl.program_id(0)], pack_ref.shape[0])
    for head in range(HEADS_G):
        parts = head_parts(pack_ref, head, keep, in_window)
        value, share, probs = parts[2], parts[7], parts[8]
        out = product((share + probs).astype(low), value)
        mixed_ref[:, VHEAD * head : VHEAD * (head + 1)] = out.astype(low)


def mix_back_kernel(lens_ref, pack_ref, grad_ref, out_ref):
    keep, in_window = masks(lens_ref[pl.program_id(0)], pack_ref.shape[0])
    grad_query, grad_key = [], []
    for head in range(HEADS_G):
        query, key, value, query_win, key_win, scores, over, share, probs = head_parts(
            pack_ref, head, keep, in_window
        )
        grad = grad_ref[:, VHEAD * head : VHEAD * (head + 1)]
        weights = product_nt(grad, value)
        grad_raw = probs * (weights - jnp.sum(weights * probs, axis=1, keepdims=True))
        grad_raw = (grad_raw * VHEAD**-0.5).astype(low)
        centred = weights - jnp.sum(weights * share, axis=1, keepdims=True)
        grad_scores = jnp.where(keep, centred * (over * FEAT**-0.5) * (1.0 + scores), 0.0)
        grad_scores = grad_scores.astype(low)
        start = 2 * LIN_G + VHEAD * head
        out_ref[:, start : start + VHEAD] = product_tn((share + probs).astype(low), grad).astype(low)
        start += WIN_G
        out_ref[:, start : start + VHEAD] = product(grad_raw, key_win).astype(low)
        start += WIN_G
        out_ref[:, start : start + VHEAD] = product_tn(grad_raw, query_win).astype(low)
        grad_query.append(product(grad_scores, key).astype(low))
        grad_key.append(product_tn(grad_scores, query).astype(low))
    out_ref[:, : 2 * LIN_G] = jnp.concatenate(grad_query + grad_key, axis=1)


def per_sequence(body, name, count, widths, out_width, out_type, lens, *arrays):
    return pl.pallas_call(
        body,
        grid=(GROUP,),
        in_specs=[pl.BlockSpec(memory_space=pltpu.SMEM)]
        + [pl.BlockSpec((count, width), lambda i: (i, 0)) for width in widths],
        out_specs=pl.BlockSpec((count, out_width), lambda i: (i, 0)),
        out_shape=jax.ShapeDtypeStruct((GROUP * count, out_width), out_type),
        compiler_params=pltpu.CompilerParams(vmem_limit_bytes=32 * 1024 * 1024),
        cost_estimate=pl.CostEstimate(
            flops=2_000_000_000, bytes_accessed=10_000_000, transcendentals=1_000_000
        ),
        name=name,
    )(lens, *arrays)


bar = lax.optimization_barrier


def swap(value, over):
    return lax.ppermute(value, "grp", [(i, i ^ over) for i in range(GROUP)])


def group_gather(own):
    peer = swap(own, 1)
    across = swap(own, 2)
    return own, peer, across, swap(across, 1)


def reorder(stack):
    me = lax.axis_index("grp")
    return jnp.concatenate([lax.dynamic_slice_in_dim(stack, me ^ r, 1) for r in range(GROUP)])


def after(token, *values):
    return bar((*values, token))[:-1]


def steps_of(axis, size):
    step = 1
    while step < size:
        yield axis, size, step
        step *= 2


def everywhere(value, wide_size):
    stack = value[None]
    for axis, size, step in list(steps_of("wide", wide_size)) + list(steps_of("grp", GROUP)):
        other = lax.ppermute(stack, axis, [(i, i ^ step) for i in range(size)])
        upper = (lax.axis_index(axis) & step) > 0
        stack = jnp.where(
            upper, jnp.concatenate([other, stack], 0), jnp.concatenate([stack, other], 0)
        )
    return stack


def sum_everywhere(value, wide_size):
    for axis, size, step in list(steps_of("grp", GROUP)) + list(steps_of("wide", wide_size)):
        value = value + lax.ppermute(value, axis, [(i, i ^ step) for i in range(size)])
    return value


SMEM = pl.BlockSpec(memory_space=pltpu.SMEM)
VMEM = pl.BlockSpec(memory_space=pltpu.VMEM)
ANY = pl.BlockSpec(memory_space=pl.ANY)


def params(mib):
    return pltpu.CompilerParams(vmem_limit_bytes=mib * 1024 * 1024)


def cost(nbytes, flops=0):
    return pl.CostEstimate(flops=flops, bytes_accessed=nbytes, transcendentals=0)


def split_mixer(table, weights):
    rows = weights[0].shape[0]

    def body(table_ref, *refs):
        out = refs[-1]
        for j in range(GROUP):
            pieces = []
            for ref in refs[:-1]:
                width = ref.shape[1] // GROUP
                pieces.append(ref[:, j * width : (j + 1) * width].astype(low))
            out[j ^ table_ref[0]] = jnp.concatenate(pieces, axis=1)

    return pl.pallas_call(
        body,
        in_specs=[SMEM] + [VMEM] * len(weights),
        out_specs=VMEM,
        out_shape=jax.ShapeDtypeStruct((GROUP, rows, PACK), low),
        compiler_params=params(24),
        cost_estimate=cost(rows * PACK * GROUP * 6),
        name="split_mixer",
    )(table, *weights)


def split_gate_up(table, w_gate, w_up, wide_size, part, part_p):
    rows = w_gate.shape[0]
    hid_p = wide_size * part_p

    def body(table_ref, gate_ref, up_ref, out):
        fill = jnp.zeros((rows, part_p - part), f32)
        for j in range(GROUP):
            pieces = []
            for ref in (gate_ref, up_ref):
                for w in range(wide_size):
                    start = (j * wide_size + w) * part
                    pieces += [ref[:, start : start + part], fill]
            out[j ^ table_ref[0]] = jnp.concatenate(pieces, axis=1).astype(low)

    return pl.pallas_call(
        body,
        in_specs=[SMEM, VMEM, VMEM],
        out_specs=VMEM,
        out_shape=jax.ShapeDtypeStruct((GROUP, rows, 2 * hid_p), low),
        compiler_params=params(24),
        cost_estimate=cost(rows * hid_p * GROUP * 12),
        name="split_gate_up",
    )(table, w_gate, w_up)


def merge_gate_up(table, pieces, wide_size, part, part_p):
    rows = pieces[0].shape[0]
    hid_p = wide_size * part_p
    full = jax.ShapeDtypeStruct((rows, GROUP * wide_size * part), f32)

    def body(table_ref, a, b, c, d, gate_ref, up_ref, held):
        for r, ref in enumerate((a, b, c, d)):
            held[r] = ref[...].astype(f32)
        for at, out in ((0, gate_ref), (hid_p, up_ref)):
            for j in range(GROUP):
                block = held[j ^ table_ref[0]]
                parts = [block[:, at + w * part_p : at + w * part_p + part] for w in range(wide_size)]
                start = j * wide_size * part
                out[:, start : start + wide_size * part] = jnp.concatenate(parts, axis=1)

    return pl.pallas_call(
        body,
        in_specs=[SMEM] + [VMEM] * 4,
        out_specs=[VMEM, VMEM],
        out_shape=[full, full],
        scratch_shapes=[pltpu.VMEM((GROUP, rows, 2 * hid_p), f32)],
        compiler_params=params(24),
        cost_estimate=cost(rows * hid_p * GROUP * 12),
        name="merge_gate_up",
    )(table, *pieces)


def merge_mixer(table, pieces):
    rows = pieces[0].shape[0]
    widths = [LIN_G, LIN_G, WIN_G, WIN_G, WIN_G]

    def body(table_ref, a, b, c, d, *refs):
        outs, held = refs[:-1], refs[-1]
        for r, ref in enumerate((a, b, c, d)):
            held[r] = ref[...].astype(f32)
        blocks = [held[j ^ table_ref[0]] for j in range(GROUP)]
        at = 0
        for width, out in zip(widths, outs):
            out[...] = jnp.concatenate([block[:, at : at + width] for block in blocks], axis=1)
            at += width

    return pl.pallas_call(
        body,
        in_specs=[SMEM] + [VMEM] * 4,
        out_specs=[VMEM] * 5,
        out_shape=[jax.ShapeDtypeStruct((rows, GROUP * width), f32) for width in widths],
        scratch_shapes=[pltpu.VMEM((GROUP, rows, PACK), f32)],
        compiler_params=params(24),
        cost_estimate=cost(rows * PACK * GROUP * 6),
        name="merge_mixer",
    )(table, *pieces)


def place(table, ways, grouped, size):
    piece = ways[0][0]
    rows, width = piece.shape[-2:]
    shape = (GROUP, size, rows, width) if grouped else (size, rows, 2 * width)

    def body(table_ref, *refs):
        out, sems = refs[-2:]
        copies = []
        for d in (0, 1):
            for s in range(size):
                ref = refs[d * size + s]
                owner = table_ref[1 + d * size + s]
                if grouped:
                    for i in range(2):
                        copies.append((ref.at[i], out.at[(2 * d + i) ^ table_ref[0], owner]))
                else:
                    copies.append((ref, out.at[owner, :, d * width : (d + 1) * width]))
        copies = [pltpu.make_async_copy(of, to, sems.at[k]) for k, (of, to) in enumerate(copies)]
        for copy in copies:
            copy.start()
        for copy in copies:
            copy.wait()

    return pl.pallas_call(
        body,
        in_specs=[SMEM] + [ANY] * (2 * size),
        out_specs=ANY,
        out_shape=jax.ShapeDtypeStruct(shape, low),
        scratch_shapes=[pltpu.SemaphoreType.DMA(((4 if grouped else 2) * size,))],
        compiler_params=params(2),
        cost_estimate=cost(8 * size * rows * width * piece.ndim),
        name="place",
    )(table, *ways[0], *ways[1])


def pick_add(table, terms, got, step, size, keep_rows=None):
    grouped = terms.ndim == 4
    rows, width = terms.shape[-2:]
    k = (step + 1) % size
    if not grouped:
        width //= 2

    def body(table_ref, *refs):
        mine, outs = refs[:2], refs[-2:] if keep_rows is None else refs[-1:]
        for d in (0, 1):
            total = mine[d][...].reshape(rows, width).astype(f32)
            if got is not None:
                total = total + refs[2 + d][...].reshape(rows, width).astype(f32)
            if keep_rows is None:
                outs[d][...] = total.reshape(outs[d].shape).astype(low)
            else:
                outs[0][:, d * width : (d + 1) * width] = total[:keep_rows]

    def owner(table_ref, d):
        return table_ref[1 + d * size + k]

    if grouped:
        grid = (2,)
        term_specs = [
            pl.BlockSpec(
                (1, 1, rows, width),
                lambda i, t, d=d: ((2 * d + i) ^ t[0], owner(t, d), 0, 0),
            )
            for d in (0, 1)
        ]
        piece = pl.BlockSpec((1, rows, width), lambda i, t: (i, 0, 0))
        shape = jax.ShapeDtypeStruct((2, rows, width), low)
    else:
        grid = (1,)
        term_specs = [
            pl.BlockSpec((1, rows, width), lambda i, t, d=d: (owner(t, d), 0, d)) for d in (0, 1)
        ]
        piece = pl.BlockSpec((rows, width), lambda i, t: (0, 0))
        shape = jax.ShapeDtypeStruct((rows, width), low)
    out_specs, out_shape = [piece, piece], [shape, shape]
    if keep_rows is not None:
        out_specs = [pl.BlockSpec((keep_rows, 2 * width), lambda i, t: (0, 0))]
        out_shape = [jax.ShapeDtypeStruct((keep_rows, 2 * width), f32)]
    came = [] if got is None else list(got)

    return pl.pallas_call(
        body,
        grid_spec=pltpu.PrefetchScalarGridSpec(
            num_scalar_prefetch=1,
            grid=grid,
            in_specs=term_specs + [piece] * len(came),
            out_specs=out_specs,
        ),
        out_shape=out_shape,
        compiler_params=params(16),
        cost_estimate=cost(8 * rows * width * 3),
        name="pick_add",
    )(table, terms, terms, *came)


def round_ring(cycle, d):
    size = len(cycle)
    way = [(cycle[i], cycle[(i + 1) % size]) for i in range(size)]
    return way if d == 0 else [(to, of) for of, to in way]


class GatherRing:
    def __init__(self, halves, grouped, size, table):
        self.held = [[half] for half in halves]
        self.grouped, self.size, self.table = grouped, size, table
        self.steps = size - 1 if size in CYCLES else 0

    def step(self, token=None):
        if self.steps == 0:
            return
        self.steps -= 1
        for d, held in enumerate(self.held):
            value = held[-1] if token is None else after(token, held[-1])[0]
            held.append(lax.ppermute(value, "wide", round_ring(CYCLES[self.size], d)))

    def done(self, token=None):
        while self.steps:
            self.step()
        if self.size in CYCLES:
            ways = self.held
            if token is not None:
                ways = [list(after(token, *held)) for held in ways]
            out = place(self.table, ways, self.grouped, self.size)
        elif self.grouped:
            block = jnp.concatenate([self.held[0][0], self.held[1][0]], axis=0)
            out = jnp.moveaxis(lax.all_gather(block, "wide"), 0, 1)
            out = reorder(out)
        else:
            block = jnp.concatenate([self.held[0][0], self.held[1][0]], axis=1)
            out = lax.all_gather(block, "wide")
        return out.reshape(-1, out.shape[-1])


class SumRing:
    def __init__(self, terms, size, table, keep_rows=None):
        self.terms, self.size, self.table, self.keep_rows = terms, size, table, keep_rows
        self.at, self.got = 0, None
        self.left = size - 1 if size in CYCLES else 0

    def step(self, token=None):
        if self.left == 0:
            return
        self.left -= 1
        got = self.got
        if token is not None:
            got = after(token, *got) if got is not None else None
            if got is None:
                self.terms = after(token, self.terms)[0]
        sums = pick_add(self.table, self.terms, got, self.at, self.size)
        self.at += 1
        cycle = CYCLES[self.size]
        self.got = [lax.ppermute(sums[d], "wide", round_ring(cycle, d)) for d in (0, 1)]

    def done(self):
        while self.left:
            self.step()
        if self.size in CYCLES:
            out = pick_add(
                self.table, self.terms, self.got, self.at, self.size, self.keep_rows
            )
            return out if self.keep_rows is None else out[0]
        if self.keep_rows is None:
            full = lax.psum_scatter(
                self.terms.astype(f32), "wide", scatter_dimension=1, tiled=True
            )[:, 0]
            full = reorder(full).astype(low)
            return full[:2], full[2:]
        full = lax.psum_scatter(self.terms.astype(f32), "wide", scatter_dimension=0, tiled=True)
        return full[0, : self.keep_rows]


def table_of(wide_size):
    me = lax.axis_index("grp").astype(jnp.int32)
    if wide_size not in CYCLES:
        return me[None]
    cycle = CYCLES[wide_size]
    rows = []
    for w in range(wide_size):
        at = cycle.index(w)
        rows.append(
            [cycle[(at - s) % wide_size] for s in range(wide_size)]
            + [cycle[(at + s) % wide_size] for s in range(wide_size)]
        )
    row = lax.dynamic_index_in_dim(
        jnp.array(rows, jnp.int32), lax.axis_index("wide"), 0, keepdims=False
    )
    return jnp.concatenate([me[None], row])


def shards(
    tokens,
    lengths,
    cotangent,
    norm_gain,
    conv_weight,
    w_query,
    w_key,
    w_value,
    w_query_window,
    w_key_window,
    w_out,
    ffn_gain,
    w_gate,
    w_up,
    w_down,
    *,
    wide_size,
):
    me = lax.axis_index("grp")
    spot = me * wide_size + lax.axis_index("wide")
    count = tokens.shape[0]
    rows = w_query.shape[0]
    part = w_down.shape[0]
    part_p = -(-part // 16) * 16
    hid_p = wide_size * part_p
    length = lengths[0]
    is_valid = (jnp.arange(count, dtype=jnp.int32) < length).astype(f32)
    table = table_of(wide_size)

    small = jnp.concatenate(
        [
            norm_gain[None],
            conv_weight.T,
            ffn_gain[None],
            jnp.broadcast_to(length.astype(f32), (1, rows)),
            jnp.zeros((2, rows), f32),
        ],
        axis=0,
    ).astype(low)
    small_all = everywhere(small, wide_size)

    half = D // 2
    out_low = w_out.astype(low)
    out_ring = GatherRing([out_low[:, :half], out_low[:, half:]], False, wide_size, table)
    mixer_blocks = split_mixer(table, (w_query, w_key, w_value, w_query_window, w_key_window))
    mixer_got = [mixer_blocks[0]] + [swap(mixer_blocks[r], r) for r in range(1, GROUP)]
    mix_ring = GatherRing(
        [jnp.stack(mixer_got[:2]), jnp.stack(mixer_got[2:])], True, wide_size, table
    )
    gu_blocks = split_gate_up(table, w_gate, w_up, wide_size, part, part_p)
    gu_blocks = after(mixer_got[3], gu_blocks)[0]
    gu_got = [gu_blocks[0]] + [swap(gu_blocks[r], r) for r in range(1, GROUP)]
    gu_ring = GatherRing([jnp.stack(gu_got[:2]), jnp.stack(gu_got[2:])], True, wide_size, table)
    down_low = jnp.pad(w_down.astype(low), ((0, part_p - part), (0, 0)))
    down_ring = GatherRing([down_low[:, :half], down_low[:, half:]], False, wide_size, table)

    g_one, tap_0, tap_1, tap_2, g_two = [
        small_all[:, i].reshape(D).astype(f32) for i in range(5)
    ]
    taps = jnp.stack([tap_0, tap_1, tap_2])
    group_lens = small_all[:, 5, 0].astype(jnp.int32).reshape(GROUP, wide_size)
    group_lens = lax.dynamic_index_in_dim(group_lens, lax.axis_index("wide"), 1, keepdims=False)
    group_lens = reorder(group_lens)

    inputs = tokens.astype(f32)
    conv_out, front_pull = jax.vjp(front_part, inputs, g_one, taps)
    conv_low = jnp.concatenate(group_gather(conv_out.astype(low)), axis=0)
    grad_outer = cotangent.astype(f32) * is_valid[:, None]
    down_own = after(conv_low, grad_outer.astype(low))[0]
    down_in = jnp.concatenate(group_gather(down_own), axis=0)

    for _ in range(3):
        out_ring.step()
    for _ in range(4):
        mix_ring.step()
        out_ring.step()
    token = mix_ring.held[0][-1]
    gu_ring.step(token)
    mix_ring.step()
    down_ring.step(token)
    mix_ring.step()
    mix_ring.step()
    w_mix = mix_ring.done()
    wo = out_ring.done()

    def advance(rings, token):
        for ring in rings:
            ring.step(token)

    ffn_rings = (gu_ring, down_ring)
    pack = product(conv_low, w_mix)
    advance(ffn_rings, pack)
    mixed = per_sequence(
        mix_kernel, "mix", count, (PACK,), WIN_G, low, group_lens, pack
    )
    advance(ffn_rings, mixed)

    def partial_sum(make, rings):
        far = make(slice(2 * count, 4 * count)).astype(low)
        over = swap(far[count:], 1)
        near = make(slice(0, 2 * count)).astype(low)
        peer = swap(near[count:], 1)
        across = (far[:count].astype(f32) + over.astype(f32)).astype(low)
        got = swap(across, 2)
        advance(rings, across)
        return near[:count].astype(f32) + peer.astype(f32) + got.astype(f32)

    resid = inputs + partial_sum(lambda part_: product(mixed[part_], wo), ffn_rings)
    normed_f, middle_pull = jax.vjp(rms_norm, resid, g_two)
    normed_own = normed_f.astype(low)
    advance(ffn_rings, normed_own)
    normed = jnp.concatenate(group_gather(normed_own), axis=0)
    advance(ffn_rings, normed)
    w_gu = gu_ring.done()
    gate_up = product(normed, w_gu)
    wd = down_ring.done()
    gate_pre, up_pre = gate_up[:, :hid_p], gate_up[:, hid_p:]
    sigma = jax.nn.sigmoid(gate_pre)
    silu_gate = gate_pre * sigma
    hidden = (silu_gate * up_pre).astype(low)

    grad_down = product_tn(hidden, down_in).astype(low)
    down_sum = SumRing(grad_down.reshape(wide_size, part_p, D), wide_size, table, part)
    down_sum.step()
    grad_hidden = product_nt(down_in, wd).astype(low).astype(f32)
    grad_gu = jnp.concatenate(
        [
            (grad_hidden * up_pre * sigma * (1.0 + gate_pre * (1.0 - sigma))).astype(low),
            (grad_hidden * silu_gate).astype(low),
        ],
        axis=1,
    )
    down_sum.step(grad_gu)
    grad_normed = partial_sum(lambda part_: product_nt(grad_gu[part_], w_gu), (down_sum,))
    grad_w_gu = product_tn(normed, grad_gu).astype(low)
    down_sum.step(grad_w_gu)
    gu_sum = SumRing(grad_w_gu.reshape(GROUP, wide_size, rows, 2 * hid_p), wide_size, table)
    gu_sum.step()
    grad_resid_norm, grad_ffn_gain = middle_pull(grad_normed.astype(low).astype(f32))
    grad_resid = grad_outer + grad_resid_norm
    branch_own = grad_resid.astype(low)
    ffn_sums = (down_sum, gu_sum)
    advance(ffn_sums, branch_own)
    branch_in = jnp.concatenate(group_gather(branch_own), axis=0)
    advance(ffn_sums, branch_in)
    grad_mixed = product_nt(branch_in, wo).astype(low)
    grad_pack = per_sequence(
        mix_back_kernel, "mix_back", count, (PACK, WIN_G), PACK, low, group_lens, pack, grad_mixed
    )
    advance(ffn_sums, grad_pack)
    grad_mix = product_tn(conv_low, grad_pack).astype(low)
    advance(ffn_sums, grad_mix)
    grad_conv_low = partial_sum(lambda part_: product_nt(grad_pack[part_], w_mix), ffn_sums)
    grad_out = product_tn(mixed, branch_in).astype(low)
    advance(ffn_sums, grad_out)
    grad_front, grad_norm_gain, grad_taps = front_pull(grad_conv_low.astype(low).astype(f32))
    grad_tokens = (grad_resid + grad_front).astype(low)
    advance(ffn_sums, grad_tokens)
    grad_w_down = down_sum.done()
    gu_halves = gu_sum.done()

    mix_sum = SumRing(grad_mix.reshape(GROUP, wide_size, rows, PACK), wide_size, table)
    out_sum = SumRing(grad_out.reshape(wide_size, rows, D), wide_size, table, rows)

    down = partial_sum(lambda part_: product(hidden[part_], wd), ())
    block_out = ((resid + down) * is_valid[:, None]).astype(low)

    def to_owner(halves):
        blocks = [halves[0][0], halves[0][1], halves[1][0], halves[1][1]]
        return [blocks[0]] + [swap(blocks[r], r) for r in range(1, GROUP)]

    grad_gate, grad_up = merge_gate_up(table, to_owner(gu_halves), wide_size, part, part_p)
    grad_w_out = out_sum.done()
    mixer_grads = merge_mixer(table, to_owner(mix_sum.done()))
    gains = jnp.concatenate(
        [grad_norm_gain[None], grad_taps, grad_ffn_gain[None], jnp.zeros((3, D), f32)], axis=0
    )
    gains = sum_everywhere(gains, wide_size).reshape(8, GROUP * wide_size, rows)
    gains = lax.dynamic_index_in_dim(gains, spot, 1, keepdims=False)
    return (
        block_out,
        grad_tokens,
        gains[0],
        gains[1 : 1 + CONV_K].T,
        *mixer_grads,
        grad_w_out,
        gains[1 + CONV_K],
        grad_gate,
        grad_up,
        grad_w_down,
    )


def solution(mesh):
    rows = P(("grp", "wide"), None)
    flat = P(("grp", "wide"))
    return jax.shard_map(
        functools.partial(shards, wide_size=mesh.shape["wide"]),
        mesh=mesh,
        in_specs=(rows, flat, rows, flat, rows, rows, rows, rows, rows, rows, rows, flat, rows, rows, rows),
        out_specs=(rows, rows, flat, rows, rows, rows, rows, rows, rows, rows, flat, rows, rows, rows),
        check_vma=False,
    )
```

time: 1060 us -> 845 us (0.80)
  waiting for transfers between devices: 444 us -> 353 us
  between operations: 84 us -> 3.51 us
  Pallas kernels: 21.8 us -> 80.9 us
  local copies, waits for them, and re-layouts: 119 us -> 64.6 us
  other arithmetic: 68 us -> 40.7 us
  starting transfers between devices: 175 us -> 153 us
    ppermute x140 -> x112, waiting for transfers between devices: 379 us -> 305 us  [the longest x56 167 us: step(): held.append(lax.ppermute(value, 'wide', round_ring(CYCLES[self.size], d)))]
    pallas_call x0 -> x40, Pallas kernels: none -> 59.1 us  [the longest x32 33.4 us: pick_add(): pl.pallas_call(body, grid_spec=pltpu.PrefetchScalarGridSpec(num_scalar_pr...]
    unnamed x206 -> x276, local copies, waits for them, and re-layouts: 18.4 us -> 53.4 us
    dynamic_update_slice x76 -> x0, local copies, waits for them, and re-layouts: 25.4 us -> none  [wide_gather(): lax.dynamic_update_slice(whole, jnp.expand_dims(halves[d], at), index)]
    convert_element_type x4 -> x1, local copies, waits for them, and re-layouts: 18.7 us -> 0.08 us  [shards(): group_lens = small_all[:, 5, 0].astype(jnp.int32).reshape(GROUP, wide_size)]
    ppermute x140 -> x112, starting transfers between devices: 138 us -> 120 us  [the longest x56 63.8 us: step(): held.append(lax.ppermute(value, 'wide', round_ring(CYCLES[self.size], d)))]
    convert_element_type x45 -> x10, other arithmetic: 25.8 us -> 10.1 us  [the longest x4 7.07 us: partial_sum(): across = (far[:count].astype(f32) + over.astype(f32)).astype(low)]
    reshape x9 -> x0, local copies, waits for them, and re-layouts: 14.1 us -> none  [the longest x1 6.01 us: shards(): wide_gather(w_down.astype(low).reshape(hid_rows, 1, D), 0, wide_size)]
  transfers between devices with their start and end apart: 192 -> 158, of which waited for: 105 -> 65; matrix products, arithmetic and copies ran while one was open for 24% -> 18% of each run, Pallas kernels for 2% -> 9%
where the time goes in v2:
time: 845 us; the launch traced here: 837 us
  waiting for transfers between devices  353 us (42%)
  starting transfers between devices  153 us (18%)
  matrix products  141 us (17%)
  Pallas kernels  80.9 us (10%)
  local copies, waits for them, and re-layouts  64.6 us (8%)
  other arithmetic  40.7 us (5%)
    ppermute x56, waiting for transfers between devices, step(): held.append(lax.ppermute(value, 'wide', round_ring(CYCLES[self.size], d)))  167 us
    dot_general x16, matrix products, dot(): lax.dot_general(left, right, (((over_left,), (over_right,)), ((), ())), p...  141 us
    ppermute x56, waiting for transfers between devices, step(): lax.ppermute(sums[d], 'wide', round_ring(cycle, d))  138 us
    ppermute x56, starting transfers between devices, step(): held.append(lax.ppermute(value, 'wide', round_ring(CYCLES[self.size], d)))  63.8 us
    ppermute x56, starting transfers between devices, step(): lax.ppermute(sums[d], 'wide', round_ring(cycle, d))  56.5 us
    unnamed x276, local copies, waits for them, and re-layouts  53.4 us
    ppermute x36, waiting for transfers between devices, swap(): return lax.ppermute(value, 'grp', [(i, i ^ over) for i in range(GROUP)])  40.6 us
    pallas_call x32, Pallas kernels, pick_add(): pl.pallas_call(body, grid_spec=pltpu.PrefetchScalarGridSpec(num_scalar_pr...  33.4 us
  transfers between devices with their start and end apart: 158, of which 65 were waited for; matrix products, arithmetic and copies ran while one was open for 18% of the time, Pallas kernels for 9%

profile of v2, /device:TPU:0, one launch (start us, length us, event | category | flops | bytes accessed | tf_op | source)
XLA Modules:
  0.0 837.5 jit_solution(7438558959759442026)
XLA Ops:
  132.2 9.0 %place.4 = bf16[4,8,64,1664]{3,2,1,0:T(8,128)(2,1)S(1)} custom-call(s32[17]{0:T(128)S(1)} %pad_add_fusion.2.table_ref, bf16[2,64,1664]{2,1,0:T(8,128)(2,1)S(1)} %pad_maximum_fusion.6.refs_0_, bf16[2,64,1664]{2,1,0:T(8,128)(2,1)S(1)} %collective-permute-done.9.refs_1_, bf16[2,64,1664]{2,1,0:T(8,128)(2,1)S(1)} %copy-done.26, ...), custom_call_target="tpu_custom_call" | custom-call | bytes 20447232 | tf_op jit(solution)/shard_map/place/pallas_call | solution.py:323
  141.1 12.7 %fusion.44.pack_ref = f32[1024,1664]{1,0:T(8,128)S(1)} fusion(bf16[2048,1664]{1,0:T(8,128)(2,1)S(1)} %bitcast.170, bf16[256,2048]{1,0:T(8,128)(2,1)} %collective-permute-done.7, bf16[256,2048]{1,0:T(8,128)(2,1)} %collective-permute-done.6, bf16[256,2048]{1,0:T(8,128)(2,1)} %collective-permute-done.5, bf16[256,2048]{1,0:T(8,128)(2,1)} %add_convert_fusion.6), kind=kOutput, calls=%fused_computation.146 | convolution fusion | flops 6996099072 | bytes 17825792 | tf_op jit(solution)/shard_map/dot_general | solution.py:29
  153.9 7.4 mix.1
  173.7 8.2 collective-permute-done.53
  186.4 13.4 %collective-permute-done.55.refs_9_ = bf16[2,64,2816]{2,1,0:T(8,128)(2,1)} collective-permute-done((bf16[2,64,2816]{2,1,0:T(8,128)(2,1)S(1)}, bf16[2,64,2816]{2,1,0:T(8,128)(2,1)}, u32[]{:S(2)}, u32[]{:S(2)}) %collective-permute-start.55) | collective-permute-done | bytes 720928 | tf_op jit(solution)/shard_map/ppermute | solution.py:413
  209.4 14.9 %collective-permute-done.56.refs_10_ = bf16[2,64,2816]{2,1,0:T(8,128)(2,1)S(1)} collective-permute-done((bf16[2,64,2816]{2,1,0:T(8,128)(2,1)}, bf16[2,64,2816]{2,1,0:T(8,128)(2,1)S(1)}, u32[]{:S(2)}, u32[]{:S(2)}) %collective-permute-start.56) | collective-permute-done | bytes 720928 | tf_op jit(solution)/shard_map/ppermute | solution.py:413
  228.4 8.7 %collective-permute-done.63.refs_2_ = bf16[176,1024]{1,0:T(8,128)(2,1)S(1)} collective-permute-done((bf16[176,1024]{1,0:T(8,128)(2,1)S(1)}, bf16[176,1024]{1,0:T(8,128)(2,1)S(1)}, u32[]{:S(2)}, u32[]{:S(2)}) %collective-permute-start.63) | collective-permute-done | bytes 360480 | tf_op jit(solution)/shard_map/ppermute | solution.py:413
  237.7 10.6 %collective-permute-done.70.refs_10_ = bf16[176,1024]{1,0:T(8,128)(2,1)S(1)} collective-permute-done((bf16[176,1024]{1,0:T(8,128)(2,1)S(1)}, bf16[176,1024]{1,0:T(8,128)(2,1)S(1)}, u32[]{:S(2)}, u32[]{:S(2)}) %collective-permute-start.70) | collective-permute-done | bytes 360480 | tf_op jit(solution)/shard_map/ppermute | solution.py:413
  261.5 9.8 %collective-permute-done.58.refs_12_ = bf16[2,64,2816]{2,1,0:T(8,128)(2,1)S(1)} collective-permute-done((bf16[2,64,2816]{2,1,0:T(8,128)(2,1)S(1)}, bf16[2,64,2816]{2,1,0:T(8,128)(2,1)S(1)}, u32[]{:S(2)}, u32[]{:S(2)}) %collective-permute-start.58) | collective-permute-done | bytes 720928 | tf_op jit(solution)/shard_map/ppermute | solution.py:413
  282.3 7.1 collective-permute-done.59.refs_13_
  297.5 20.6 %collective-permute-done.73.refs_13_ = bf16[176,1024]{1,0:T(8,128)(2,1)S(1)} collective-permute-done((bf16[176,1024]{1,0:T(8,128)(2,1)S(1)}, bf16[176,1024]{1,0:T(8,128)(2,1)S(1)}, u32[]{:S(2)}, u32[]{:S(2)}) %collective-permute-start.73) | collective-permute-done | bytes 360480 | tf_op jit(solution)/shard_map/ppermute | solution.py:413
  322.3 7.0 collective-permute-done.67.refs_6_
  331.7 15.3 %collective-permute-done.68.refs_7_ = bf16[176,1024]{1,0:T(8,128)(2,1)S(1)} collective-permute-done((bf16[176,1024]{1,0:T(8,128)(2,1)S(1)}, bf16[176,1024]{1,0:T(8,128)(2,1)S(1)}, u32[]{:S(2)}, u32[]{:S(2)}) %collective-permute-start.68) | collective-permute-done | bytes 360480 | tf_op jit(solution)/shard_map/ppermute | solution.py:413
  357.5 18.3 %fusion.43 = f32[1024,2816]{1,0:T(8,128)} fusion(bf16[2048,2816]{1,0:T(8,128)(2,1)S(1)} %bitcast.165, bf16[256,2048]{1,0:T(8,128)(2,1)} %copy-done.119, bf16[256,2048]{1,0:T(8,128)(2,1)} %copy-done.118, bf16[256,2048]{1,0:T(8,128)(2,1)} %collective-permute-done.42, bf16[256,2048]{1,0:T(8,128)(2,1)S(1)} %copy-done.92), kind=kOutput, calls=%fused_computation.145 | convolution fusion | flops 11827937280 | bytes 27262976 | tf_op jit(solution)/shard_map/dot_general | solution.py:29
  375.8 16.6 %fusion.3 = (bf16[1024,1408]{1,0:T(8,128)(2,1)}, bf16[1024,1408]{1,0:T(8,128)(2,1)}, bf16[1024,1408]{1,0:T(8,128)(2,1)}) fusion(f32[1024,2816]{1,0:T(8,128)} %fusion.43, bf16[1024,2048]{1,0:T(8,128)(2,1)} %copy-done.94, bf16[1408,2048]{1,0:T(8,128)(2,1)} %bitcast.173), kind=kOutput, calls=%fused_computation.13 | convolution fusion | flops 5930090496 | bytes 30146560 | tf_op jit(solution)/shard_map/dot_general | solution.py:29
  392.4 10.5 %convolution_convert_fusion.7 = bf16[512,2048]{1,0:T(8,128)(2,1)S(1)} fusion(bf16[2048,2816]{1,0:T(8,128)(2,1)} %bitcast.166, bf16[1024,1408]{1,0:T(8,128)(2,1)} %get-tuple-element.267, bf16[1024,1408]{1,0:T(8,128)(2,1)} %get-tuple-element.266), kind=kOutput, calls=%fused_computation.31 | convolution fusion | flops 5912395776 | bytes 19398656 | tf_op jit(solution)/shard_map/dot_general | solution.py:29
  403.1 7.7 convolution_convert_fusion.8
  413.3 8.3 convolution_convert_fusion.1
  424.2 8.5 %collective-permute-done.144.refs_2_ = bf16[176,1024]{1,0:T(8,128)(2,1)S(1)} collective-permute-done((bf16[176,1024]{1,0:T(8,128)(2,1)S(1)}, bf16[176,1024]{1,0:T(8,128)(2,1)S(1)}, u32[]{:S(2)}, u32[]{:S(2)}) %collective-permute-start.144) | collective-permute-done | bytes 360480 | tf_op jit(solution)/shard_map/ppermute | solution.py:451
  436.7 7.7 collective-permute-done.146.refs_2_
  452.4 18.7 %convolution_convert_fusion = bf16[2048,2816]{1,0:T(8,128)(2,1)} fusion(bf16[1024,1408]{1,0:T(8,128)(2,1)} %get-tuple-element.266, bf16[1024,1408]{1,0:T(8,128)(2,1)} %get-tuple-element.267, bf16[256,2048]{1,0:T(8,128)(2,1)} %copy-done.119, bf16[256,2048]{1,0:T(8,128)(2,1)} %copy-done.118, bf16[256,2048]{1,0:T(8,128)(2,1)} %collective-permute-done.42, ...), kind=kOutput, calls=%fused_computation | convolution fusion | flops 11845238784 | bytes 21495808 | tf_op jit(solution)/shard_map/dot_general | solution.py:29
  478.8 25.3 %collective-permute-done.149.refs_3_ = bf16[176,1024]{1,0:T(8,128)(2,1)S(1)} collective-permute-done((bf16[176,1024]{1,0:T(8,128)(2,1)S(1)}, bf16[176,1024]{1,0:T(8,128)(2,1)S(1)}, u32[]{:S(2)}, u32[]{:S(2)}) %collective-permute-start.149) | collective-permute-done | bytes 360480 | tf_op jit(solution)/shard_map/ppermute | solution.py:451
  529.1 14.4 %mix_back.1 = bf16[1024,1664]{1,0:T(8,128)(2,1)S(1)} custom-call(s32[4]{0:T(128)S(1)} %copy-done.64, f32[1024,1664]{1,0:T(8,128)S(1)} %bitcast.164, bf16[1024,512]{1,0:T(8,128)(2,1)S(1)} %convolution_convert_fusion.13.grad_ref), custom_call_target="tpu_custom_call" | custom-call | flops 2000000000 | bytes 10000000 | tf_op jit(solution)/shard_map/mix_back/pallas_call | solution.py:125
  546.2 7.1 convolution_convert_fusion.5
  557.2 9.6 %convolution_convert_fusion.2 = bf16[2048,1664]{1,0:T(8,128)(2,1)S(1)} fusion(bf16[1024,1664]{1,0:T(8,128)(2,1)S(1)} %mix_back.1, bf16[256,2048]{1,0:T(8,128)(2,1)} %collective-permute-done.7, bf16[256,2048]{1,0:T(8,128)(2,1)} %collective-permute-done.6, bf16[256,2048]{1,0:T(8,128)(2,1)} %collective-permute-done.5, bf16[256,2048]{1,0:T(8,128)(2,1)} %add_convert_fusion.6), kind=kOutput, calls=%fused_computation.2 | convolution fusion | flops 6999506944 | bytes 14417920 | tf_op jit(solution)/shard_map/dot_general | solution.py:29
  569.8 8.8 %convolution_convert_fusion.6 = bf16[512,2048]{1,0:T(8,128)(2,1)} fusion(bf16[2048,1664]{1,0:T(8,128)(2,1)} %bitcast.172, bf16[1024,1664]{1,0:T(8,128)(2,1)} %copy-done.11), kind=kOutput, calls=%fused_computation.30 | convolution fusion | flops 3490709504 | bytes 10616832 | tf_op jit(solution)/shard_map/dot_general | solution.py:29
  600.4 16.2 %collective-permute-done.98.refs_2_ = bf16[2,64,1664]{2,1,0:T(8,128)(2,1)S(1)} collective-permute-done((bf16[2,64,1664]{2,1,0:T(8,128)(2,1)S(1)}, bf16[2,64,1664]{2,1,0:T(8,128)(2,1)S(1)}, u32[]{:S(2)}, u32[]{:S(2)}) %collective-permute-start.98) | collective-permute-done | bytes 426016 | tf_op jit(solution)/shard_map/ppermute | solution.py:451
  681.7 7.0 collective-permute-done.134.refs_3_
  706.4 6.6 collective-permute-done.104.refs_2_
  718.1 14.6 %collective-permute-done.105.refs_3_ = bf16[2,64,1664]{2,1,0:T(8,128)(2,1)S(1)} collective-permute-done((bf16[2,64,1664]{2,1,0:T(8,128)(2,1)S(1)}, bf16[2,64,1664]{2,1,0:T(8,128)(2,1)S(1)}, u32[]{:S(2)}, u32[]{:S(2)}) %collective-permute-start.105) | collective-permute-done | bytes 426016 | tf_op jit(solution)/shard_map/ppermute | solution.py:451
  760.9 10.9 %collective-permute-done.107.refs_3_ = bf16[2,64,1664]{2,1,0:T(8,128)(2,1)} collective-permute-done((bf16[2,64,1664]{2,1,0:T(8,128)(2,1)}, bf16[2,64,1664]{2,1,0:T(8,128)(2,1)}, u32[]{:S(2)}, u32[]{:S(2)}) %collective-permute-start.107) | collective-permute-done | bytes 426016 | tf_op jit(solution)/shard_map/ppermute | solution.py:451
  808.4 18.8 %collective-permute-done.111.c = bf16[64,1664]{1,0:T(8,128)(2,1)S(1)} collective-permute-done((bf16[64,1664]{1,0:T(8,128)(2,1)S(1)}, bf16[64,1664]{1,0:T(8,128)(2,1)S(1)}, u32[]{:S(2)}, u32[]{:S(2)}) %collective-permute-start.111) | collective-permute-done | bytes 213024 | tf_op jit(solution)/shard_map/ppermute | solution.py:144
  (703 shorter events, 453.7 us)
Async XLA Ops:
  54.9 48.6 %collective-permute-start.6 = (bf16[256,2048]{1,0:T(8,128)(2,1)}, bf16[256,2048]{1,0:T(8,128)(2,1)}, u32[]{:S(2)}, u32[]{:S(2)}) collective-permute-start(bf16[256,2048]{1,0:T(8,128)(2,1)} %add_convert_fusion.6), channel_id=1, source_target_pairs={{0,16},{8,24},{16,0},{24,8},{1,17},{9,25},{17,1},{25,9},{2,18},{10... | collective-permute-start | bytes 3145736 | tf_op jit(solution)/shard_map/ppermute | solution.py:144
  103.5 37.7 %collective-permute-start.5 = (bf16[256,2048]{1,0:T(8,128)(2,1)}, bf16[256,2048]{1,0:T(8,128)(2,1)}, u32[]{:S(2)}, u32[]{:S(2)}) collective-permute-start(bf16[256,2048]{1,0:T(8,128)(2,1)} %add_convert_fusion.6), channel_id=1, source_target_pairs={{0,8},{8,0},{16,24},{24,16},{1,9},{9,1},{17,25},{25,17},{2,10},{10... | collective-permute-start | bytes 3145736 | tf_op jit(solution)/shard_map/ppermute | solution.py:144
  103.5 37.7 %collective-permute-start.7 = (bf16[256,2048]{1,0:T(8,128)(2,1)}, bf16[256,2048]{1,0:T(8,128)(2,1)}, u32[]{:S(2)}, u32[]{:S(2)}) collective-permute-start(bf16[256,2048]{1,0:T(8,128)(2,1)} %collective-permute-done.6), channel_id=1, source_target_pairs={{0,8},{8,0},{16,24},{24,16},{1,9},{9,1},{17,25},{25,17},{2,10},{10... | collective-permute-start | bytes 3145736 | tf_op jit(solution)/shard_map/ppermute | solution.py:144
  121.9 43.1 %collective-permute-start.45 = (bf16[64,2816]{1,0:T(8,128)(2,1)S(1)}, bf16[64,2816]{1,0:T(8,128)(2,1)S(1)}, u32[]{:S(2)}, u32[]{:S(2)}) collective-permute-start(bf16[64,2816]{1,0:T(8,128)(2,1)S(1)} %get-tuple-element.273), channel_id=1, source_target_pairs={{0,8},{8,0},{16,24},{24,16},{1,9},{9,1},{17,25},{25,17},{2,10},{10... | collective-permute-start | bytes 1081352 | tf_op jit(solution)/shard_map/ppermute | solution.py:144
  168.9 35.4 %collective-permute-start.39 = (bf16[256,2048]{1,0:T(8,128)(2,1)}, bf16[256,2048]{1,0:T(8,128)(2,1)}, u32[]{:S(2)}, u32[]{:S(2)}) collective-permute-start(bf16[256,2048]{1,0:T(8,128)(2,1)} %slice.249), channel_id=1, source_target_pairs={{0,8},{8,0},{16,24},{24,16},{1,9},{9,1},{17,25},{25,17},{2,10},{10... | collective-permute-start | bytes 3145736 | tf_op jit(solution)/shard_map/ppermute | solution.py:144
  170.2 34.4 %collective-permute-start.41 = (bf16[256,2048]{1,0:T(8,128)(2,1)}, bf16[256,2048]{1,0:T(8,128)(2,1)}, u32[]{:S(2)}, u32[]{:S(2)}) collective-permute-start(bf16[256,2048]{1,0:T(8,128)(2,1)} %add_convert_fusion.5), channel_id=1, source_target_pairs={{0,16},{8,24},{16,0},{24,8},{1,17},{9,25},{17,1},{25,9},{2,18},{10... | collective-permute-start | bytes 3145736 | tf_op jit(solution)/shard_map/ppermute | solution.py:144
  185.0 40.7 %collective-permute-start.62 = (bf16[176,1024]{1,0:T(8,128)(2,1)S(1)}, bf16[176,1024]{1,0:T(8,128)(2,1)S(1)}, u32[]{:S(2)}, u32[]{:S(2)}) collective-permute-start(bf16[176,1024]{1,0:T(8,128)(2,1)S(1)} %get-tuple-element.144.refs_0_), channel_id=1, source_target_pairs={{0,2},{2,4},{4,6},{6,7},{7,5},{5,3},{3,1},{1,0},{8,10},{10,12},{12... | collective-permute-start | bytes 1081352 | tf_op jit(solution)/shard_map/ppermute | solution.py:413
  207.8 53.4 %collective-permute-start.43 = (bf16[256,2048]{1,0:T(8,128)(2,1)S(1)}, bf16[256,2048]{1,0:T(8,128)(2,1)S(1)}, u32[]{:S(2)}, u32[]{:S(2)}) collective-permute-start(bf16[256,2048]{1,0:T(8,128)(2,1)S(1)} %multiply_convert_fusion.2), channel_id=1, source_target_pairs={{0,16},{8,24},{16,0},{24,8},{1,17},{9,25},{17,1},{25,9},{2,18},{10... | collective-permute-start | bytes 3145736 | tf_op jit(solution)/shard_map/ppermute | solution.py:144
  227.7 30.4 %collective-permute-start.49 = (bf16[2,64,2816]{2,1,0:T(8,128)(2,1)S(1)}, bf16[2,64,2816]{2,1,0:T(8,128)(2,1)S(1)}, u32[]{:S(2)}, u32[]{:S(2)}) collective-permute-start(bf16[2,64,2816]{2,1,0:T(8,128)(2,1)S(1)} %collective-permute-done.48.refs_3_), channel_id=1, source_target_pairs={{0,2},{2,4},{4,6},{6,7},{7,5},{5,3},{3,1},{1,0},{8,10},{10,12},{12... | collective-permute-start | bytes 2162696 | tf_op jit(solution)/shard_map/ppermute | solution.py:413
  280.3 39.1 %collective-permute-start.79 = (bf16[256,2048]{1,0:T(8,128)(2,1)S(1)}, bf16[256,2048]{1,0:T(8,128)(2,1)S(1)}, u32[]{:S(2)}, u32[]{:S(2)}) collective-permute-start(bf16[256,2048]{1,0:T(8,128)(2,1)S(1)} %fusion.21), channel_id=1, source_target_pairs={{0,8},{8,0},{16,24},{24,16},{1,9},{9,1},{17,25},{25,17},{2,10},{10... | collective-permute-start | bytes 3145736 | tf_op jit(solution)/shard_map/ppermute | solution.py:144
  289.4 30.7 %collective-permute-start.51 = (bf16[2,64,2816]{2,1,0:T(8,128)(2,1)S(1)}, bf16[2,64,2816]{2,1,0:T(8,128)(2,1)S(1)}, u32[]{:S(2)}, u32[]{:S(2)}) collective-permute-start(bf16[2,64,2816]{2,1,0:T(8,128)(2,1)S(1)} %collective-permute-done.50.refs_5_), channel_id=1, source_target_pairs={{0,2},{2,4},{4,6},{6,7},{7,5},{5,3},{3,1},{1,0},{8,10},{10,12},{12... | collective-permute-start | bytes 2162696 | tf_op jit(solution)/shard_map/ppermute | solution.py:413
  297.4 34.1 %collective-permute-start.81 = (bf16[256,2048]{1,0:T(8,128)(2,1)S(1)}, bf16[256,2048]{1,0:T(8,128)(2,1)S(1)}, u32[]{:S(2)}, u32[]{:S(2)}) collective-permute-start(bf16[256,2048]{1,0:T(8,128)(2,1)S(1)} %collective-permute-done.80), channel_id=1, source_target_pairs={{0,8},{8,0},{16,24},{24,16},{1,9},{9,1},{17,25},{25,17},{2,10},{10... | collective-permute-start | bytes 3145736 | tf_op jit(solution)/shard_map/ppermute | solution.py:144
  320.1 31.8 %collective-permute-start.52 = (bf16[2,64,2816]{2,1,0:T(8,128)(2,1)S(1)}, bf16[2,64,2816]{2,1,0:T(8,128)(2,1)S(1)}, u32[]{:S(2)}, u32[]{:S(2)}) collective-permute-start(bf16[2,64,2816]{2,1,0:T(8,128)(2,1)S(1)} %collective-permute-done.51.refs_6_), channel_id=1, source_target_pairs={{0,2},{2,4},{4,6},{6,7},{7,5},{5,3},{3,1},{1,0},{8,10},{10,12},{12... | collective-permute-start | bytes 2162696 | tf_op jit(solution)/shard_map/ppermute | solution.py:413
  321.6 30.3 %collective-permute-start.61 = (bf16[2,64,2816]{2,1,0:T(8,128)(2,1)S(1)}, bf16[2,64,2816]{2,1,0:T(8,128)(2,1)S(1)}, u32[]{:S(2)}, u32[]{:S(2)}) collective-permute-start(bf16[2,64,2816]{2,1,0:T(8,128)(2,1)S(1)} %collective-permute-done.60.refs_14_), channel_id=1, source_target_pairs={{2,0},{4,2},{6,4},{7,6},{5,7},{3,5},{1,3},{0,1},{10,8},{12,10},{14... | collective-permute-start | bytes 2162696 | tf_op jit(solution)/shard_map/ppermute | solution.py:413
  411.0 37.4 %collective-permute-start.82 = (bf16[256,2048]{1,0:T(8,128)(2,1)S(1)}, bf16[256,2048]{1,0:T(8,128)(2,1)S(1)}, u32[]{:S(2)}, u32[]{:S(2)}) collective-permute-start(bf16[256,2048]{1,0:T(8,128)(2,1)S(1)} %slice.265), channel_id=1, source_target_pairs={{0,8},{8,0},{16,24},{24,16},{1,9},{9,1},{17,25},{25,17},{2,10},{10... | collective-permute-start | bytes 3145736 | tf_op jit(solution)/shard_map/ppermute | solution.py:144
  411.9 36.5 %collective-permute-start.84 = (bf16[256,2048]{1,0:T(8,128)(2,1)S(1)}, bf16[256,2048]{1,0:T(8,128)(2,1)S(1)}, u32[]{:S(2)}, u32[]{:S(2)}) collective-permute-start(bf16[256,2048]{1,0:T(8,128)(2,1)S(1)} %add_convert_fusion.3), channel_id=1, source_target_pairs={{0,16},{8,24},{16,0},{24,8},{1,17},{9,25},{17,1},{25,9},{2,18},{10... | collective-permute-start | bytes 3145736 | tf_op jit(solution)/shard_map/ppermute | solution.py:144
  446.9 31.7 %collective-permute-start.148 = (bf16[176,1024]{1,0:T(8,128)(2,1)}, bf16[176,1024]{1,0:T(8,128)(2,1)S(1)}, u32[]{:S(2)}, u32[]{:S(2)}) collective-permute-start(bf16[176,1024]{1,0:T(8,128)(2,1)} %get-tuple-element.230), channel_id=1, source_target_pairs={{0,2},{2,4},{4,6},{6,7},{7,5},{5,3},{3,1},{1,0},{8,10},{10,12},{12... | collective-permute-start | bytes 1081352 | tf_op jit(solution)/shard_map/ppermute | solution.py:451
  476.0 30.6 %collective-permute-start.127 = (bf16[2,64,2816]{2,1,0:T(8,128)(2,1)S(1)}, bf16[2,64,2816]{2,1,0:T(8,128)(2,1)S(1)}, u32[]{:S(2)}, u32[]{:S(2)}) collective-permute-start(bf16[2,64,2816]{2,1,0:T(8,128)(2,1)S(1)} %get-tuple-element.192), channel_id=1, source_target_pairs={{0,2},{2,4},{4,6},{6,7},{7,5},{5,3},{3,1},{1,0},{8,10},{10,12},{12... | collective-permute-start | bytes 2162696 | tf_op jit(solution)/shard_map/ppermute | solution.py:451
  477.8 40.2 %collective-permute-start.85 = (bf16[256,2048]{1,0:T(8,128)(2,1)}, bf16[256,2048]{1,0:T(8,128)(2,1)S(1)}, u32[]{:S(2)}, u32[]{:S(2)}) collective-permute-start(bf16[256,2048]{1,0:T(8,128)(2,1)} %fusion.42), channel_id=1, source_target_pairs={{0,8},{8,0},{16,24},{24,16},{1,9},{9,1},{17,25},{25,17},{2,10},{10... | collective-permute-start | bytes 3145736 | tf_op jit(solution)/shard_map/ppermute | solution.py:144
  477.8 40.2 %collective-permute-start.87 = (bf16[256,2048]{1,0:T(8,128)(2,1)}, bf16[256,2048]{1,0:T(8,128)(2,1)S(1)}, u32[]{:S(2)}, u32[]{:S(2)}) collective-permute-start(bf16[256,2048]{1,0:T(8,128)(2,1)} %collective-permute-done.86), channel_id=1, source_target_pairs={{0,8},{8,0},{16,24},{24,16},{1,9},{9,1},{17,25},{25,17},{2,10},{10... | collective-permute-start | bytes 3145736 | tf_op jit(solution)/shard_map/ppermute | solution.py:144
  508.7 70.5 %collective-permute-start.129 = (bf16[2,64,2816]{2,1,0:T(8,128)(2,1)}, bf16[2,64,2816]{2,1,0:T(8,128)(2,1)S(1)}, u32[]{:S(2)}, u32[]{:S(2)}) collective-permute-start(bf16[2,64,2816]{2,1,0:T(8,128)(2,1)} %get-tuple-element.196), channel_id=1, source_target_pairs={{0,2},{2,4},{4,6},{6,7},{7,5},{5,3},{3,1},{1,0},{8,10},{10,12},{12... | collective-permute-start | bytes 2162696 | tf_op jit(solution)/shard_map/ppermute | solution.py:451
  516.2 65.0 %collective-permute-start.130 = (bf16[2,64,2816]{2,1,0:T(8,128)(2,1)}, bf16[2,64,2816]{2,1,0:T(8,128)(2,1)}, u32[]{:S(2)}, u32[]{:S(2)}) collective-permute-start(bf16[2,64,2816]{2,1,0:T(8,128)(2,1)} %get-tuple-element.197), channel_id=1, source_target_pairs={{2,0},{4,2},{6,4},{7,6},{5,7},{3,5},{1,3},{0,1},{10,8},{12,10},{14... | collective-permute-start | bytes 2162696 | tf_op jit(solution)/shard_map/ppermute | solution.py:451
  554.5 41.0 %collective-permute-start.89 = (bf16[256,2048]{1,0:T(8,128)(2,1)}, bf16[256,2048]{1,0:T(8,128)(2,1)}, u32[]{:S(2)}, u32[]{:S(2)}) collective-permute-start(bf16[256,2048]{1,0:T(8,128)(2,1)} %slice.275), channel_id=1, source_target_pairs={{0,8},{8,0},{16,24},{24,16},{1,9},{9,1},{17,25},{25,17},{2,10},{10... | collective-permute-start | bytes 3145736 | tf_op jit(solution)/shard_map/ppermute | solution.py:144
  586.3 66.0 %collective-permute-start.88 = (bf16[256,2048]{1,0:T(8,128)(2,1)}, bf16[256,2048]{1,0:T(8,128)(2,1)}, u32[]{:S(2)}, u32[]{:S(2)}) collective-permute-start(bf16[256,2048]{1,0:T(8,128)(2,1)} %slice.272), channel_id=1, source_target_pairs={{0,8},{8,0},{16,24},{24,16},{1,9},{9,1},{17,25},{25,17},{2,10},{10... | collective-permute-start | bytes 3145736 | tf_op jit(solution)/shard_map/ppermute | solution.py:144
  590.9 35.3 %collective-permute-start.131 = (bf16[2,64,2816]{2,1,0:T(8,128)(2,1)S(1)}, bf16[2,64,2816]{2,1,0:T(8,128)(2,1)S(1)}, u32[]{:S(2)}, u32[]{:S(2)}) collective-permute-start(bf16[2,64,2816]{2,1,0:T(8,128)(2,1)S(1)} %get-tuple-element.200), channel_id=1, source_target_pairs={{0,2},{2,4},{4,6},{6,7},{7,5},{5,3},{3,1},{1,0},{8,10},{10,12},{12... | collective-permute-start | bytes 2162696 | tf_op jit(solution)/shard_map/ppermute | solution.py:451
  599.1 53.6 %collective-permute-start.90 = (bf16[256,2048]{1,0:T(8,128)(2,1)}, bf16[256,2048]{1,0:T(8,128)(2,1)}, u32[]{:S(2)}, u32[]{:S(2)}) collective-permute-start(bf16[256,2048]{1,0:T(8,128)(2,1)} %add_convert_fusion.1), channel_id=1, source_target_pairs={{0,16},{8,24},{16,0},{24,8},{1,17},{9,25},{17,1},{25,9},{2,18},{10... | collective-permute-start | bytes 3145736 | tf_op jit(solution)/shard_map/ppermute | solution.py:144
  669.7 31.3 %collective-permute-start.77 = (bf16[256,2048]{1,0:T(8,128)(2,1)}, bf16[256,2048]{1,0:T(8,128)(2,1)}, u32[]{:S(2)}, u32[]{:S(2)}) collective-permute-start(bf16[256,2048]{1,0:T(8,128)(2,1)} %slice.261), channel_id=1, source_target_pairs={{0,8},{8,0},{16,24},{24,16},{1,9},{9,1},{17,25},{25,17},{2,10},{10... | collective-permute-start | bytes 3145736 | tf_op jit(solution)/shard_map/ppermute | solution.py:144
  700.9 80.9 %collective-permute-start.76 = (bf16[256,2048]{1,0:T(8,128)(2,1)}, bf16[256,2048]{1,0:T(8,128)(2,1)}, u32[]{:S(2)}, u32[]{:S(2)}) collective-permute-start(bf16[256,2048]{1,0:T(8,128)(2,1)} %slice.258), channel_id=1, source_target_pairs={{0,8},{8,0},{16,24},{24,16},{1,9},{9,1},{17,25},{25,17},{2,10},{10... | collective-permute-start | bytes 3145736 | tf_op jit(solution)/shard_map/ppermute | solution.py:144
  701.8 32.6 %collective-permute-start.135 = (bf16[2,64,2816]{2,1,0:T(8,128)(2,1)S(1)}, bf16[2,64,2816]{2,1,0:T(8,128)(2,1)S(1)}, u32[]{:S(2)}, u32[]{:S(2)}) collective-permute-start(bf16[2,64,2816]{2,1,0:T(8,128)(2,1)S(1)} %get-tuple-element.208), channel_id=1, source_target_pairs={{0,2},{2,4},{4,6},{6,7},{7,5},{5,3},{3,1},{1,0},{8,10},{10,12},{12... | collective-permute-start | bytes 2162696 | tf_op jit(solution)/shard_map/ppermute | solution.py:451
  705.9 31.8 %collective-permute-start.136 = (bf16[2,64,2816]{2,1,0:T(8,128)(2,1)S(1)}, bf16[2,64,2816]{2,1,0:T(8,128)(2,1)S(1)}, u32[]{:S(2)}, u32[]{:S(2)}) collective-permute-start(bf16[2,64,2816]{2,1,0:T(8,128)(2,1)S(1)} %get-tuple-element.209), channel_id=1, source_target_pairs={{2,0},{4,2},{6,4},{7,6},{5,7},{3,5},{1,3},{0,1},{10,8},{12,10},{14... | collective-permute-start | bytes 2162696 | tf_op jit(solution)/shard_map/ppermute | solution.py:451
  717.4 65.2 %collective-permute-start.78 = (bf16[256,2048]{1,0:T(8,128)(2,1)}, bf16[256,2048]{1,0:T(8,128)(2,1)}, u32[]{:S(2)}, u32[]{:S(2)}) collective-permute-start(bf16[256,2048]{1,0:T(8,128)(2,1)} %add_convert_fusion.4), channel_id=1, source_target_pairs={{0,16},{8,24},{16,0},{24,8},{1,17},{9,25},{17,1},{25,9},{2,18},{10... | collective-permute-start | bytes 3145736 | tf_op jit(solution)/shard_map/ppermute | solution.py:144
  743.2 32.6 %collective-permute-start.137 = (bf16[2,64,2816]{2,1,0:T(8,128)(2,1)}, bf16[2,64,2816]{2,1,0:T(8,128)(2,1)S(1)}, u32[]{:S(2)}, u32[]{:S(2)}) collective-permute-start(bf16[2,64,2816]{2,1,0:T(8,128)(2,1)} %get-tuple-element.212), channel_id=1, source_target_pairs={{0,2},{2,4},{4,6},{6,7},{7,5},{5,3},{3,1},{1,0},{8,10},{10,12},{12... | collective-permute-start | bytes 2162696 | tf_op jit(solution)/shard_map/ppermute | solution.py:451
  (262 other events, 4149.5 us)

commit v3 on v2

--- a/solution.py
+++ b/solution.py
@@ -144,10 +144,14 @@
     return lax.ppermute(value, "grp", [(i, i ^ over) for i in range(GROUP)])
 
 
-def group_gather(own):
-    peer = swap(own, 1)
+def group_gather(own, between=lambda: None):
     across = swap(own, 2)
-    return own, peer, across, swap(across, 1)
+    token = between()
+    if token is not None:
+        across = after(token, across)[0]
+    count = own.shape[0]
+    got = swap(jnp.concatenate([own, across]), 1)
+    return jnp.concatenate([own, got[:count], across, got[count:]])
 
 
 def reorder(stack):
@@ -412,6 +416,9 @@
             value = held[-1] if token is None else after(token, held[-1])[0]
             held.append(lax.ppermute(value, "wide", round_ring(CYCLES[self.size], d)))
 
+    def seen(self):
+        return self.held[0][max(len(self.held[0]) - 2, 0)]
+
     def done(self, token=None):
         while self.steps:
             self.step()
@@ -433,7 +440,7 @@
 class SumRing:
     def __init__(self, terms, size, table, keep_rows=None):
         self.terms, self.size, self.table, self.keep_rows = terms, size, table, keep_rows
-        self.at, self.got = 0, None
+        self.at, self.got, self.last = 0, None, terms
         self.left = size - 1 if size in CYCLES else 0
 
     def step(self, token=None):
@@ -446,17 +453,17 @@
             if got is None:
                 self.terms = after(token, self.terms)[0]
         sums = pick_add(self.table, self.terms, got, self.at, self.size)
+        self.last = sums[0]
         self.at += 1
         cycle = CYCLES[self.size]
         self.got = [lax.ppermute(sums[d], "wide", round_ring(cycle, d)) for d in (0, 1)]
 
-    def done(self):
+    def done(self, token=None):
         while self.left:
             self.step()
         if self.size in CYCLES:
-            out = pick_add(
-                self.table, self.terms, self.got, self.at, self.size, self.keep_rows
-            )
+            got = self.got if token is None else after(token, *self.got)
+            out = pick_add(self.table, self.terms, got, self.at, self.size, self.keep_rows)
             return out if self.keep_rows is None else out[0]
         if self.keep_rows is None:
             full = lax.psum_scatter(
@@ -553,64 +560,79 @@
 
     inputs = tokens.astype(f32)
     conv_out, front_pull = jax.vjp(front_part, inputs, g_one, taps)
-    conv_low = jnp.concatenate(group_gather(conv_out.astype(low)), axis=0)
+    conv_low = group_gather(conv_out.astype(low))
     grad_outer = cotangent.astype(f32) * is_valid[:, None]
     down_own = after(conv_low, grad_outer.astype(low))[0]
-    down_in = jnp.concatenate(group_gather(down_own), axis=0)
+    down_in = group_gather(down_own)
 
     for _ in range(3):
         out_ring.step()
-    for _ in range(4):
+    for k in range(7):
         mix_ring.step()
         out_ring.step()
-    token = mix_ring.held[0][-1]
-    gu_ring.step(token)
-    mix_ring.step()
-    down_ring.step(token)
-    mix_ring.step()
-    mix_ring.step()
+        if k == 4:
+            gu_ring.step(mix_ring.seen())
+    gu_ring.step(mix_ring.held[0][-1])
     w_mix = mix_ring.done()
     wo = out_ring.done()
 
-    def advance(rings, token):
+    def advance(token, *rings):
         for ring in rings:
             ring.step(token)
 
-    ffn_rings = (gu_ring, down_ring)
     pack = product(conv_low, w_mix)
-    advance(ffn_rings, pack)
+    advance(pack, gu_ring)
     mixed = per_sequence(
         mix_kernel, "mix", count, (PACK,), WIN_G, low, group_lens, pack
     )
-    advance(ffn_rings, mixed)
-
-    def partial_sum(make, rings):
-        far = make(slice(2 * count, 4 * count)).astype(low)
+    advance(mixed, gu_ring)
+
+    def partial_sum(make, between=lambda across: ()):
+        far = make(1).astype(low)
         over = swap(far[count:], 1)
-        near = make(slice(0, 2 * count)).astype(low)
+        near = make(0).astype(low)
         peer = swap(near[count:], 1)
         across = (far[:count].astype(f32) + over.astype(f32)).astype(low)
         got = swap(across, 2)
-        advance(rings, across)
+        for token in between(across):
+            got = after(token, got)[0]
         return near[:count].astype(f32) + peer.astype(f32) + got.astype(f32)
 
-    resid = inputs + partial_sum(lambda part_: product(mixed[part_], wo), ffn_rings)
+    def rows_of(value, x):
+        return value[2 * x * count : 2 * (x + 1) * count]
+
+    def in_forward(across):
+        advance(across, gu_ring)
+        advance(gu_ring.seen(), gu_ring)
+        return [gu_ring.seen()]
+
+    resid = inputs + partial_sum(lambda x: product(rows_of(mixed, x), wo), in_forward)
     normed_f, middle_pull = jax.vjp(rms_norm, resid, g_two)
     normed_own = normed_f.astype(low)
-    advance(ffn_rings, normed_own)
-    normed = jnp.concatenate(group_gather(normed_own), axis=0)
-    advance(ffn_rings, normed)
-    w_gu = gu_ring.done()
-    gate_up = product(normed, w_gu)
-    wd = down_ring.done()
+    advance(normed_own, gu_ring)
+
+    def in_gather():
+        down_ring.step(gu_ring.seen())
+        down_ring.step()
+        return down_ring.seen()
+
+    normed = group_gather(normed_own, in_gather)
+    w_gu = gu_ring.done(down_ring.seen())
+    down_ring.step(w_gu)
+    gate_up = product(*after(down_ring.seen(), normed, w_gu))
+    advance(gate_up, down_ring)
     gate_pre, up_pre = gate_up[:, :hid_p], gate_up[:, hid_p:]
     sigma = jax.nn.sigmoid(gate_pre)
     silu_gate = gate_pre * sigma
-    hidden = (silu_gate * up_pre).astype(low)
-
-    grad_down = product_tn(hidden, down_in).astype(low)
+    hidden = bar((silu_gate * up_pre).astype(low))
+    advance(hidden, down_ring)
+
+    grad_down = product_tn(*after(down_ring.seen(), hidden, down_in)).astype(low)
+    advance(grad_down, down_ring)
     down_sum = SumRing(grad_down.reshape(wide_size, part_p, D), wide_size, table, part)
     down_sum.step()
+    down_ring.step(down_sum.last)
+    wd = down_ring.done()
     grad_hidden = product_nt(down_in, wd).astype(low).astype(f32)
     grad_gu = jnp.concatenate(
         [
@@ -619,46 +641,79 @@
         ],
         axis=1,
     )
+    grad_gu = bar(grad_gu)
     down_sum.step(grad_gu)
-    grad_normed = partial_sum(lambda part_: product_nt(grad_gu[part_], w_gu), (down_sum,))
-    grad_w_gu = product_tn(normed, grad_gu).astype(low)
-    down_sum.step(grad_w_gu)
-    gu_sum = SumRing(grad_w_gu.reshape(GROUP, wide_size, rows, 2 * hid_p), wide_size, table)
-    gu_sum.step()
+    sums = []
+
+    def in_backward(across):
+        down_sum.step(across)
+        grad_w_gu = product_tn(*after((across, down_sum.last), normed, grad_gu)).astype(low)
+        gu_sum = SumRing(grad_w_gu.reshape(GROUP, wide_size, rows, 2 * hid_p), wide_size, table)
+        gu_sum.step()
+        down_sum.step(gu_sum.last)
+        gu_sum.step(down_sum.last)
+        sums.append(gu_sum)
+        return [gu_sum.last]
+
+    grad_normed = partial_sum(lambda x: product_nt(rows_of(grad_gu, x), w_gu), in_backward)
+    gu_sum = sums[0]
     grad_resid_norm, grad_ffn_gain = middle_pull(grad_normed.astype(low).astype(f32))
     grad_resid = grad_outer + grad_resid_norm
     branch_own = grad_resid.astype(low)
-    ffn_sums = (down_sum, gu_sum)
-    advance(ffn_sums, branch_own)
-    branch_in = jnp.concatenate(group_gather(branch_own), axis=0)
-    advance(ffn_sums, branch_in)
+    advance(branch_own, down_sum)
+
+    def in_branch():
+        gu_sum.step(down_sum.last)
+        return gu_sum.last
+
+    branch_in = group_gather(branch_own, in_branch)
+    down_sum.step(branch_in)
     grad_mixed = product_nt(branch_in, wo).astype(low)
+    advance(grad_mixed, gu_sum)
+    grad_mixed = after(gu_sum.last, grad_mixed)[0]
     grad_pack = per_sequence(
         mix_back_kernel, "mix_back", count, (PACK, WIN_G), PACK, low, group_lens, pack, grad_mixed
     )
-    advance(ffn_sums, grad_pack)
-    grad_mix = product_tn(conv_low, grad_pack).astype(low)
-    advance(ffn_sums, grad_mix)
-    grad_conv_low = partial_sum(lambda part_: product_nt(grad_pack[part_], w_mix), ffn_sums)
-    grad_out = product_tn(mixed, branch_in).astype(low)
-    advance(ffn_sums, grad_out)
+    advance(grad_pack, gu_sum)
+    grad_w_down = down_sum.done(grad_pack)
+    grad_mix = product_tn(*after(gu_sum.last, conv_low, grad_pack)).astype(low)
+    mix_sum = SumRing(grad_mix.reshape(GROUP, wide_size, rows, PACK), wide_size, table)
+    mix_sum.step()
+    advance(mix_sum.last, gu_sum)
+    grad_pack = after(gu_sum.last, grad_pack)[0]
+
+    def in_front(across):
+        advance(across, mix_sum, gu_sum)
+        grad_out = product_tn(*after(gu_sum.last, mixed, branch_in)).astype(low)
+        advance(grad_out, mix_sum)
+        sums.append(grad_out)
+        return [mix_sum.last]
+
+    grad_conv_low = partial_sum(lambda x: product_nt(rows_of(grad_pack, x), w_mix), in_front)
+    grad_out = sums[1]
     grad_front, grad_norm_gain, grad_taps = front_pull(grad_conv_low.astype(low).astype(f32))
     grad_tokens = (grad_resid + grad_front).astype(low)
-    advance(ffn_sums, grad_tokens)
-    grad_w_down = down_sum.done()
-    gu_halves = gu_sum.done()
-
-    mix_sum = SumRing(grad_mix.reshape(GROUP, wide_size, rows, PACK), wide_size, table)
+    gu_halves = gu_sum.done(mix_sum.last)
     out_sum = SumRing(grad_out.reshape(wide_size, rows, D), wide_size, table, rows)
-
-    down = partial_sum(lambda part_: product(hidden[part_], wd), ())
+    out_sum.step(gu_halves[0])
+    advance(gu_halves[0], mix_sum)
+
+    def in_down(across):
+        advance(across, mix_sum, out_sum)
+        return []
+
+    hidden_late = after(gu_halves[0], hidden)[0]
+    down = partial_sum(lambda x: product(rows_of(hidden_late, x), wd), in_down)
     block_out = ((resid + down) * is_valid[:, None]).astype(low)
 
     def to_owner(halves):
         blocks = [halves[0][0], halves[0][1], halves[1][0], halves[1][1]]
         return [blocks[0]] + [swap(blocks[r], r) for r in range(1, GROUP)]
 
+    mix_sum.step()
+    out_sum.step()
     grad_gate, grad_up = merge_gate_up(table, to_owner(gu_halves), wide_size, part, part_p)
+    advance(grad_gate, mix_sum, out_sum)
     grad_w_out = out_sum.done()
     mixer_grads = merge_mixer(table, to_owner(mix_sum.done()))
     gains = jnp.concatenate(

time: 845 us -> 819 us (0.969)
  matrix products: 141 us -> 120 us
  other arithmetic: 40.7 us -> 54.6 us
  local copies, waits for them, and re-layouts: 64.6 us -> 54.2 us
    dot_general x16, matrix products: 141 us -> 120 us  [dot(): lax.dot_general(left, right, (((over_left,), (over_right,)), ((), ())), p...]
    concatenate x0 -> x9, other arithmetic: none -> 20.1 us  [the longest x4 12.1 us: group_gather(): return jnp.concatenate([own, got[:count], across, got[count:]])]
    unnamed x276 -> x333, local copies, waits for them, and re-layouts: 53.4 us -> 40.6 us
    ppermute x56, waiting for transfers between devices: 138 us -> 127 us  [step(): lax.ppermute(sums[d], 'wide', round_ring(cycle, d))]
    ppermute x56, waiting for transfers between devices: 167 us -> 177 us  [step(): held.append(lax.ppermute(value, 'wide', round_ring(CYCLES[self.size], d)))]
    ppermute x36 -> x32, waiting for transfers between devices: 40.6 us -> 35 us  [swap(): return lax.ppermute(value, 'grp', [(i, i ^ over) for i in range(GROUP)])]
    ppermute x36 -> x32, starting transfers between devices: 19 us -> 15.3 us  [swap(): return lax.ppermute(value, 'grp', [(i, i ^ over) for i in range(GROUP)])]
  transfers between devices with their start and end apart: 158 -> 154, of which waited for: 65 -> 61; matrix products, arithmetic and copies ran while one was open for 18% -> 22% of each run, Pallas kernels for 9% -> 9%
where the time goes in v3:
time: 819 us; the launch traced here: 810 us
  waiting for transfers between devices  350 us (43%)
  starting transfers between devices  146 us (18%)
  matrix products  120 us (15%)
  Pallas kernels  80.8 us (10%)
  other arithmetic  54.6 us (7%)
  local copies, waits for them, and re-layouts  54.2 us (7%)
    ppermute x56, waiting for transfers between devices, step(): held.append(lax.ppermute(value, 'wide', round_ring(CYCLES[self.size], d)))  177 us
    ppermute x56, waiting for transfers between devices, step(): lax.ppermute(sums[d], 'wide', round_ring(cycle, d))  127 us
    dot_general x16, matrix products, dot(): lax.dot_general(left, right, (((over_left,), (over_right,)), ((), ())), p...  120 us
    ppermute x56, starting transfers between devices, step(): lax.ppermute(sums[d], 'wide', round_ring(cycle, d))  59.9 us
    ppermute x56, starting transfers between devices, step(): held.append(lax.ppermute(value, 'wide', round_ring(CYCLES[self.size], d)))  57.5 us
    unnamed x333, local copies, waits for them, and re-layouts  40.6 us
    ppermute x32, waiting for transfers between devices, swap(): return lax.ppermute(value, 'grp', [(i, i ^ over) for i in range(GROUP)])  35 us
    pallas_call x32, Pallas kernels, pick_add(): pl.pallas_call(body, grid_spec=pltpu.PrefetchScalarGridSpec(num_scalar_pr...  32.9 us
  transfers between devices with their start and end apart: 154, of which 61 were waited for; matrix products, arithmetic and copies ran while one was open for 22% of the time, Pallas kernels for 9%

profile of v3, /device:TPU:0, one launch (start us, length us, event | category | flops | bytes accessed | tf_op | source)
XLA Modules:
  0.0 810.0 jit_solution(16588249885155066393)
XLA Ops:
  22.8 7.9 collective-permute-done.4
  36.7 8.8 %collective-permute-done.8.refs_1_ = bf16[2,64,1664]{2,1,0:T(8,128)(2,1)S(1)} collective-permute-done((bf16[2,64,1664]{2,1,0:T(8,128)(2,1)S(1)}, bf16[2,64,1664]{2,1,0:T(8,128)(2,1)S(1)}, u32[]{:S(2)}, u32[]{:S(2)}) %collective-permute-start.8) | collective-permute-done | bytes 426016 | tf_op jit(solution)/shard_map/ppermute | solution.py:417
  48.1 10.2 %collective-permute-done.9.refs_2_ = bf16[2,64,1664]{2,1,0:T(8,128)(2,1)S(1)} collective-permute-done((bf16[2,64,1664]{2,1,0:T(8,128)(2,1)S(1)}, bf16[2,64,1664]{2,1,0:T(8,128)(2,1)S(1)}, u32[]{:S(2)}, u32[]{:S(2)}) %collective-permute-start.9) | collective-permute-done | bytes 426016 | tf_op jit(solution)/shard_map/ppermute | solution.py:417
  81.2 8.8 %collective-permute-done.11.refs_4_ = bf16[2,64,1664]{2,1,0:T(8,128)(2,1)S(1)} collective-permute-done((bf16[2,64,1664]{2,1,0:T(8,128)(2,1)S(1)}, bf16[2,64,1664]{2,1,0:T(8,128)(2,1)S(1)}, u32[]{:S(2)}, u32[]{:S(2)}) %collective-permute-start.11) | collective-permute-done | bytes 426016 | tf_op jit(solution)/shard_map/ppermute | solution.py:417
  141.5 8.9 %collective-permute-done.14.refs_7_ = bf16[2,64,1664]{2,1,0:T(8,128)(2,1)S(1)} collective-permute-done((bf16[2,64,1664]{2,1,0:T(8,128)(2,1)}, bf16[2,64,1664]{2,1,0:T(8,128)(2,1)S(1)}, u32[]{:S(2)}, u32[]{:S(2)}) %collective-permute-start.14) | collective-permute-done | bytes 426016 | tf_op jit(solution)/shard_map/ppermute | solution.py:417
  153.2 9.9 %place.4 = bf16[4,8,64,1664]{3,2,1,0:T(8,128)(2,1)S(1)} custom-call(s32[17]{0:T(128)S(1)} %pad_add_fusion.2.table_ref, bf16[2,64,1664]{2,1,0:T(8,128)(2,1)S(1)} %pad_maximum_fusion.11.refs_0_, bf16[2,64,1664]{2,1,0:T(8,128)(2,1)S(1)} %copy-done.24, bf16[2,64,1664]{2,1,0:T(8,128)(2,1)S(1)} %copy-done.28, bf16[2,64,1664]{2,1,0:T(8,128)(2,1)S(1)} %copy-done.32, ...), custom_call_target="tpu_custom_call" | custom-call | bytes 20447232 | tf_op jit(solution)/shard_map/place/pallas_call | solution.py:327
  163.2 7.7 fusion.39.pack_ref
  183.1 9.7 %collective-permute-done.52 = bf16[64,2816]{1,0:T(8,128)(2,1)S(1)} collective-permute-done((bf16[64,2816]{1,0:T(8,128)(2,1)S(1)}, bf16[64,2816]{1,0:T(8,128)(2,1)S(1)}, u32[]{:S(2)}, u32[]{:S(2)}) %collective-permute-start.52) | collective-permute-done | bytes 360480 | tf_op jit(solution)/shard_map/ppermute | solution.py:144
  206.0 12.5 %collective-permute-done.54.refs_9_ = bf16[2,64,2816]{2,1,0:T(8,128)(2,1)} collective-permute-done((bf16[2,64,2816]{2,1,0:T(8,128)(2,1)S(1)}, bf16[2,64,2816]{2,1,0:T(8,128)(2,1)}, u32[]{:S(2)}, u32[]{:S(2)}) %collective-permute-start.54) | collective-permute-done | bytes 720928 | tf_op jit(solution)/shard_map/ppermute | solution.py:417
  226.4 10.8 %collective-permute-done.55.refs_10_ = bf16[2,64,2816]{2,1,0:T(8,128)(2,1)} collective-permute-done((bf16[2,64,2816]{2,1,0:T(8,128)(2,1)}, bf16[2,64,2816]{2,1,0:T(8,128)(2,1)}, u32[]{:S(2)}, u32[]{:S(2)}) %collective-permute-start.55) | collective-permute-done | bytes 720928 | tf_op jit(solution)/shard_map/ppermute | solution.py:417
  242.8 12.5 %collective-permute-done.56.refs_11_ = bf16[2,64,2816]{2,1,0:T(8,128)(2,1)S(1)} collective-permute-done((bf16[2,64,2816]{2,1,0:T(8,128)(2,1)}, bf16[2,64,2816]{2,1,0:T(8,128)(2,1)S(1)}, u32[]{:S(2)}, u32[]{:S(2)}) %collective-permute-start.56) | collective-permute-done | bytes 720928 | tf_op jit(solution)/shard_map/ppermute | solution.py:417
  259.5 12.5 %collective-permute-done.57.refs_12_ = bf16[2,64,2816]{2,1,0:T(8,128)(2,1)S(1)} collective-permute-done((bf16[2,64,2816]{2,1,0:T(8,128)(2,1)S(1)}, bf16[2,64,2816]{2,1,0:T(8,128)(2,1)S(1)}, u32[]{:S(2)}, u32[]{:S(2)}) %collective-permute-start.57) | collective-permute-done | bytes 720928 | tf_op jit(solution)/shard_map/ppermute | solution.py:417
  273.9 14.4 %collective-permute-done.58.refs_13_ = bf16[2,64,2816]{2,1,0:T(8,128)(2,1)S(1)} collective-permute-done((bf16[2,64,2816]{2,1,0:T(8,128)(2,1)S(1)}, bf16[2,64,2816]{2,1,0:T(8,128)(2,1)S(1)}, u32[]{:S(2)}, u32[]{:S(2)}) %collective-permute-start.58) | collective-permute-done | bytes 720928 | tf_op jit(solution)/shard_map/ppermute | solution.py:417
  288.9 15.7 %collective-permute-done.59.refs_14_ = bf16[2,64,2816]{2,1,0:T(8,128)(2,1)S(1)} collective-permute-done((bf16[2,64,2816]{2,1,0:T(8,128)(2,1)S(1)}, bf16[2,64,2816]{2,1,0:T(8,128)(2,1)S(1)}, u32[]{:S(2)}, u32[]{:S(2)}) %collective-permute-start.59) | collective-permute-done | bytes 720928 | tf_op jit(solution)/shard_map/ppermute | solution.py:417
  309.0 19.7 %collective-permute-done.69.refs_9_ = bf16[176,1024]{1,0:T(8,128)(2,1)S(1)} collective-permute-done((bf16[176,1024]{1,0:T(8,128)(2,1)S(1)}, bf16[176,1024]{1,0:T(8,128)(2,1)S(1)}, u32[]{:S(2)}, u32[]{:S(2)}) %collective-permute-start.69) | collective-permute-done | bytes 360480 | tf_op jit(solution)/shard_map/ppermute | solution.py:417
  344.1 14.1 %fusion.47 = f32[1024,2816]{1,0:T(8,128)S(1)} fusion(bf16[1024,2048]{1,0:T(8,128)(2,1)} %pad_maximum_fusion.2, bf16[2048,2816]{1,0:T(8,128)(2,1)S(1)} %bitcast.169), kind=kOutput, calls=%fused_computation.148 | convolution fusion | flops 11811160064 | bytes 27262976 | tf_op jit(solution)/shard_map/dot_general | solution.py:29
  377.0 8.4 %collective-permute-done.74.refs_14_ = bf16[176,1024]{1,0:T(8,128)(2,1)S(1)} collective-permute-done((bf16[176,1024]{1,0:T(8,128)(2,1)S(1)}, bf16[176,1024]{1,0:T(8,128)(2,1)S(1)}, u32[]{:S(2)}, u32[]{:S(2)}) %collective-permute-start.74) | collective-permute-done | bytes 360480 | tf_op jit(solution)/shard_map/ppermute | solution.py:417
  397.0 15.9 %fusion.2 = (bf16[1024,1408]{1,0:T(8,128)(2,1)}, bf16[1024,1408]{1,0:T(8,128)(2,1)}) fusion(f32[1024,2816]{1,0:T(8,128)} %copy-done.83, bf16[1408,2048]{1,0:T(8,128)(2,1)} %bitcast.177, bf16[256,2048]{1,0:T(8,128)(2,1)} %copy-done.103, bf16[256,2048]{1,0:T(8,128)(2,1)} %copy-done.100, bf16[256,2048]{1,0:T(8,128)(2,1)} %copy-done.102, ...), kind=kOutput, calls=%fused_computation.7 | convolution fusion | flops 5943984128 | bytes 27262976 | tf_op jit(solution)/shard_map/dot_general | solution.py:29
  418.6 10.0 %convolution_convert_fusion.8 = bf16[512,2048]{1,0:T(8,128)(2,1)S(1)} fusion(bf16[2048,2816]{1,0:T(8,128)(2,1)} %bitcast.170, bf16[1024,2816]{1,0:T(8,128)(2,1)} %pad_maximum_fusion), kind=kOutput, calls=%fused_computation.29 | convolution fusion | flops 5906628608 | bytes 16515072 | tf_op jit(solution)/shard_map/dot_general | solution.py:29
  428.9 8.8 %convolution_convert_fusion.7 = bf16[512,2048]{1,0:T(8,128)(2,1)} fusion(bf16[2048,2816]{1,0:T(8,128)(2,1)S(1)} %bitcast.173, bf16[1024,2816]{1,0:T(8,128)(2,1)} %pad_maximum_fusion), kind=kOutput, calls=%fused_computation.28 | convolution fusion | flops 5906628608 | bytes 16515072 | tf_op jit(solution)/shard_map/dot_general | solution.py:29
  456.2 15.8 %convolution_convert_fusion = bf16[2048,2816]{1,0:T(8,128)(2,1)S(1)} fusion(bf16[1024,2048]{1,0:T(8,128)(2,1)} %pad_maximum_fusion.2, bf16[1024,2816]{1,0:T(8,128)(2,1)} %pad_maximum_fusion), kind=kOutput, calls=%fused_computation | convolution fusion | flops 11816927232 | bytes 21495808 | tf_op jit(solution)/shard_map/dot_general | solution.py:29
  475.3 23.1 %collective-permute-done.84.refs_3_ = bf16[176,1024]{1,0:T(8,128)(2,1)S(1)} collective-permute-done((bf16[176,1024]{1,0:T(8,128)(2,1)S(1)}, bf16[176,1024]{1,0:T(8,128)(2,1)S(1)}, u32[]{:S(2)}, u32[]{:S(2)}) %collective-permute-start.84) | collective-permute-done | bytes 360480 | tf_op jit(solution)/shard_map/ppermute | solution.py:459
  510.4 18.7 %collective-permute-done.87.refs_2_ = bf16[176,1024]{1,0:T(8,128)(2,1)S(1)} collective-permute-done((bf16[176,1024]{1,0:T(8,128)(2,1)S(1)}, bf16[176,1024]{1,0:T(8,128)(2,1)S(1)}, u32[]{:S(2)}, u32[]{:S(2)}) %collective-permute-start.87) | collective-permute-done | bytes 360480 | tf_op jit(solution)/shard_map/ppermute | solution.py:459
  542.1 9.7 %collective-permute-done.91.refs_2_ = bf16[2,64,2816]{2,1,0:T(8,128)(2,1)S(1)} collective-permute-done((bf16[2,64,2816]{2,1,0:T(8,128)(2,1)S(1)}, bf16[2,64,2816]{2,1,0:T(8,128)(2,1)S(1)}, u32[]{:S(2)}, u32[]{:S(2)}) %collective-permute-start.91) | collective-permute-done | bytes 720928 | tf_op jit(solution)/shard_map/ppermute | solution.py:459
  555.4 14.4 %mix_back.1 = bf16[1024,1664]{1,0:T(8,128)(2,1)S(1)} custom-call(s32[4]{0:T(128)S(1)} %pad_add_fusion.1.lens_ref, f32[1024,1664]{1,0:T(8,128)S(1)} %bitcast.168, bf16[1024,512]{1,0:T(8,128)(2,1)S(1)} %convolution_convert_fusion.13.grad_ref), custom_call_target="tpu_custom_call" | custom-call | flops 2000000000 | bytes 10000000 | tf_op jit(solution)/shard_map/mix_back/pallas_call | solution.py:125
  574.2 8.1 convolution_convert_fusion.1
  617.5 9.9 %collective-permute-done.100.refs_3_ = bf16[2,64,2816]{2,1,0:T(8,128)(2,1)S(1)} collective-permute-done((bf16[2,64,2816]{2,1,0:T(8,128)(2,1)}, bf16[2,64,2816]{2,1,0:T(8,128)(2,1)S(1)}, u32[]{:S(2)}, u32[]{:S(2)}) %collective-permute-start.100) | collective-permute-done | bytes 720928 | tf_op jit(solution)/shard_map/ppermute | solution.py:459
  631.2 8.8 %convolution_convert_fusion.5 = bf16[512,2048]{1,0:T(8,128)(2,1)} fusion(bf16[2048,1664]{1,0:T(8,128)(2,1)} %bitcast.176, bf16[1024,1664]{1,0:T(8,128)(2,1)} %copy-done.11), kind=kOutput, calls=%fused_computation.26 | convolution fusion | flops 3490709504 | bytes 10616832 | tf_op jit(solution)/shard_map/dot_general | solution.py:29
  649.2 9.4 %collective-permute-done.106.refs_2_ = bf16[2,64,1664]{2,1,0:T(8,128)(2,1)S(1)} collective-permute-done((bf16[2,64,1664]{2,1,0:T(8,128)(2,1)S(1)}, bf16[2,64,1664]{2,1,0:T(8,128)(2,1)S(1)}, u32[]{:S(2)}, u32[]{:S(2)}) %collective-permute-start.106) | collective-permute-done | bytes 426016 | tf_op jit(solution)/shard_map/ppermute | solution.py:459
  673.6 8.7 %collective-permute-done.112 = bf16[256,2048]{1,0:T(8,128)(2,1)} collective-permute-done((bf16[256,2048]{1,0:T(8,128)(2,1)S(1)}, bf16[256,2048]{1,0:T(8,128)(2,1)}, u32[]{:S(2)}, u32[]{:S(2)}) %collective-permute-start.112) | collective-permute-done | bytes 1048608 | tf_op jit(solution)/shard_map/ppermute | solution.py:144
  725.9 13.6 %collective-permute-done.141.refs_3_ = bf16[64,1024]{1,0:T(8,128)(2,1)S(1)} collective-permute-done((bf16[64,1024]{1,0:T(8,128)(2,1)S(1)}, bf16[64,1024]{1,0:T(8,128)(2,1)S(1)}, u32[]{:S(2)}, u32[]{:S(2)}) %collective-permute-start.141) | collective-permute-done | bytes 131104 | tf_op jit(solution)/shard_map/ppermute | solution.py:459
  777.2 10.1 %collective-permute-done.147.refs_3_ = bf16[64,1024]{1,0:T(8,128)(2,1)S(1)} collective-permute-done((bf16[64,1024]{1,0:T(8,128)(2,1)S(1)}, bf16[64,1024]{1,0:T(8,128)(2,1)S(1)}, u32[]{:S(2)}, u32[]{:S(2)}) %collective-permute-start.147) | collective-permute-done | bytes 131104 | tf_op jit(solution)/shard_map/ppermute | solution.py:459
  (766 shorter events, 428.3 us)
Async XLA Ops:
  32.9 27.4 %collective-permute-start.5 = (bf16[256,2048]{1,0:T(8,128)(2,1)S(1)}, bf16[256,2048]{1,0:T(8,128)(2,1)S(1)}, u32[]{:S(2)}, u32[]{:S(2)}) collective-permute-start(bf16[256,2048]{1,0:T(8,128)(2,1)S(1)} %add_convert_fusion.6), channel_id=1, source_target_pairs={{0,16},{8,24},{16,0},{24,8},{1,17},{9,25},{17,1},{25,9},{2,18},{10... | collective-permute-start | bytes 3145736 | tf_op jit(solution)/shard_map/ppermute | solution.py:144
  61.9 77.7 %collective-permute-start.6 = (bf16[512,2048]{1,0:T(8,128)(2,1)}, bf16[512,2048]{1,0:T(8,128)(2,1)}, u32[]{:S(2)}, u32[]{:S(2)}) collective-permute-start(bf16[512,2048]{1,0:T(8,128)(2,1)} %pad_maximum_fusion.5), channel_id=1, source_target_pairs={{0,8},{8,0},{16,24},{24,16},{1,9},{9,1},{17,25},{25,17},{2,10},{10... | collective-permute-start | bytes 6291464 | tf_op jit(solution)/shard_map/ppermute | solution.py:144
  150.4 29.5 %collective-permute-start.43 = (bf16[2,64,2816]{2,1,0:T(8,128)(2,1)S(1)}, bf16[2,64,2816]{2,1,0:T(8,128)(2,1)S(1)}, u32[]{:S(2)}, u32[]{:S(2)}) collective-permute-start(bf16[2,64,2816]{2,1,0:T(8,128)(2,1)S(1)} %collective-permute-done.42.refs_1_), channel_id=1, source_target_pairs={{0,2},{2,4},{4,6},{6,7},{7,5},{5,3},{3,1},{1,0},{8,10},{10,12},{12... | collective-permute-start | bytes 2162696 | tf_op jit(solution)/shard_map/ppermute | solution.py:417
  203.0 34.6 %collective-permute-start.40 = (bf16[256,2048]{1,0:T(8,128)(2,1)}, bf16[256,2048]{1,0:T(8,128)(2,1)}, u32[]{:S(2)}, u32[]{:S(2)}) collective-permute-start(bf16[256,2048]{1,0:T(8,128)(2,1)} %add_convert_fusion.5), channel_id=1, source_target_pairs={{0,16},{8,24},{16,0},{24,8},{1,17},{9,25},{17,1},{25,9},{2,18},{10... | collective-permute-start | bytes 3145736 | tf_op jit(solution)/shard_map/ppermute | solution.py:144
  206.0 31.7 %collective-permute-start.38 = (bf16[256,2048]{1,0:T(8,128)(2,1)}, bf16[256,2048]{1,0:T(8,128)(2,1)}, u32[]{:S(2)}, u32[]{:S(2)}) collective-permute-start(bf16[256,2048]{1,0:T(8,128)(2,1)} %slice.283), channel_id=1, source_target_pairs={{0,8},{8,0},{16,24},{24,16},{1,9},{9,1},{17,25},{25,17},{2,10},{10... | collective-permute-start | bytes 3145736 | tf_op jit(solution)/shard_map/ppermute | solution.py:144
  225.9 29.8 %collective-permute-start.62 = (bf16[256,2048]{1,0:T(8,128)(2,1)S(1)}, bf16[256,2048]{1,0:T(8,128)(2,1)S(1)}, u32[]{:S(2)}, u32[]{:S(2)}) collective-permute-start(bf16[256,2048]{1,0:T(8,128)(2,1)S(1)} %copy-done.91), channel_id=1, source_target_pairs={{0,16},{8,24},{16,0},{24,8},{1,17},{9,25},{17,1},{25,9},{2,18},{10... | collective-permute-start | bytes 3145736 | tf_op jit(solution)/shard_map/ppermute | solution.py:144
  242.2 31.3 %collective-permute-start.47 = (bf16[256,2048]{1,0:T(8,128)(2,1)S(1)}, bf16[256,2048]{1,0:T(8,128)(2,1)S(1)}, u32[]{:S(2)}, u32[]{:S(2)}) collective-permute-start(bf16[256,2048]{1,0:T(8,128)(2,1)S(1)} %multiply_convert_fusion.2), channel_id=1, source_target_pairs={{0,16},{8,24},{16,0},{24,8},{1,17},{9,25},{17,1},{25,9},{2,18},{10... | collective-permute-start | bytes 3145736 | tf_op jit(solution)/shard_map/ppermute | solution.py:144
  255.9 51.4 %collective-permute-start.63 = (bf16[512,2048]{1,0:T(8,128)(2,1)S(1)}, bf16[512,2048]{1,0:T(8,128)(2,1)S(1)}, u32[]{:S(2)}, u32[]{:S(2)}) collective-permute-start(bf16[512,2048]{1,0:T(8,128)(2,1)S(1)} %pad_maximum_fusion.7), channel_id=1, source_target_pairs={{0,8},{8,0},{16,24},{24,16},{1,9},{9,1},{17,25},{25,17},{2,10},{10... | collective-permute-start | bytes 6291464 | tf_op jit(solution)/shard_map/ppermute | solution.py:144
  273.8 67.8 %collective-permute-start.50 = (bf16[512,2048]{1,0:T(8,128)(2,1)S(1)}, bf16[512,2048]{1,0:T(8,128)(2,1)S(1)}, u32[]{:S(2)}, u32[]{:S(2)}) collective-permute-start(bf16[512,2048]{1,0:T(8,128)(2,1)S(1)} %pad_maximum_fusion.6), channel_id=1, source_target_pairs={{0,8},{8,0},{16,24},{24,16},{1,9},{9,1},{17,25},{25,17},{2,10},{10... | collective-permute-start | bytes 6291464 | tf_op jit(solution)/shard_map/ppermute | solution.py:144
  304.6 26.9 %collective-permute-start.60 = (bf16[2,64,2816]{2,1,0:T(8,128)(2,1)S(1)}, bf16[2,64,2816]{2,1,0:T(8,128)(2,1)S(1)}, u32[]{:S(2)}, u32[]{:S(2)}) collective-permute-start(bf16[2,64,2816]{2,1,0:T(8,128)(2,1)S(1)} %collective-permute-done.59.refs_14_), channel_id=1, source_target_pairs={{2,0},{4,2},{6,4},{7,6},{5,7},{3,5},{1,3},{0,1},{10,8},{12,10},{14... | collective-permute-start | bytes 2162696 | tf_op jit(solution)/shard_map/ppermute | solution.py:417
  305.2 26.3 %collective-permute-start.51 = (bf16[2,64,2816]{2,1,0:T(8,128)(2,1)S(1)}, bf16[2,64,2816]{2,1,0:T(8,128)(2,1)S(1)}, u32[]{:S(2)}, u32[]{:S(2)}) collective-permute-start(bf16[2,64,2816]{2,1,0:T(8,128)(2,1)S(1)} %collective-permute-done.48.refs_6_), channel_id=1, source_target_pairs={{0,2},{2,4},{4,6},{6,7},{7,5},{5,3},{3,1},{1,0},{8,10},{10,12},{12... | collective-permute-start | bytes 2162696 | tf_op jit(solution)/shard_map/ppermute | solution.py:417
  307.5 32.3 %collective-permute-start.61 = (bf16[176,1024]{1,0:T(8,128)(2,1)S(1)}, bf16[176,1024]{1,0:T(8,128)(2,1)S(1)}, u32[]{:S(2)}, u32[]{:S(2)}) collective-permute-start(bf16[176,1024]{1,0:T(8,128)(2,1)S(1)} %collective-permute-done.49.refs_1_), channel_id=1, source_target_pairs={{0,2},{2,4},{4,6},{6,7},{7,5},{5,3},{3,1},{1,0},{8,10},{10,12},{12... | collective-permute-start | bytes 1081352 | tf_op jit(solution)/shard_map/ppermute | solution.py:417
  387.5 52.9 %collective-permute-start.77 = (bf16[176,1024]{1,0:T(8,128)(2,1)S(1)}, bf16[176,1024]{1,0:T(8,128)(2,1)S(1)}, u32[]{:S(2)}, u32[]{:S(2)}) collective-permute-start(bf16[176,1024]{1,0:T(8,128)(2,1)S(1)} %get-tuple-element.227), channel_id=1, source_target_pairs={{0,2},{2,4},{4,6},{6,7},{7,5},{5,3},{3,1},{1,0},{8,10},{10,12},{12... | collective-permute-start | bytes 1081352 | tf_op jit(solution)/shard_map/ppermute | solution.py:459
  388.3 52.1 %collective-permute-start.78 = (bf16[176,1024]{1,0:T(8,128)(2,1)S(1)}, bf16[176,1024]{1,0:T(8,128)(2,1)S(1)}, u32[]{:S(2)}, u32[]{:S(2)}) collective-permute-start(bf16[176,1024]{1,0:T(8,128)(2,1)S(1)} %get-tuple-element.235), channel_id=1, source_target_pairs={{2,0},{4,2},{6,4},{7,6},{5,7},{3,5},{1,3},{0,1},{10,8},{12,10},{14... | collective-permute-start | bytes 1081352 | tf_op jit(solution)/shard_map/ppermute | solution.py:459
  440.1 60.1 %collective-permute-start.89 = (bf16[256,2048]{1,0:T(8,128)(2,1)}, bf16[256,2048]{1,0:T(8,128)(2,1)}, u32[]{:S(2)}, u32[]{:S(2)}) collective-permute-start(bf16[256,2048]{1,0:T(8,128)(2,1)} %slice.299), channel_id=1, source_target_pairs={{0,8},{8,0},{16,24},{24,16},{1,9},{9,1},{17,25},{25,17},{2,10},{10... | collective-permute-start | bytes 3145736 | tf_op jit(solution)/shard_map/ppermute | solution.py:144
  455.6 44.5 %collective-permute-start.90 = (bf16[256,2048]{1,0:T(8,128)(2,1)}, bf16[256,2048]{1,0:T(8,128)(2,1)}, u32[]{:S(2)}, u32[]{:S(2)}) collective-permute-start(bf16[256,2048]{1,0:T(8,128)(2,1)} %add_convert_fusion.4), channel_id=1, source_target_pairs={{0,16},{8,24},{16,0},{24,8},{1,17},{9,25},{17,1},{25,9},{2,18},{10... | collective-permute-start | bytes 3145736 | tf_op jit(solution)/shard_map/ppermute | solution.py:144
  472.6 26.5 %collective-permute-start.81 = (bf16[2,64,2816]{2,1,0:T(8,128)(2,1)S(1)}, bf16[2,64,2816]{2,1,0:T(8,128)(2,1)S(1)}, u32[]{:S(2)}, u32[]{:S(2)}) collective-permute-start(bf16[2,64,2816]{2,1,0:T(8,128)(2,1)S(1)} %get-tuple-element.245), channel_id=1, source_target_pairs={{0,2},{2,4},{4,6},{6,7},{7,5},{5,3},{3,1},{1,0},{8,10},{10,12},{12... | collective-permute-start | bytes 2162696 | tf_op jit(solution)/shard_map/ppermute | solution.py:459
  504.8 28.0 %collective-permute-start.93 = (bf16[256,2048]{1,0:T(8,128)(2,1)S(1)}, bf16[256,2048]{1,0:T(8,128)(2,1)S(1)}, u32[]{:S(2)}, u32[]{:S(2)}) collective-permute-start(bf16[256,2048]{1,0:T(8,128)(2,1)S(1)} %fusion.38), channel_id=1, source_target_pairs={{0,16},{8,24},{16,0},{24,8},{1,17},{9,25},{17,1},{25,9},{2,18},{10... | collective-permute-start | bytes 3145736 | tf_op jit(solution)/shard_map/ppermute | solution.py:144
  506.4 25.5 %collective-permute-start.85 = (bf16[2,64,2816]{2,1,0:T(8,128)(2,1)S(1)}, bf16[2,64,2816]{2,1,0:T(8,128)(2,1)S(1)}, u32[]{:S(2)}, u32[]{:S(2)}) collective-permute-start(bf16[2,64,2816]{2,1,0:T(8,128)(2,1)S(1)} %get-tuple-element.253), channel_id=1, source_target_pairs={{0,2},{2,4},{4,6},{6,7},{7,5},{5,3},{3,1},{1,0},{8,10},{10,12},{12... | collective-permute-start | bytes 2162696 | tf_op jit(solution)/shard_map/ppermute | solution.py:459
  601.5 25.8 %collective-permute-start.99 = (bf16[2,64,2816]{2,1,0:T(8,128)(2,1)S(1)}, bf16[2,64,2816]{2,1,0:T(8,128)(2,1)S(1)}, u32[]{:S(2)}, u32[]{:S(2)}) collective-permute-start(bf16[2,64,2816]{2,1,0:T(8,128)(2,1)S(1)} %get-tuple-element.279), channel_id=1, source_target_pairs={{0,2},{2,4},{4,6},{6,7},{7,5},{5,3},{3,1},{1,0},{8,10},{10,12},{12... | collective-permute-start | bytes 2162696 | tf_op jit(solution)/shard_map/ppermute | solution.py:459
  614.1 28.1 %collective-permute-start.104 = (bf16[2,64,1664]{2,1,0:T(8,128)(2,1)}, bf16[2,64,1664]{2,1,0:T(8,128)(2,1)}, u32[]{:S(2)}, u32[]{:S(2)}) collective-permute-start(bf16[2,64,1664]{2,1,0:T(8,128)(2,1)} %get-tuple-element.276), channel_id=1, source_target_pairs={{0,2},{2,4},{4,6},{6,7},{7,5},{5,3},{3,1},{1,0},{8,10},{10,12},{12... | collective-permute-start | bytes 1277960 | tf_op jit(solution)/shard_map/ppermute | solution.py:459
  614.8 27.5 %collective-permute-start.105 = (bf16[2,64,1664]{2,1,0:T(8,128)(2,1)}, bf16[2,64,1664]{2,1,0:T(8,128)(2,1)}, u32[]{:S(2)}, u32[]{:S(2)}) collective-permute-start(bf16[2,64,1664]{2,1,0:T(8,128)(2,1)} %get-tuple-element.286), channel_id=1, source_target_pairs={{2,0},{4,2},{6,4},{7,6},{5,7},{3,5},{1,3},{0,1},{10,8},{12,10},{14... | collective-permute-start | bytes 1277960 | tf_op jit(solution)/shard_map/ppermute | solution.py:459
  629.2 31.7 %collective-permute-start.102 = (bf16[2,64,2816]{2,1,0:T(8,128)(2,1)}, bf16[2,64,2816]{2,1,0:T(8,128)(2,1)S(1)}, u32[]{:S(2)}, u32[]{:S(2)}) collective-permute-start(bf16[2,64,2816]{2,1,0:T(8,128)(2,1)} %get-tuple-element.284), channel_id=1, source_target_pairs={{0,2},{2,4},{4,6},{6,7},{7,5},{5,3},{3,1},{1,0},{8,10},{10,12},{12... | collective-permute-start | bytes 2162696 | tf_op jit(solution)/shard_map/ppermute | solution.py:459
  629.8 32.3 %collective-permute-start.103 = (bf16[2,64,2816]{2,1,0:T(8,128)(2,1)}, bf16[2,64,2816]{2,1,0:T(8,128)(2,1)S(1)}, u32[]{:S(2)}, u32[]{:S(2)}) collective-permute-start(bf16[2,64,2816]{2,1,0:T(8,128)(2,1)} %get-tuple-element.285), channel_id=1, source_target_pairs={{2,0},{4,2},{6,4},{7,6},{5,7},{3,5},{1,3},{0,1},{10,8},{12,10},{14... | collective-permute-start | bytes 2162696 | tf_op jit(solution)/shard_map/ppermute | solution.py:459
  642.3 40.0 %collective-permute-start.111 = (bf16[256,2048]{1,0:T(8,128)(2,1)}, bf16[256,2048]{1,0:T(8,128)(2,1)}, u32[]{:S(2)}, u32[]{:S(2)}) collective-permute-start(bf16[256,2048]{1,0:T(8,128)(2,1)} %slice.309), channel_id=1, source_target_pairs={{0,8},{8,0},{16,24},{24,16},{1,9},{9,1},{17,25},{25,17},{2,10},{10... | collective-permute-start | bytes 3145736 | tf_op jit(solution)/shard_map/ppermute | solution.py:144
  663.7 25.0 %collective-permute-start.134 = (bf16[64,1024]{1,0:T(8,128)(2,1)S(1)}, bf16[64,1024]{1,0:T(8,128)(2,1)S(1)}, u32[]{:S(2)}, u32[]{:S(2)}) collective-permute-start(bf16[64,1024]{1,0:T(8,128)(2,1)S(1)} %get-tuple-element.326), channel_id=1, source_target_pairs={{0,2},{2,4},{4,6},{6,7},{7,5},{5,3},{3,1},{1,0},{8,10},{10,12},{12... | collective-permute-start | bytes 393224 | tf_op jit(solution)/shard_map/ppermute | solution.py:459
  712.3 29.0 %collective-permute-start.152 = (bf16[176,1024]{1,0:T(8,128)(2,1)S(1)}, bf16[176,1024]{1,0:T(8,128)(2,1)S(1)}, u32[]{:S(2)}, u32[]{:S(2)}) collective-permute-start(bf16[176,1024]{1,0:T(8,128)(2,1)S(1)} %get-tuple-element.350), channel_id=1, source_target_pairs={{0,2},{2,4},{4,6},{6,7},{7,5},{5,3},{3,1},{1,0},{8,10},{10,12},{12... | collective-permute-start | bytes 1081352 | tf_op jit(solution)/shard_map/ppermute | solution.py:459
  719.6 25.7 %collective-permute-start.153 = (bf16[176,1024]{1,0:T(8,128)(2,1)S(1)}, bf16[176,1024]{1,0:T(8,128)(2,1)S(1)}, u32[]{:S(2)}, u32[]{:S(2)}) collective-permute-start(bf16[176,1024]{1,0:T(8,128)(2,1)S(1)} %get-tuple-element.351), channel_id=1, source_target_pairs={{2,0},{4,2},{6,4},{7,6},{5,7},{3,5},{1,3},{0,1},{10,8},{12,10},{14... | collective-permute-start | bytes 1081352 | tf_op jit(solution)/shard_map/ppermute | solution.py:459
  722.6 33.5 %collective-permute-start.122 = (bf16[2,64,1664]{2,1,0:T(8,128)(2,1)}, bf16[2,64,1664]{2,1,0:T(8,128)(2,1)S(1)}, u32[]{:S(2)}, u32[]{:S(2)}) collective-permute-start(bf16[2,64,1664]{2,1,0:T(8,128)(2,1)} %get-tuple-element.308), channel_id=1, source_target_pairs={{0,2},{2,4},{4,6},{6,7},{7,5},{5,3},{3,1},{1,0},{8,10},{10,12},{12... | collective-permute-start | bytes 1277960 | tf_op jit(solution)/shard_map/ppermute | solution.py:459
  723.2 32.9 %collective-permute-start.123 = (bf16[2,64,1664]{2,1,0:T(8,128)(2,1)}, bf16[2,64,1664]{2,1,0:T(8,128)(2,1)S(1)}, u32[]{:S(2)}, u32[]{:S(2)}) collective-permute-start(bf16[2,64,1664]{2,1,0:T(8,128)(2,1)} %get-tuple-element.309), channel_id=1, source_target_pairs={{2,0},{4,2},{6,4},{7,6},{5,7},{3,5},{1,3},{0,1},{10,8},{12,10},{14... | collective-permute-start | bytes 1277960 | tf_op jit(solution)/shard_map/ppermute | solution.py:459
  767.4 28.8 %collective-permute-start.108 = (bf16[256,2048]{1,0:T(8,128)(2,1)}, bf16[256,2048]{1,0:T(8,128)(2,1)}, u32[]{:S(2)}, u32[]{:S(2)}) collective-permute-start(bf16[256,2048]{1,0:T(8,128)(2,1)} %slice.305), channel_id=1, source_target_pairs={{0,8},{8,0},{16,24},{24,16},{1,9},{9,1},{17,25},{25,17},{2,10},{10... | collective-permute-start | bytes 3145736 | tf_op jit(solution)/shard_map/ppermute | solution.py:144
  775.6 26.3 %collective-permute-start.110 = (bf16[256,2048]{1,0:T(8,128)(2,1)}, bf16[256,2048]{1,0:T(8,128)(2,1)S(1)}, u32[]{:S(2)}, u32[]{:S(2)}) collective-permute-start(bf16[256,2048]{1,0:T(8,128)(2,1)} %add_convert_fusion.1), channel_id=1, source_target_pairs={{0,16},{8,24},{16,0},{24,8},{1,17},{9,25},{17,1},{25,9},{2,18},{10... | collective-permute-start | bytes 3145736 | tf_op jit(solution)/shard_map/ppermute | solution.py:144
  (288 other events, 3561.1 us)

commit v4 on v3

--- a/solution.py
+++ b/solution.py
@@ -181,9 +181,12 @@
     return stack
 
 
-def sum_everywhere(value, wide_size):
-    for axis, size, step in list(steps_of("grp", GROUP)) + list(steps_of("wide", wide_size)):
-        value = value + lax.ppermute(value, axis, [(i, i ^ step) for i in range(size)])
+def sum_everywhere(value, wide_size, tokens):
+    for k, (axis, size, step) in enumerate(
+        list(steps_of("grp", GROUP)) + list(steps_of("wide", wide_size))
+    ):
+        got = lax.ppermute(value, axis, [(i, i ^ step) for i in range(size)])
+        value = value + (after(tokens[k], got)[0] if k < len(tokens) else got)
     return value
 
 
@@ -603,18 +606,17 @@
 
     def in_forward(across):
         advance(across, gu_ring)
-        advance(gu_ring.seen(), gu_ring)
+        advance(gu_ring.seen(), gu_ring, down_ring)
         return [gu_ring.seen()]
 
     resid = inputs + partial_sum(lambda x: product(rows_of(mixed, x), wo), in_forward)
     normed_f, middle_pull = jax.vjp(rms_norm, resid, g_two)
     normed_own = normed_f.astype(low)
-    advance(normed_own, gu_ring)
+    advance(normed_own, gu_ring, down_ring)
 
     def in_gather():
         down_ring.step(gu_ring.seen())
-        down_ring.step()
-        return down_ring.seen()
+        return (gu_ring.seen(), down_ring.seen())
 
     normed = group_gather(normed_own, in_gather)
     w_gu = gu_ring.done(down_ring.seen())
@@ -691,35 +693,51 @@
 
     grad_conv_low = partial_sum(lambda x: product_nt(rows_of(grad_pack, x), w_mix), in_front)
     grad_out = sums[1]
-    grad_front, grad_norm_gain, grad_taps = front_pull(grad_conv_low.astype(low).astype(f32))
-    grad_tokens = (grad_resid + grad_front).astype(low)
+    mix_sum.step(grad_conv_low)
     gu_halves = gu_sum.done(mix_sum.last)
     out_sum = SumRing(grad_out.reshape(wide_size, rows, D), wide_size, table, rows)
     out_sum.step(gu_halves[0])
-    advance(gu_halves[0], mix_sum)
+    grad_conv_low = after(out_sum.last, grad_conv_low)[0]
+    grad_front, grad_norm_gain, grad_taps = front_pull(grad_conv_low.astype(low).astype(f32))
+    grad_tokens = bar((grad_resid + grad_front).astype(low))
+    mix_sum.step(grad_tokens)
+    out_sum.step(mix_sum.last)
+    out_sum.step()
 
     def in_down(across):
-        advance(across, mix_sum, out_sum)
-        return []
-
-    hidden_late = after(gu_halves[0], hidden)[0]
+        mix_sum.step(across)
+        out_sum.step(mix_sum.last)
+        out_sum.step()
+        return [out_sum.last]
+
+    hidden_late = after(out_sum.last, hidden)[0]
     down = partial_sum(lambda x: product(rows_of(hidden_late, x), wd), in_down)
-    block_out = ((resid + down) * is_valid[:, None]).astype(low)
+    block_out = bar(((resid + down) * is_valid[:, None]).astype(low))
+    mix_sum.step(block_out)
+    out_sum.step(mix_sum.last)
+    out_sum.step()
+    gains = jnp.concatenate(
+        [grad_norm_gain[None], grad_taps, grad_ffn_gain[None], jnp.zeros((3, D), f32)], axis=0
+    )
+    gains = after(out_sum.last, gains)[0]
+    seen = []
 
     def to_owner(halves):
         blocks = [halves[0][0], halves[0][1], halves[1][0], halves[1][1]]
         return [blocks[0]] + [swap(blocks[r], r) for r in range(1, GROUP)]
 
-    mix_sum.step()
-    out_sum.step()
-    grad_gate, grad_up = merge_gate_up(table, to_owner(gu_halves), wide_size, part, part_p)
-    advance(grad_gate, mix_sum, out_sum)
-    grad_w_out = out_sum.done()
-    mixer_grads = merge_mixer(table, to_owner(mix_sum.done()))
-    gains = jnp.concatenate(
-        [grad_norm_gain[None], grad_taps, grad_ffn_gain[None], jnp.zeros((3, D), f32)], axis=0
-    )
-    gains = sum_everywhere(gains, wide_size).reshape(8, GROUP * wide_size, rows)
+    gu_blocks = to_owner(after(out_sum.last, *gu_halves))
+    mix_blocks = to_owner(mix_sum.done(out_sum.last))
+    seen.append(mix_blocks[0])
+    grad_w_out = out_sum.done(mix_blocks[0])
+    seen.append(grad_w_out)
+    grad_gate, grad_up = merge_gate_up(
+        table, after(grad_w_out, *gu_blocks), wide_size, part, part_p
+    )
+    seen.append(grad_gate)
+    mixer_grads = merge_mixer(table, after(grad_gate, *mix_blocks))
+    seen.append(mixer_grads[0])
+    gains = sum_everywhere(gains, wide_size, seen).reshape(8, GROUP * wide_size, rows)
     gains = lax.dynamic_index_in_dim(gains, spot, 1, keepdims=False)
     return (
         block_out,

time: 819 us -> 824 us (level)
  waiting for transfers between devices: 350 us -> 378 us
  other arithmetic: 54.6 us -> 46.3 us
    ppermute x56, waiting for transfers between devices: 127 us -> 158 us  [step(): lax.ppermute(sums[d], 'wide', round_ring(cycle, d))]
    unnamed x333 -> x295, local copies, waits for them, and re-layouts: 40.6 us -> 34.1 us
  transfers between devices with their start and end apart: 154 -> 154, of which waited for: 61 -> 68; matrix products, arithmetic and copies ran while one was open for 22% -> 19% of each run, Pallas kernels for 9% -> 8%
where the time goes in v4:
time: 824 us; the launch traced here: 817 us
  waiting for transfers between devices  378 us (46%)
  starting transfers between devices  148 us (18%)
  matrix products  118 us (14%)
  Pallas kernels  75.3 us (9%)
  local copies, waits for them, and re-layouts  47.1 us (6%)
  other arithmetic  46.3 us (6%)
    ppermute x56, waiting for transfers between devices, step(): held.append(lax.ppermute(value, 'wide', round_ring(CYCLES[self.size], d)))  175 us
    ppermute x56, waiting for transfers between devices, step(): lax.ppermute(sums[d], 'wide', round_ring(cycle, d))  158 us
    dot_general x16, matrix products, dot(): lax.dot_general(left, right, (((over_left,), (over_right,)), ((), ())), p...  118 us
    ppermute x56, starting transfers between devices, step(): lax.ppermute(sums[d], 'wide', round_ring(cycle, d))  58.9 us
    ppermute x56, starting transfers between devices, step(): held.append(lax.ppermute(value, 'wide', round_ring(CYCLES[self.size], d)))  58.7 us
    unnamed x295, local copies, waits for them, and re-layouts  34.1 us
    ppermute x32, waiting for transfers between devices, swap(): return lax.ppermute(value, 'grp', [(i, i ^ over) for i in range(GROUP)])  32.7 us
    pallas_call x32, Pallas kernels, pick_add(): pl.pallas_call(body, grid_spec=pltpu.PrefetchScalarGridSpec(num_scalar_pr...  28.5 us
  transfers between devices with their start and end apart: 154, of which 68 were waited for; matrix products, arithmetic and copies ran while one was open for 19% of the time, Pallas kernels for 8%

profile of v4, /device:TPU:0, one launch (start us, length us, event | category | flops | bytes accessed | tf_op | source)
XLA Modules:
  0.0 816.6 jit_solution(8028886194952598885)
XLA Ops:
  22.8 7.9 collective-permute-done.4
  36.7 8.8 %collective-permute-done.8.refs_1_ = bf16[2,64,1664]{2,1,0:T(8,128)(2,1)S(1)} collective-permute-done((bf16[2,64,1664]{2,1,0:T(8,128)(2,1)S(1)}, bf16[2,64,1664]{2,1,0:T(8,128)(2,1)S(1)}, u32[]{:S(2)}, u32[]{:S(2)}) %collective-permute-start.8) | collective-permute-done | bytes 426016 | tf_op jit(solution)/shard_map/ppermute | solution.py:420
  48.1 10.2 %collective-permute-done.9.refs_2_ = bf16[2,64,1664]{2,1,0:T(8,128)(2,1)S(1)} collective-permute-done((bf16[2,64,1664]{2,1,0:T(8,128)(2,1)S(1)}, bf16[2,64,1664]{2,1,0:T(8,128)(2,1)S(1)}, u32[]{:S(2)}, u32[]{:S(2)}) %collective-permute-start.9) | collective-permute-done | bytes 426016 | tf_op jit(solution)/shard_map/ppermute | solution.py:420
  81.1 8.8 %collective-permute-done.11.refs_4_ = bf16[2,64,1664]{2,1,0:T(8,128)(2,1)S(1)} collective-permute-done((bf16[2,64,1664]{2,1,0:T(8,128)(2,1)S(1)}, bf16[2,64,1664]{2,1,0:T(8,128)(2,1)S(1)}, u32[]{:S(2)}, u32[]{:S(2)}) %collective-permute-start.11) | collective-permute-done | bytes 426016 | tf_op jit(solution)/shard_map/ppermute | solution.py:420
  141.9 8.0 collective-permute-done.14.refs_7_
  153.2 8.9 %place.4 = bf16[4,8,64,1664]{3,2,1,0:T(8,128)(2,1)S(1)} custom-call(s32[17]{0:T(128)S(1)} %pad_add_fusion.2.table_ref, bf16[2,64,1664]{2,1,0:T(8,128)(2,1)S(1)} %pad_maximum_fusion.11.refs_0_, bf16[2,64,1664]{2,1,0:T(8,128)(2,1)S(1)} %collective-permute-done.8.refs_1_, bf16[2,64,1664]{2,1,0:T(8,128)(2,1)S(1)} %copy-done.21, ...), custom_call_target="tpu_custom_call" | custom-call | bytes 20447232 | tf_op jit(solution)/shard_map/place/pallas_call | solution.py:330
  162.2 7.7 fusion.38.pack_ref
  170.0 7.4 mix.1
  182.4 9.7 %collective-permute-done.53 = bf16[64,2816]{1,0:T(8,128)(2,1)S(1)} collective-permute-done((bf16[64,2816]{1,0:T(8,128)(2,1)S(1)}, bf16[64,2816]{1,0:T(8,128)(2,1)S(1)}, u32[]{:S(2)}, u32[]{:S(2)}) %collective-permute-start.53) | collective-permute-done | bytes 360480 | tf_op jit(solution)/shard_map/ppermute | solution.py:144
  205.0 12.5 %collective-permute-done.55.refs_9_ = bf16[2,64,2816]{2,1,0:T(8,128)(2,1)} collective-permute-done((bf16[2,64,2816]{2,1,0:T(8,128)(2,1)S(1)}, bf16[2,64,2816]{2,1,0:T(8,128)(2,1)}, u32[]{:S(2)}, u32[]{:S(2)}) %collective-permute-start.55) | collective-permute-done | bytes 720928 | tf_op jit(solution)/shard_map/ppermute | solution.py:420
  225.3 10.7 %collective-permute-done.56.refs_10_ = bf16[2,64,2816]{2,1,0:T(8,128)(2,1)} collective-permute-done((bf16[2,64,2816]{2,1,0:T(8,128)(2,1)}, bf16[2,64,2816]{2,1,0:T(8,128)(2,1)}, u32[]{:S(2)}, u32[]{:S(2)}) %collective-permute-start.56) | collective-permute-done | bytes 720928 | tf_op jit(solution)/shard_map/ppermute | solution.py:420
  240.8 13.0 %collective-permute-done.57.refs_11_ = bf16[2,64,2816]{2,1,0:T(8,128)(2,1)S(1)} collective-permute-done((bf16[2,64,2816]{2,1,0:T(8,128)(2,1)}, bf16[2,64,2816]{2,1,0:T(8,128)(2,1)S(1)}, u32[]{:S(2)}, u32[]{:S(2)}) %collective-permute-start.57) | collective-permute-done | bytes 720928 | tf_op jit(solution)/shard_map/ppermute | solution.py:420
  257.7 7.8 collective-permute-done.49.refs_1_
  270.8 15.2 %collective-permute-done.50.refs_2_ = bf16[176,1024]{1,0:T(8,128)(2,1)S(1)} collective-permute-done((bf16[176,1024]{1,0:T(8,128)(2,1)S(1)}, bf16[176,1024]{1,0:T(8,128)(2,1)S(1)}, u32[]{:S(2)}, u32[]{:S(2)}) %collective-permute-start.50) | collective-permute-done | bytes 360480 | tf_op jit(solution)/shard_map/ppermute | solution.py:420
  288.3 24.3 %collective-permute-done.69.refs_9_ = bf16[176,1024]{1,0:T(8,128)(2,1)S(1)} collective-permute-done((bf16[176,1024]{1,0:T(8,128)(2,1)S(1)}, bf16[176,1024]{1,0:T(8,128)(2,1)S(1)}, u32[]{:S(2)}, u32[]{:S(2)}) %collective-permute-start.69) | collective-permute-done | bytes 360480 | tf_op jit(solution)/shard_map/ppermute | solution.py:420
  315.2 8.7 %collective-permute-done.70.refs_10_ = bf16[176,1024]{1,0:T(8,128)(2,1)S(1)} collective-permute-done((bf16[176,1024]{1,0:T(8,128)(2,1)S(1)}, bf16[176,1024]{1,0:T(8,128)(2,1)S(1)}, u32[]{:S(2)}, u32[]{:S(2)}) %collective-permute-start.70) | collective-permute-done | bytes 360480 | tf_op jit(solution)/shard_map/ppermute | solution.py:420
  328.2 11.2 %collective-permute-done.61.refs_15_ = bf16[2,64,2816]{2,1,0:T(8,128)(2,1)S(1)} collective-permute-done((bf16[2,64,2816]{2,1,0:T(8,128)(2,1)S(1)}, bf16[2,64,2816]{2,1,0:T(8,128)(2,1)S(1)}, u32[]{:S(2)}, u32[]{:S(2)}) %collective-permute-start.61) | collective-permute-done | bytes 720928 | tf_op jit(solution)/shard_map/ppermute | solution.py:420
  350.2 14.1 %fusion.45 = f32[1024,2816]{1,0:T(8,128)S(1)} fusion(bf16[1024,2048]{1,0:T(8,128)(2,1)} %pad_maximum_fusion.2, bf16[2048,2816]{1,0:T(8,128)(2,1)S(1)} %bitcast.167), kind=kOutput, calls=%fused_computation.146 | convolution fusion | flops 11811160064 | bytes 27262976 | tf_op jit(solution)/shard_map/dot_general | solution.py:29
  396.2 16.1 %fusion.2 = (bf16[1024,1408]{1,0:T(8,128)(2,1)}, bf16[1024,1408]{1,0:T(8,128)(2,1)}) fusion(f32[1024,2816]{1,0:T(8,128)} %copy-done.73, bf16[1408,2048]{1,0:T(8,128)(2,1)} %bitcast.177, bf16[256,2048]{1,0:T(8,128)(2,1)} %copy-done.94, bf16[256,2048]{1,0:T(8,128)(2,1)S(1)} %copy-done.90, bf16[256,2048]{1,0:T(8,128)(2,1)} %copy-done.93, ...), kind=kOutput, calls=%fused_computation.7 | convolution fusion | flops 5943984128 | bytes 27262976 | tf_op jit(solution)/shard_map/dot_general | solution.py:29
  418.0 11.5 %convolution_convert_fusion.7 = bf16[512,2048]{1,0:T(8,128)(2,1)} fusion(bf16[2048,2816]{1,0:T(8,128)(2,1)} %bitcast.168, bf16[1024,2816]{1,0:T(8,128)(2,1)S(1)} %pad_maximum_fusion), kind=kOutput, calls=%fused_computation.28 | convolution fusion | flops 5906628608 | bytes 16515072 | tf_op jit(solution)/shard_map/dot_general | solution.py:29
  431.1 7.9 convolution_convert_fusion.8
  443.7 8.1 collective-permute-done.81.refs_2_
  456.5 15.8 %convolution_convert_fusion = bf16[2048,2816]{1,0:T(8,128)(2,1)S(1)} fusion(bf16[1024,2048]{1,0:T(8,128)(2,1)} %pad_maximum_fusion.2, bf16[1024,2816]{1,0:T(8,128)(2,1)} %copy-done.84), kind=kOutput, calls=%fused_computation | convolution fusion | flops 11816927232 | bytes 21495808 | tf_op jit(solution)/shard_map/dot_general | solution.py:29
  475.5 22.7 %collective-permute-done.86.refs_3_ = bf16[176,1024]{1,0:T(8,128)(2,1)S(1)} collective-permute-done((bf16[176,1024]{1,0:T(8,128)(2,1)S(1)}, bf16[176,1024]{1,0:T(8,128)(2,1)S(1)}, u32[]{:S(2)}, u32[]{:S(2)}) %collective-permute-start.86) | collective-permute-done | bytes 360480 | tf_op jit(solution)/shard_map/ppermute | solution.py:462
  510.8 18.8 %collective-permute-done.90.refs_2_ = bf16[176,1024]{1,0:T(8,128)(2,1)S(1)} collective-permute-done((bf16[176,1024]{1,0:T(8,128)(2,1)S(1)}, bf16[176,1024]{1,0:T(8,128)(2,1)S(1)}, u32[]{:S(2)}, u32[]{:S(2)}) %collective-permute-start.90) | collective-permute-done | bytes 360480 | tf_op jit(solution)/shard_map/ppermute | solution.py:462
  541.3 9.8 %collective-permute-done.93.refs_2_ = bf16[2,64,2816]{2,1,0:T(8,128)(2,1)S(1)} collective-permute-done((bf16[2,64,2816]{2,1,0:T(8,128)(2,1)S(1)}, bf16[2,64,2816]{2,1,0:T(8,128)(2,1)S(1)}, u32[]{:S(2)}, u32[]{:S(2)}) %collective-permute-start.93) | collective-permute-done | bytes 720928 | tf_op jit(solution)/shard_map/ppermute | solution.py:462
  555.4 14.4 %mix_back.1 = bf16[1024,1664]{1,0:T(8,128)(2,1)S(1)} custom-call(s32[4]{0:T(128)S(1)} %copy-done.59, f32[1024,1664]{1,0:T(8,128)S(1)} %bitcast.166, bf16[1024,512]{1,0:T(8,128)(2,1)S(1)} %convolution_convert_fusion.13.grad_ref), custom_call_target="tpu_custom_call" | custom-call | flops 2000000000 | bytes 10000000 | tf_op jit(solution)/shard_map/mix_back/pallas_call | solution.py:125
  574.3 8.2 %convolution_convert_fusion.1 = bf16[2048,1664]{1,0:T(8,128)(2,1)S(1)} fusion(bf16[1024,2048]{1,0:T(8,128)(2,1)S(1)} %copy-done.85, bf16[1024,1664]{1,0:T(8,128)(2,1)S(1)} %mix_back.1), kind=kOutput, calls=%fused_computation.1 | convolution fusion | flops 6982729728 | bytes 14417920 | tf_op jit(solution)/shard_map/dot_general | solution.py:29
  618.2 9.2 %collective-permute-done.100.refs_3_ = bf16[2,64,2816]{2,1,0:T(8,128)(2,1)S(1)} collective-permute-done((bf16[2,64,2816]{2,1,0:T(8,128)(2,1)}, bf16[2,64,2816]{2,1,0:T(8,128)(2,1)S(1)}, u32[]{:S(2)}, u32[]{:S(2)}) %collective-permute-start.100) | collective-permute-done | bytes 720928 | tf_op jit(solution)/shard_map/ppermute | solution.py:462
  645.3 15.6 %collective-permute-done.108.refs_2_ = bf16[2,64,1664]{2,1,0:T(8,128)(2,1)S(1)} collective-permute-done((bf16[2,64,1664]{2,1,0:T(8,128)(2,1)S(1)}, bf16[2,64,1664]{2,1,0:T(8,128)(2,1)S(1)}, u32[]{:S(2)}, u32[]{:S(2)}) %collective-permute-start.108) | collective-permute-done | bytes 426016 | tf_op jit(solution)/shard_map/ppermute | solution.py:462
  707.4 8.0 collective-permute-done.148.refs_2_
  787.1 8.0 collective-permute-done.142.d
  (729 shorter events, 443.7 us)
Async XLA Ops:
  32.9 27.4 %collective-permute-start.5 = (bf16[256,2048]{1,0:T(8,128)(2,1)S(1)}, bf16[256,2048]{1,0:T(8,128)(2,1)S(1)}, u32[]{:S(2)}, u32[]{:S(2)}) collective-permute-start(bf16[256,2048]{1,0:T(8,128)(2,1)S(1)} %add_convert_fusion.5), channel_id=1, source_target_pairs={{0,16},{8,24},{16,0},{24,8},{1,17},{9,25},{17,1},{25,9},{2,18},{10... | collective-permute-start | bytes 3145736 | tf_op jit(solution)/shard_map/ppermute | solution.py:144
  62.0 78.0 %collective-permute-start.6 = (bf16[512,2048]{1,0:T(8,128)(2,1)}, bf16[512,2048]{1,0:T(8,128)(2,1)}, u32[]{:S(2)}, u32[]{:S(2)}) collective-permute-start(bf16[512,2048]{1,0:T(8,128)(2,1)} %pad_maximum_fusion.5), channel_id=1, source_target_pairs={{0,8},{8,0},{16,24},{24,16},{1,9},{9,1},{17,25},{25,17},{2,10},{10... | collective-permute-start | bytes 6291464 | tf_op jit(solution)/shard_map/ppermute | solution.py:144
  113.7 25.1 %collective-permute-start.22 = (bf16[2,64,1664]{2,1,0:T(8,128)(2,1)}, bf16[2,64,1664]{2,1,0:T(8,128)(2,1)}, u32[]{:S(2)}, u32[]{:S(2)}) collective-permute-start(bf16[2,64,1664]{2,1,0:T(8,128)(2,1)} %collective-permute-done.21.refs_13_), channel_id=1, source_target_pairs={{2,0},{4,2},{6,4},{7,6},{5,7},{3,5},{1,3},{0,1},{10,8},{12,10},{14... | collective-permute-start | bytes 1277960 | tf_op jit(solution)/shard_map/ppermute | solution.py:420
  149.9 29.0 %collective-permute-start.43 = (bf16[2,64,2816]{2,1,0:T(8,128)(2,1)S(1)}, bf16[2,64,2816]{2,1,0:T(8,128)(2,1)S(1)}, u32[]{:S(2)}, u32[]{:S(2)}) collective-permute-start(bf16[2,64,2816]{2,1,0:T(8,128)(2,1)S(1)} %collective-permute-done.42.refs_1_), channel_id=1, source_target_pairs={{0,2},{2,4},{4,6},{6,7},{7,5},{5,3},{3,1},{1,0},{8,10},{10,12},{12... | collective-permute-start | bytes 2162696 | tf_op jit(solution)/shard_map/ppermute | solution.py:420
  201.9 34.4 %collective-permute-start.40 = (bf16[256,2048]{1,0:T(8,128)(2,1)}, bf16[256,2048]{1,0:T(8,128)(2,1)}, u32[]{:S(2)}, u32[]{:S(2)}) collective-permute-start(bf16[256,2048]{1,0:T(8,128)(2,1)} %add_convert_fusion.4), channel_id=1, source_target_pairs={{0,16},{8,24},{16,0},{24,8},{1,17},{9,25},{17,1},{25,9},{2,18},{10... | collective-permute-start | bytes 3145736 | tf_op jit(solution)/shard_map/ppermute | solution.py:144
  204.9 31.4 %collective-permute-start.38 = (bf16[256,2048]{1,0:T(8,128)(2,1)}, bf16[256,2048]{1,0:T(8,128)(2,1)}, u32[]{:S(2)}, u32[]{:S(2)}) collective-permute-start(bf16[256,2048]{1,0:T(8,128)(2,1)} %slice.283), channel_id=1, source_target_pairs={{0,8},{8,0},{16,24},{24,16},{1,9},{9,1},{17,25},{25,17},{2,10},{10... | collective-permute-start | bytes 3145736 | tf_op jit(solution)/shard_map/ppermute | solution.py:144
  224.8 32.6 %collective-permute-start.63 = (bf16[256,2048]{1,0:T(8,128)(2,1)S(1)}, bf16[256,2048]{1,0:T(8,128)(2,1)S(1)}, u32[]{:S(2)}, u32[]{:S(2)}) collective-permute-start(bf16[256,2048]{1,0:T(8,128)(2,1)S(1)} %copy-done.81), channel_id=1, source_target_pairs={{0,16},{8,24},{16,0},{24,8},{1,17},{9,25},{17,1},{25,9},{2,18},{10... | collective-permute-start | bytes 3145736 | tf_op jit(solution)/shard_map/ppermute | solution.py:144
  238.8 47.2 %collective-permute-start.47 = (bf16[256,2048]{1,0:T(8,128)(2,1)S(1)}, bf16[256,2048]{1,0:T(8,128)(2,1)S(1)}, u32[]{:S(2)}, u32[]{:S(2)}) collective-permute-start(bf16[256,2048]{1,0:T(8,128)(2,1)S(1)} %multiply_convert_fusion.2), channel_id=1, source_target_pairs={{0,16},{8,24},{16,0},{24,8},{1,17},{9,25},{17,1},{25,9},{2,18},{10... | collective-permute-start | bytes 3145736 | tf_op jit(solution)/shard_map/ppermute | solution.py:144
  255.8 30.2 %collective-permute-start.48 = (bf16[2,64,2816]{2,1,0:T(8,128)(2,1)}, bf16[2,64,2816]{2,1,0:T(8,128)(2,1)S(1)}, u32[]{:S(2)}, u32[]{:S(2)}) collective-permute-start(bf16[2,64,2816]{2,1,0:T(8,128)(2,1)} %collective-permute-done.46.refs_5_), channel_id=1, source_target_pairs={{0,2},{2,4},{4,6},{6,7},{7,5},{5,3},{3,1},{1,0},{8,10},{10,12},{12... | collective-permute-start | bytes 2162696 | tf_op jit(solution)/shard_map/ppermute | solution.py:420
  257.6 57.3 %collective-permute-start.64 = (bf16[512,2048]{1,0:T(8,128)(2,1)S(1)}, bf16[512,2048]{1,0:T(8,128)(2,1)S(1)}, u32[]{:S(2)}, u32[]{:S(2)}) collective-permute-start(bf16[512,2048]{1,0:T(8,128)(2,1)S(1)} %pad_maximum_fusion.7), channel_id=1, source_target_pairs={{0,8},{8,0},{16,24},{24,16},{1,9},{9,1},{17,25},{25,17},{2,10},{10... | collective-permute-start | bytes 6291464 | tf_op jit(solution)/shard_map/ppermute | solution.py:144
  286.2 61.5 %collective-permute-start.51 = (bf16[512,2048]{1,0:T(8,128)(2,1)S(1)}, bf16[512,2048]{1,0:T(8,128)(2,1)S(1)}, u32[]{:S(2)}, u32[]{:S(2)}) collective-permute-start(bf16[512,2048]{1,0:T(8,128)(2,1)S(1)} %pad_maximum_fusion.6), channel_id=1, source_target_pairs={{0,8},{8,0},{16,24},{24,16},{1,9},{9,1},{17,25},{25,17},{2,10},{10... | collective-permute-start | bytes 6291464 | tf_op jit(solution)/shard_map/ppermute | solution.py:144
  286.3 26.5 %collective-permute-start.60 = (bf16[2,64,2816]{2,1,0:T(8,128)(2,1)S(1)}, bf16[2,64,2816]{2,1,0:T(8,128)(2,1)S(1)}, u32[]{:S(2)}, u32[]{:S(2)}) collective-permute-start(bf16[2,64,2816]{2,1,0:T(8,128)(2,1)S(1)} %collective-permute-done.59.refs_13_), channel_id=1, source_target_pairs={{2,0},{4,2},{6,4},{7,6},{5,7},{3,5},{1,3},{0,1},{10,8},{12,10},{14... | collective-permute-start | bytes 2162696 | tf_op jit(solution)/shard_map/ppermute | solution.py:420
  286.7 25.9 %collective-permute-start.69 = (bf16[176,1024]{1,0:T(8,128)(2,1)S(1)}, bf16[176,1024]{1,0:T(8,128)(2,1)S(1)}, u32[]{:S(2)}, u32[]{:S(2)}) collective-permute-start(bf16[176,1024]{1,0:T(8,128)(2,1)S(1)} %get-tuple-element.256.refs_8_), channel_id=1, source_target_pairs={{2,0},{4,2},{6,4},{7,6},{5,7},{3,5},{1,3},{0,1},{10,8},{12,10},{14... | collective-permute-start | bytes 1081352 | tf_op jit(solution)/shard_map/ppermute | solution.py:420
  312.9 26.5 %collective-permute-start.61 = (bf16[2,64,2816]{2,1,0:T(8,128)(2,1)S(1)}, bf16[2,64,2816]{2,1,0:T(8,128)(2,1)S(1)}, u32[]{:S(2)}, u32[]{:S(2)}) collective-permute-start(bf16[2,64,2816]{2,1,0:T(8,128)(2,1)S(1)} %collective-permute-done.60.refs_14_), channel_id=1, source_target_pairs={{2,0},{4,2},{6,4},{7,6},{5,7},{3,5},{1,3},{0,1},{10,8},{12,10},{14... | collective-permute-start | bytes 2162696 | tf_op jit(solution)/shard_map/ppermute | solution.py:420
  384.2 56.3 %collective-permute-start.79 = (bf16[176,1024]{1,0:T(8,128)(2,1)S(1)}, bf16[176,1024]{1,0:T(8,128)(2,1)S(1)}, u32[]{:S(2)}, u32[]{:S(2)}) collective-permute-start(bf16[176,1024]{1,0:T(8,128)(2,1)S(1)} %get-tuple-element.263), channel_id=1, source_target_pairs={{0,2},{2,4},{4,6},{6,7},{7,5},{5,3},{3,1},{1,0},{8,10},{10,12},{12... | collective-permute-start | bytes 1081352 | tf_op jit(solution)/shard_map/ppermute | solution.py:462
  385.8 54.7 %collective-permute-start.80 = (bf16[176,1024]{1,0:T(8,128)(2,1)S(1)}, bf16[176,1024]{1,0:T(8,128)(2,1)S(1)}, u32[]{:S(2)}, u32[]{:S(2)}) collective-permute-start(bf16[176,1024]{1,0:T(8,128)(2,1)S(1)} %get-tuple-element.264), channel_id=1, source_target_pairs={{2,0},{4,2},{6,4},{7,6},{5,7},{3,5},{1,3},{0,1},{10,8},{12,10},{14... | collective-permute-start | bytes 1081352 | tf_op jit(solution)/shard_map/ppermute | solution.py:462
  440.2 59.8 %collective-permute-start.76 = (bf16[256,2048]{1,0:T(8,128)(2,1)}, bf16[256,2048]{1,0:T(8,128)(2,1)}, u32[]{:S(2)}, u32[]{:S(2)}) collective-permute-start(bf16[256,2048]{1,0:T(8,128)(2,1)} %slice.296), channel_id=1, source_target_pairs={{0,8},{8,0},{16,24},{24,16},{1,9},{9,1},{17,25},{25,17},{2,10},{10... | collective-permute-start | bytes 3145736 | tf_op jit(solution)/shard_map/ppermute | solution.py:144
  455.9 44.0 %collective-permute-start.78 = (bf16[256,2048]{1,0:T(8,128)(2,1)S(1)}, bf16[256,2048]{1,0:T(8,128)(2,1)}, u32[]{:S(2)}, u32[]{:S(2)}) collective-permute-start(bf16[256,2048]{1,0:T(8,128)(2,1)S(1)} %add_convert_fusion.3), channel_id=1, source_target_pairs={{0,16},{8,24},{16,0},{24,8},{1,17},{9,25},{17,1},{25,9},{2,18},{10... | collective-permute-start | bytes 3145736 | tf_op jit(solution)/shard_map/ppermute | solution.py:144
  472.9 26.0 %collective-permute-start.83 = (bf16[2,64,2816]{2,1,0:T(8,128)(2,1)S(1)}, bf16[2,64,2816]{2,1,0:T(8,128)(2,1)S(1)}, u32[]{:S(2)}, u32[]{:S(2)}) collective-permute-start(bf16[2,64,2816]{2,1,0:T(8,128)(2,1)S(1)} %get-tuple-element.274), channel_id=1, source_target_pairs={{0,2},{2,4},{4,6},{6,7},{7,5},{5,3},{3,1},{1,0},{8,10},{10,12},{12... | collective-permute-start | bytes 2162696 | tf_op jit(solution)/shard_map/ppermute | solution.py:462
  505.2 27.0 %collective-permute-start.87 = (bf16[256,2048]{1,0:T(8,128)(2,1)S(1)}, bf16[256,2048]{1,0:T(8,128)(2,1)S(1)}, u32[]{:S(2)}, u32[]{:S(2)}) collective-permute-start(bf16[256,2048]{1,0:T(8,128)(2,1)S(1)} %fusion.37), channel_id=1, source_target_pairs={{0,16},{8,24},{16,0},{24,8},{1,17},{9,25},{17,1},{25,9},{2,18},{10... | collective-permute-start | bytes 3145736 | tf_op jit(solution)/shard_map/ppermute | solution.py:144
  601.4 27.6 %collective-permute-start.99 = (bf16[2,64,2816]{2,1,0:T(8,128)(2,1)}, bf16[2,64,2816]{2,1,0:T(8,128)(2,1)S(1)}, u32[]{:S(2)}, u32[]{:S(2)}) collective-permute-start(bf16[2,64,2816]{2,1,0:T(8,128)(2,1)} %get-tuple-element.308), channel_id=1, source_target_pairs={{0,2},{2,4},{4,6},{6,7},{7,5},{5,3},{3,1},{1,0},{8,10},{10,12},{12... | collective-permute-start | bytes 2162696 | tf_op jit(solution)/shard_map/ppermute | solution.py:462
  601.9 25.5 %collective-permute-start.100 = (bf16[2,64,2816]{2,1,0:T(8,128)(2,1)}, bf16[2,64,2816]{2,1,0:T(8,128)(2,1)S(1)}, u32[]{:S(2)}, u32[]{:S(2)}) collective-permute-start(bf16[2,64,2816]{2,1,0:T(8,128)(2,1)} %copy-done.60), channel_id=1, source_target_pairs={{2,0},{4,2},{6,4},{7,6},{5,7},{3,5},{1,3},{0,1},{10,8},{12,10},{14... | collective-permute-start | bytes 2162696 | tf_op jit(solution)/shard_map/ppermute | solution.py:462
  606.3 35.8 %collective-permute-start.111 = (bf16[256,2048]{1,0:T(8,128)(2,1)}, bf16[256,2048]{1,0:T(8,128)(2,1)}, u32[]{:S(2)}, u32[]{:S(2)}) collective-permute-start(bf16[256,2048]{1,0:T(8,128)(2,1)} %add_convert_fusion.1), channel_id=1, source_target_pairs={{0,16},{8,24},{16,0},{24,8},{1,17},{9,25},{17,1},{25,9},{2,18},{10... | collective-permute-start | bytes 3145736 | tf_op jit(solution)/shard_map/ppermute | solution.py:144
  614.8 28.8 %collective-permute-start.110 = (bf16[256,2048]{1,0:T(8,128)(2,1)S(1)}, bf16[256,2048]{1,0:T(8,128)(2,1)S(1)}, u32[]{:S(2)}, u32[]{:S(2)}) collective-permute-start(bf16[256,2048]{1,0:T(8,128)(2,1)S(1)} %slice.305), channel_id=1, source_target_pairs={{0,8},{8,0},{16,24},{24,16},{1,9},{9,1},{17,25},{25,17},{2,10},{10... | collective-permute-start | bytes 3145736 | tf_op jit(solution)/shard_map/ppermute | solution.py:144
  629.9 34.1 %collective-permute-start.102 = (bf16[2,64,2816]{2,1,0:T(8,128)(2,1)S(1)}, bf16[2,64,2816]{2,1,0:T(8,128)(2,1)S(1)}, u32[]{:S(2)}, u32[]{:S(2)}) collective-permute-start(bf16[2,64,2816]{2,1,0:T(8,128)(2,1)S(1)} %get-tuple-element.313), channel_id=1, source_target_pairs={{0,2},{2,4},{4,6},{6,7},{7,5},{5,3},{3,1},{1,0},{8,10},{10,12},{12... | collective-permute-start | bytes 2162696 | tf_op jit(solution)/shard_map/ppermute | solution.py:462
  636.8 27.2 %collective-permute-start.103 = (bf16[2,64,2816]{2,1,0:T(8,128)(2,1)S(1)}, bf16[2,64,2816]{2,1,0:T(8,128)(2,1)S(1)}, u32[]{:S(2)}, u32[]{:S(2)}) collective-permute-start(bf16[2,64,2816]{2,1,0:T(8,128)(2,1)S(1)} %get-tuple-element.316), channel_id=1, source_target_pairs={{2,0},{4,2},{6,4},{7,6},{5,7},{3,5},{1,3},{0,1},{10,8},{12,10},{14... | collective-permute-start | bytes 2162696 | tf_op jit(solution)/shard_map/ppermute | solution.py:462
  699.7 41.3 %collective-permute-start.120 = (bf16[256,2048]{1,0:T(8,128)(2,1)S(1)}, bf16[256,2048]{1,0:T(8,128)(2,1)S(1)}, u32[]{:S(2)}, u32[]{:S(2)}) collective-permute-start(bf16[256,2048]{1,0:T(8,128)(2,1)S(1)} %add_convert_fusion), channel_id=1, source_target_pairs={{0,16},{8,24},{16,0},{24,8},{1,17},{9,25},{17,1},{25,9},{2,18},{10... | collective-permute-start | bytes 3145736 | tf_op jit(solution)/shard_map/ppermute | solution.py:144
  704.0 38.1 %collective-permute-start.118 = (bf16[256,2048]{1,0:T(8,128)(2,1)S(1)}, bf16[256,2048]{1,0:T(8,128)(2,1)S(1)}, u32[]{:S(2)}, u32[]{:S(2)}) collective-permute-start(bf16[256,2048]{1,0:T(8,128)(2,1)S(1)} %slice.307), channel_id=1, source_target_pairs={{0,8},{8,0},{16,24},{24,16},{1,9},{9,1},{17,25},{25,17},{2,10},{10... | collective-permute-start | bytes 3145736 | tf_op jit(solution)/shard_map/ppermute | solution.py:144
  726.3 45.7 %collective-permute-start.150 = (bf16[176,1024]{1,0:T(8,128)(2,1)S(1)}, bf16[176,1024]{1,0:T(8,128)(2,1)S(1)}, u32[]{:S(2)}, u32[]{:S(2)}) collective-permute-start(bf16[176,1024]{1,0:T(8,128)(2,1)S(1)} %get-tuple-element.402), channel_id=1, source_target_pairs={{0,2},{2,4},{4,6},{6,7},{7,5},{5,3},{3,1},{1,0},{8,10},{10,12},{12... | collective-permute-start | bytes 1081352 | tf_op jit(solution)/shard_map/ppermute | solution.py:462
  749.5 25.2 %collective-permute-start.151 = (bf16[176,1024]{1,0:T(8,128)(2,1)S(1)}, bf16[176,1024]{1,0:T(8,128)(2,1)S(1)}, u32[]{:S(2)}, u32[]{:S(2)}) collective-permute-start(bf16[176,1024]{1,0:T(8,128)(2,1)S(1)} %get-tuple-element.403), channel_id=1, source_target_pairs={{2,0},{4,2},{6,4},{7,6},{5,7},{3,5},{1,3},{0,1},{10,8},{12,10},{14... | collective-permute-start | bytes 1081352 | tf_op jit(solution)/shard_map/ppermute | solution.py:462
  776.0 34.1 %collective-permute-start.152 = (bf16[176,1024]{1,0:T(8,128)(2,1)S(1)}, bf16[176,1024]{1,0:T(8,128)(2,1)S(1)}, u32[]{:S(2)}, u32[]{:S(2)}) collective-permute-start(bf16[176,1024]{1,0:T(8,128)(2,1)S(1)} %get-tuple-element.404), channel_id=1, source_target_pairs={{0,2},{2,4},{4,6},{6,7},{7,5},{5,3},{3,1},{1,0},{8,10},{10,12},{12... | collective-permute-start | bytes 1081352 | tf_op jit(solution)/shard_map/ppermute | solution.py:462
  779.2 31.0 %collective-permute-start.153 = (bf16[176,1024]{1,0:T(8,128)(2,1)S(1)}, bf16[176,1024]{1,0:T(8,128)(2,1)S(1)}, u32[]{:S(2)}, u32[]{:S(2)}) collective-permute-start(bf16[176,1024]{1,0:T(8,128)(2,1)S(1)} %get-tuple-element.405), channel_id=1, source_target_pairs={{2,0},{4,2},{6,4},{7,6},{5,7},{3,5},{1,3},{0,1},{10,8},{12,10},{14... | collective-permute-start | bytes 1081352 | tf_op jit(solution)/shard_map/ppermute | solution.py:462
  (269 other events, 3085.7 us)

commit v5 on v3

--- a/solution.py
+++ b/solution.py
@@ -190,6 +190,7 @@
 SMEM = pl.BlockSpec(memory_space=pltpu.SMEM)
 VMEM = pl.BlockSpec(memory_space=pltpu.VMEM)
 ANY = pl.BlockSpec(memory_space=pl.ANY)
+HBM = pl.BlockSpec(memory_space=pltpu.HBM)
 
 
 def params(mib):
@@ -326,7 +327,7 @@
 
     return pl.pallas_call(
         body,
-        in_specs=[SMEM] + [ANY] * (2 * size),
+        in_specs=[SMEM] + [ANY if grouped else HBM] * (2 * size),
         out_specs=ANY,
         out_shape=jax.ShapeDtypeStruct(shape, low),
         scratch_shapes=[pltpu.SemaphoreType.DMA(((4 if grouped else 2) * size,))],

time: 819 us -> 819 us (level)
  no operation moved by 1% of the time
where the time goes in v5:
time: 819 us; the launch traced here: 810 us
  waiting for transfers between devices  350 us (43%)
  starting transfers between devices  146 us (18%)
  matrix products  120 us (15%)
  Pallas kernels  80.8 us (10%)
  other arithmetic  54.6 us (7%)
  local copies, waits for them, and re-layouts  54.2 us (7%)
    ppermute x56, waiting for transfers between devices, step(): held.append(lax.ppermute(value, 'wide', round_ring(CYCLES[self.size], d)))  177 us
    ppermute x56, waiting for transfers between devices, step(): lax.ppermute(sums[d], 'wide', round_ring(cycle, d))  127 us
    dot_general x16, matrix products, dot(): lax.dot_general(left, right, (((over_left,), (over_right,)), ((), ())), p...  120 us
    ppermute x56, starting transfers between devices, step(): lax.ppermute(sums[d], 'wide', round_ring(cycle, d))  59.9 us
    ppermute x56, starting transfers between devices, step(): held.append(lax.ppermute(value, 'wide', round_ring(CYCLES[self.size], d)))  57.5 us
    unnamed x333, local copies, waits for them, and re-layouts  40.6 us
    ppermute x32, waiting for transfers between devices, swap(): return lax.ppermute(value, 'grp', [(i, i ^ over) for i in range(GROUP)])  35 us
    pallas_call x32, Pallas kernels, pick_add(): pl.pallas_call(body, grid_spec=pltpu.PrefetchScalarGridSpec(num_scalar_pr...  32.9 us
  transfers between devices with their start and end apart: 154, of which 61 were waited for; matrix products, arithmetic and copies ran while one was open for 22% of the time, Pallas kernels for 9%

profile of v5, /device:TPU:0, one launch (start us, length us, event | category | flops | bytes accessed | tf_op | source)
XLA Modules:
  0.0 810.0 jit_solution(16588249885155066393)
XLA Ops:
  22.8 7.9 collective-permute-done.4
  36.7 8.8 %collective-permute-done.8.refs_1_ = bf16[2,64,1664]{2,1,0:T(8,128)(2,1)S(1)} collective-permute-done((bf16[2,64,1664]{2,1,0:T(8,128)(2,1)S(1)}, bf16[2,64,1664]{2,1,0:T(8,128)(2,1)S(1)}, u32[]{:S(2)}, u32[]{:S(2)}) %collective-permute-start.8) | collective-permute-done | bytes 426016 | tf_op jit(solution)/shard_map/ppermute | solution.py:418
  48.1 10.2 %collective-permute-done.9.refs_2_ = bf16[2,64,1664]{2,1,0:T(8,128)(2,1)S(1)} collective-permute-done((bf16[2,64,1664]{2,1,0:T(8,128)(2,1)S(1)}, bf16[2,64,1664]{2,1,0:T(8,128)(2,1)S(1)}, u32[]{:S(2)}, u32[]{:S(2)}) %collective-permute-start.9) | collective-permute-done | bytes 426016 | tf_op jit(solution)/shard_map/ppermute | solution.py:418
  81.2 8.8 %collective-permute-done.11.refs_4_ = bf16[2,64,1664]{2,1,0:T(8,128)(2,1)S(1)} collective-permute-done((bf16[2,64,1664]{2,1,0:T(8,128)(2,1)S(1)}, bf16[2,64,1664]{2,1,0:T(8,128)(2,1)S(1)}, u32[]{:S(2)}, u32[]{:S(2)}) %collective-permute-start.11) | collective-permute-done | bytes 426016 | tf_op jit(solution)/shard_map/ppermute | solution.py:418
  141.5 8.9 %collective-permute-done.14.refs_7_ = bf16[2,64,1664]{2,1,0:T(8,128)(2,1)S(1)} collective-permute-done((bf16[2,64,1664]{2,1,0:T(8,128)(2,1)}, bf16[2,64,1664]{2,1,0:T(8,128)(2,1)S(1)}, u32[]{:S(2)}, u32[]{:S(2)}) %collective-permute-start.14) | collective-permute-done | bytes 426016 | tf_op jit(solution)/shard_map/ppermute | solution.py:418
  153.2 9.9 %place.4 = bf16[4,8,64,1664]{3,2,1,0:T(8,128)(2,1)S(1)} custom-call(s32[17]{0:T(128)S(1)} %pad_add_fusion.2.table_ref, bf16[2,64,1664]{2,1,0:T(8,128)(2,1)S(1)} %pad_maximum_fusion.11.refs_0_, bf16[2,64,1664]{2,1,0:T(8,128)(2,1)S(1)} %copy-done.24, bf16[2,64,1664]{2,1,0:T(8,128)(2,1)S(1)} %copy-done.28, bf16[2,64,1664]{2,1,0:T(8,128)(2,1)S(1)} %copy-done.32, ...), custom_call_target="tpu_custom_call" | custom-call | bytes 20447232 | tf_op jit(solution)/shard_map/place/pallas_call | solution.py:328
  163.2 7.7 fusion.39.pack_ref
  183.1 9.7 %collective-permute-done.52 = bf16[64,2816]{1,0:T(8,128)(2,1)S(1)} collective-permute-done((bf16[64,2816]{1,0:T(8,128)(2,1)S(1)}, bf16[64,2816]{1,0:T(8,128)(2,1)S(1)}, u32[]{:S(2)}, u32[]{:S(2)}) %collective-permute-start.52) | collective-permute-done | bytes 360480 | tf_op jit(solution)/shard_map/ppermute | solution.py:144
  206.0 12.5 %collective-permute-done.54.refs_9_ = bf16[2,64,2816]{2,1,0:T(8,128)(2,1)} collective-permute-done((bf16[2,64,2816]{2,1,0:T(8,128)(2,1)S(1)}, bf16[2,64,2816]{2,1,0:T(8,128)(2,1)}, u32[]{:S(2)}, u32[]{:S(2)}) %collective-permute-start.54) | collective-permute-done | bytes 720928 | tf_op jit(solution)/shard_map/ppermute | solution.py:418
  226.4 10.8 %collective-permute-done.55.refs_10_ = bf16[2,64,2816]{2,1,0:T(8,128)(2,1)} collective-permute-done((bf16[2,64,2816]{2,1,0:T(8,128)(2,1)}, bf16[2,64,2816]{2,1,0:T(8,128)(2,1)}, u32[]{:S(2)}, u32[]{:S(2)}) %collective-permute-start.55) | collective-permute-done | bytes 720928 | tf_op jit(solution)/shard_map/ppermute | solution.py:418
  242.8 12.5 %collective-permute-done.56.refs_11_ = bf16[2,64,2816]{2,1,0:T(8,128)(2,1)S(1)} collective-permute-done((bf16[2,64,2816]{2,1,0:T(8,128)(2,1)}, bf16[2,64,2816]{2,1,0:T(8,128)(2,1)S(1)}, u32[]{:S(2)}, u32[]{:S(2)}) %collective-permute-start.56) | collective-permute-done | bytes 720928 | tf_op jit(solution)/shard_map/ppermute | solution.py:418
  259.5 12.5 %collective-permute-done.57.refs_12_ = bf16[2,64,2816]{2,1,0:T(8,128)(2,1)S(1)} collective-permute-done((bf16[2,64,2816]{2,1,0:T(8,128)(2,1)S(1)}, bf16[2,64,2816]{2,1,0:T(8,128)(2,1)S(1)}, u32[]{:S(2)}, u32[]{:S(2)}) %collective-permute-start.57) | collective-permute-done | bytes 720928 | tf_op jit(solution)/shard_map/ppermute | solution.py:418
  273.9 14.4 %collective-permute-done.58.refs_13_ = bf16[2,64,2816]{2,1,0:T(8,128)(2,1)S(1)} collective-permute-done((bf16[2,64,2816]{2,1,0:T(8,128)(2,1)S(1)}, bf16[2,64,2816]{2,1,0:T(8,128)(2,1)S(1)}, u32[]{:S(2)}, u32[]{:S(2)}) %collective-permute-start.58) | collective-permute-done | bytes 720928 | tf_op jit(solution)/shard_map/ppermute | solution.py:418
  288.9 15.7 %collective-permute-done.59.refs_14_ = bf16[2,64,2816]{2,1,0:T(8,128)(2,1)S(1)} collective-permute-done((bf16[2,64,2816]{2,1,0:T(8,128)(2,1)S(1)}, bf16[2,64,2816]{2,1,0:T(8,128)(2,1)S(1)}, u32[]{:S(2)}, u32[]{:S(2)}) %collective-permute-start.59) | collective-permute-done | bytes 720928 | tf_op jit(solution)/shard_map/ppermute | solution.py:418
  309.0 19.7 %collective-permute-done.69.refs_9_ = bf16[176,1024]{1,0:T(8,128)(2,1)S(1)} collective-permute-done((bf16[176,1024]{1,0:T(8,128)(2,1)S(1)}, bf16[176,1024]{1,0:T(8,128)(2,1)S(1)}, u32[]{:S(2)}, u32[]{:S(2)}) %collective-permute-start.69) | collective-permute-done | bytes 360480 | tf_op jit(solution)/shard_map/ppermute | solution.py:418
  344.1 14.1 %fusion.47 = f32[1024,2816]{1,0:T(8,128)S(1)} fusion(bf16[1024,2048]{1,0:T(8,128)(2,1)} %pad_maximum_fusion.2, bf16[2048,2816]{1,0:T(8,128)(2,1)S(1)} %bitcast.169), kind=kOutput, calls=%fused_computation.148 | convolution fusion | flops 11811160064 | bytes 27262976 | tf_op jit(solution)/shard_map/dot_general | solution.py:29
  377.0 8.4 %collective-permute-done.74.refs_14_ = bf16[176,1024]{1,0:T(8,128)(2,1)S(1)} collective-permute-done((bf16[176,1024]{1,0:T(8,128)(2,1)S(1)}, bf16[176,1024]{1,0:T(8,128)(2,1)S(1)}, u32[]{:S(2)}, u32[]{:S(2)}) %collective-permute-start.74) | collective-permute-done | bytes 360480 | tf_op jit(solution)/shard_map/ppermute | solution.py:418
  397.0 15.9 %fusion.2 = (bf16[1024,1408]{1,0:T(8,128)(2,1)}, bf16[1024,1408]{1,0:T(8,128)(2,1)}) fusion(f32[1024,2816]{1,0:T(8,128)} %copy-done.83, bf16[1408,2048]{1,0:T(8,128)(2,1)} %bitcast.177, bf16[256,2048]{1,0:T(8,128)(2,1)} %copy-done.103, bf16[256,2048]{1,0:T(8,128)(2,1)} %copy-done.100, bf16[256,2048]{1,0:T(8,128)(2,1)} %copy-done.102, ...), kind=kOutput, calls=%fused_computation.7 | convolution fusion | flops 5943984128 | bytes 27262976 | tf_op jit(solution)/shard_map/dot_general | solution.py:29
  418.6 10.0 %convolution_convert_fusion.8 = bf16[512,2048]{1,0:T(8,128)(2,1)S(1)} fusion(bf16[2048,2816]{1,0:T(8,128)(2,1)} %bitcast.170, bf16[1024,2816]{1,0:T(8,128)(2,1)} %pad_maximum_fusion), kind=kOutput, calls=%fused_computation.29 | convolution fusion | flops 5906628608 | bytes 16515072 | tf_op jit(solution)/shard_map/dot_general | solution.py:29
  428.9 8.8 %convolution_convert_fusion.7 = bf16[512,2048]{1,0:T(8,128)(2,1)} fusion(bf16[2048,2816]{1,0:T(8,128)(2,1)S(1)} %bitcast.173, bf16[1024,2816]{1,0:T(8,128)(2,1)} %pad_maximum_fusion), kind=kOutput, calls=%fused_computation.28 | convolution fusion | flops 5906628608 | bytes 16515072 | tf_op jit(solution)/shard_map/dot_general | solution.py:29
  456.2 15.8 %convolution_convert_fusion = bf16[2048,2816]{1,0:T(8,128)(2,1)S(1)} fusion(bf16[1024,2048]{1,0:T(8,128)(2,1)} %pad_maximum_fusion.2, bf16[1024,2816]{1,0:T(8,128)(2,1)} %pad_maximum_fusion), kind=kOutput, calls=%fused_computation | convolution fusion | flops 11816927232 | bytes 21495808 | tf_op jit(solution)/shard_map/dot_general | solution.py:29
  475.3 23.1 %collective-permute-done.84.refs_3_ = bf16[176,1024]{1,0:T(8,128)(2,1)S(1)} collective-permute-done((bf16[176,1024]{1,0:T(8,128)(2,1)S(1)}, bf16[176,1024]{1,0:T(8,128)(2,1)S(1)}, u32[]{:S(2)}, u32[]{:S(2)}) %collective-permute-start.84) | collective-permute-done | bytes 360480 | tf_op jit(solution)/shard_map/ppermute | solution.py:460
  510.4 18.7 %collective-permute-done.87.refs_2_ = bf16[176,1024]{1,0:T(8,128)(2,1)S(1)} collective-permute-done((bf16[176,1024]{1,0:T(8,128)(2,1)S(1)}, bf16[176,1024]{1,0:T(8,128)(2,1)S(1)}, u32[]{:S(2)}, u32[]{:S(2)}) %collective-permute-start.87) | collective-permute-done | bytes 360480 | tf_op jit(solution)/shard_map/ppermute | solution.py:460
  542.1 9.7 %collective-permute-done.91.refs_2_ = bf16[2,64,2816]{2,1,0:T(8,128)(2,1)S(1)} collective-permute-done((bf16[2,64,2816]{2,1,0:T(8,128)(2,1)S(1)}, bf16[2,64,2816]{2,1,0:T(8,128)(2,1)S(1)}, u32[]{:S(2)}, u32[]{:S(2)}) %collective-permute-start.91) | collective-permute-done | bytes 720928 | tf_op jit(solution)/shard_map/ppermute | solution.py:460
  555.4 14.4 %mix_back.1 = bf16[1024,1664]{1,0:T(8,128)(2,1)S(1)} custom-call(s32[4]{0:T(128)S(1)} %pad_add_fusion.1.lens_ref, f32[1024,1664]{1,0:T(8,128)S(1)} %bitcast.168, bf16[1024,512]{1,0:T(8,128)(2,1)S(1)} %convolution_convert_fusion.13.grad_ref), custom_call_target="tpu_custom_call" | custom-call | flops 2000000000 | bytes 10000000 | tf_op jit(solution)/shard_map/mix_back/pallas_call | solution.py:125
  574.2 8.1 convolution_convert_fusion.1
  617.5 9.9 %collective-permute-done.100.refs_3_ = bf16[2,64,2816]{2,1,0:T(8,128)(2,1)S(1)} collective-permute-done((bf16[2,64,2816]{2,1,0:T(8,128)(2,1)}, bf16[2,64,2816]{2,1,0:T(8,128)(2,1)S(1)}, u32[]{:S(2)}, u32[]{:S(2)}) %collective-permute-start.100) | collective-permute-done | bytes 720928 | tf_op jit(solution)/shard_map/ppermute | solution.py:460
  631.2 8.8 %convolution_convert_fusion.5 = bf16[512,2048]{1,0:T(8,128)(2,1)} fusion(bf16[2048,1664]{1,0:T(8,128)(2,1)} %bitcast.176, bf16[1024,1664]{1,0:T(8,128)(2,1)} %copy-done.11), kind=kOutput, calls=%fused_computation.26 | convolution fusion | flops 3490709504 | bytes 10616832 | tf_op jit(solution)/shard_map/dot_general | solution.py:29
  649.2 9.4 %collective-permute-done.106.refs_2_ = bf16[2,64,1664]{2,1,0:T(8,128)(2,1)S(1)} collective-permute-done((bf16[2,64,1664]{2,1,0:T(8,128)(2,1)S(1)}, bf16[2,64,1664]{2,1,0:T(8,128)(2,1)S(1)}, u32[]{:S(2)}, u32[]{:S(2)}) %collective-permute-start.106) | collective-permute-done | bytes 426016 | tf_op jit(solution)/shard_map/ppermute | solution.py:460
  673.6 8.7 %collective-permute-done.112 = bf16[256,2048]{1,0:T(8,128)(2,1)} collective-permute-done((bf16[256,2048]{1,0:T(8,128)(2,1)S(1)}, bf16[256,2048]{1,0:T(8,128)(2,1)}, u32[]{:S(2)}, u32[]{:S(2)}) %collective-permute-start.112) | collective-permute-done | bytes 1048608 | tf_op jit(solution)/shard_map/ppermute | solution.py:144
  725.9 13.6 %collective-permute-done.141.refs_3_ = bf16[64,1024]{1,0:T(8,128)(2,1)S(1)} collective-permute-done((bf16[64,1024]{1,0:T(8,128)(2,1)S(1)}, bf16[64,1024]{1,0:T(8,128)(2,1)S(1)}, u32[]{:S(2)}, u32[]{:S(2)}) %collective-permute-start.141) | collective-permute-done | bytes 131104 | tf_op jit(solution)/shard_map/ppermute | solution.py:460
  777.2 10.1 %collective-permute-done.147.refs_3_ = bf16[64,1024]{1,0:T(8,128)(2,1)S(1)} collective-permute-done((bf16[64,1024]{1,0:T(8,128)(2,1)S(1)}, bf16[64,1024]{1,0:T(8,128)(2,1)S(1)}, u32[]{:S(2)}, u32[]{:S(2)}) %collective-permute-start.147) | collective-permute-done | bytes 131104 | tf_op jit(solution)/shard_map/ppermute | solution.py:460
  (766 shorter events, 428.3 us)
Async XLA Ops:
  32.9 27.4 %collective-permute-start.5 = (bf16[256,2048]{1,0:T(8,128)(2,1)S(1)}, bf16[256,2048]{1,0:T(8,128)(2,1)S(1)}, u32[]{:S(2)}, u32[]{:S(2)}) collective-permute-start(bf16[256,2048]{1,0:T(8,128)(2,1)S(1)} %add_convert_fusion.6), channel_id=1, source_target_pairs={{0,16},{8,24},{16,0},{24,8},{1,17},{9,25},{17,1},{25,9},{2,18},{10... | collective-permute-start | bytes 3145736 | tf_op jit(solution)/shard_map/ppermute | solution.py:144
  61.9 77.7 %collective-permute-start.6 = (bf16[512,2048]{1,0:T(8,128)(2,1)}, bf16[512,2048]{1,0:T(8,128)(2,1)}, u32[]{:S(2)}, u32[]{:S(2)}) collective-permute-start(bf16[512,2048]{1,0:T(8,128)(2,1)} %pad_maximum_fusion.5), channel_id=1, source_target_pairs={{0,8},{8,0},{16,24},{24,16},{1,9},{9,1},{17,25},{25,17},{2,10},{10... | collective-permute-start | bytes 6291464 | tf_op jit(solution)/shard_map/ppermute | solution.py:144
  150.4 29.5 %collective-permute-start.43 = (bf16[2,64,2816]{2,1,0:T(8,128)(2,1)S(1)}, bf16[2,64,2816]{2,1,0:T(8,128)(2,1)S(1)}, u32[]{:S(2)}, u32[]{:S(2)}) collective-permute-start(bf16[2,64,2816]{2,1,0:T(8,128)(2,1)S(1)} %collective-permute-done.42.refs_1_), channel_id=1, source_target_pairs={{0,2},{2,4},{4,6},{6,7},{7,5},{5,3},{3,1},{1,0},{8,10},{10,12},{12... | collective-permute-start | bytes 2162696 | tf_op jit(solution)/shard_map/ppermute | solution.py:418
  203.0 34.6 %collective-permute-start.40 = (bf16[256,2048]{1,0:T(8,128)(2,1)}, bf16[256,2048]{1,0:T(8,128)(2,1)}, u32[]{:S(2)}, u32[]{:S(2)}) collective-permute-start(bf16[256,2048]{1,0:T(8,128)(2,1)} %add_convert_fusion.5), channel_id=1, source_target_pairs={{0,16},{8,24},{16,0},{24,8},{1,17},{9,25},{17,1},{25,9},{2,18},{10... | collective-permute-start | bytes 3145736 | tf_op jit(solution)/shard_map/ppermute | solution.py:144
  206.0 31.7 %collective-permute-start.38 = (bf16[256,2048]{1,0:T(8,128)(2,1)}, bf16[256,2048]{1,0:T(8,128)(2,1)}, u32[]{:S(2)}, u32[]{:S(2)}) collective-permute-start(bf16[256,2048]{1,0:T(8,128)(2,1)} %slice.283), channel_id=1, source_target_pairs={{0,8},{8,0},{16,24},{24,16},{1,9},{9,1},{17,25},{25,17},{2,10},{10... | collective-permute-start | bytes 3145736 | tf_op jit(solution)/shard_map/ppermute | solution.py:144
  225.9 29.8 %collective-permute-start.62 = (bf16[256,2048]{1,0:T(8,128)(2,1)S(1)}, bf16[256,2048]{1,0:T(8,128)(2,1)S(1)}, u32[]{:S(2)}, u32[]{:S(2)}) collective-permute-start(bf16[256,2048]{1,0:T(8,128)(2,1)S(1)} %copy-done.91), channel_id=1, source_target_pairs={{0,16},{8,24},{16,0},{24,8},{1,17},{9,25},{17,1},{25,9},{2,18},{10... | collective-permute-start | bytes 3145736 | tf_op jit(solution)/shard_map/ppermute | solution.py:144
  242.2 31.3 %collective-permute-start.47 = (bf16[256,2048]{1,0:T(8,128)(2,1)S(1)}, bf16[256,2048]{1,0:T(8,128)(2,1)S(1)}, u32[]{:S(2)}, u32[]{:S(2)}) collective-permute-start(bf16[256,2048]{1,0:T(8,128)(2,1)S(1)} %multiply_convert_fusion.2), channel_id=1, source_target_pairs={{0,16},{8,24},{16,0},{24,8},{1,17},{9,25},{17,1},{25,9},{2,18},{10... | collective-permute-start | bytes 3145736 | tf_op jit(solution)/shard_map/ppermute | solution.py:144
  255.9 51.4 %collective-permute-start.63 = (bf16[512,2048]{1,0:T(8,128)(2,1)S(1)}, bf16[512,2048]{1,0:T(8,128)(2,1)S(1)}, u32[]{:S(2)}, u32[]{:S(2)}) collective-permute-start(bf16[512,2048]{1,0:T(8,128)(2,1)S(1)} %pad_maximum_fusion.7), channel_id=1, source_target_pairs={{0,8},{8,0},{16,24},{24,16},{1,9},{9,1},{17,25},{25,17},{2,10},{10... | collective-permute-start | bytes 6291464 | tf_op jit(solution)/shard_map/ppermute | solution.py:144
  273.8 67.8 %collective-permute-start.50 = (bf16[512,2048]{1,0:T(8,128)(2,1)S(1)}, bf16[512,2048]{1,0:T(8,128)(2,1)S(1)}, u32[]{:S(2)}, u32[]{:S(2)}) collective-permute-start(bf16[512,2048]{1,0:T(8,128)(2,1)S(1)} %pad_maximum_fusion.6), channel_id=1, source_target_pairs={{0,8},{8,0},{16,24},{24,16},{1,9},{9,1},{17,25},{25,17},{2,10},{10... | collective-permute-start | bytes 6291464 | tf_op jit(solution)/shard_map/ppermute | solution.py:144
  304.6 26.9 %collective-permute-start.60 = (bf16[2,64,2816]{2,1,0:T(8,128)(2,1)S(1)}, bf16[2,64,2816]{2,1,0:T(8,128)(2,1)S(1)}, u32[]{:S(2)}, u32[]{:S(2)}) collective-permute-start(bf16[2,64,2816]{2,1,0:T(8,128)(2,1)S(1)} %collective-permute-done.59.refs_14_), channel_id=1, source_target_pairs={{2,0},{4,2},{6,4},{7,6},{5,7},{3,5},{1,3},{0,1},{10,8},{12,10},{14... | collective-permute-start | bytes 2162696 | tf_op jit(solution)/shard_map/ppermute | solution.py:418
  305.2 26.3 %collective-permute-start.51 = (bf16[2,64,2816]{2,1,0:T(8,128)(2,1)S(1)}, bf16[2,64,2816]{2,1,0:T(8,128)(2,1)S(1)}, u32[]{:S(2)}, u32[]{:S(2)}) collective-permute-start(bf16[2,64,2816]{2,1,0:T(8,128)(2,1)S(1)} %collective-permute-done.48.refs_6_), channel_id=1, source_target_pairs={{0,2},{2,4},{4,6},{6,7},{7,5},{5,3},{3,1},{1,0},{8,10},{10,12},{12... | collective-permute-start | bytes 2162696 | tf_op jit(solution)/shard_map/ppermute | solution.py:418
  307.5 32.3 %collective-permute-start.61 = (bf16[176,1024]{1,0:T(8,128)(2,1)S(1)}, bf16[176,1024]{1,0:T(8,128)(2,1)S(1)}, u32[]{:S(2)}, u32[]{:S(2)}) collective-permute-start(bf16[176,1024]{1,0:T(8,128)(2,1)S(1)} %collective-permute-done.49.refs_1_), channel_id=1, source_target_pairs={{0,2},{2,4},{4,6},{6,7},{7,5},{5,3},{3,1},{1,0},{8,10},{10,12},{12... | collective-permute-start | bytes 1081352 | tf_op jit(solution)/shard_map/ppermute | solution.py:418
  387.5 52.9 %collective-permute-start.77 = (bf16[176,1024]{1,0:T(8,128)(2,1)S(1)}, bf16[176,1024]{1,0:T(8,128)(2,1)S(1)}, u32[]{:S(2)}, u32[]{:S(2)}) collective-permute-start(bf16[176,1024]{1,0:T(8,128)(2,1)S(1)} %get-tuple-element.227), channel_id=1, source_target_pairs={{0,2},{2,4},{4,6},{6,7},{7,5},{5,3},{3,1},{1,0},{8,10},{10,12},{12... | collective-permute-start | bytes 1081352 | tf_op jit(solution)/shard_map/ppermute | solution.py:460
  388.3 52.1 %collective-permute-start.78 = (bf16[176,1024]{1,0:T(8,128)(2,1)S(1)}, bf16[176,1024]{1,0:T(8,128)(2,1)S(1)}, u32[]{:S(2)}, u32[]{:S(2)}) collective-permute-start(bf16[176,1024]{1,0:T(8,128)(2,1)S(1)} %get-tuple-element.235), channel_id=1, source_target_pairs={{2,0},{4,2},{6,4},{7,6},{5,7},{3,5},{1,3},{0,1},{10,8},{12,10},{14... | collective-permute-start | bytes 1081352 | tf_op jit(solution)/shard_map/ppermute | solution.py:460
  440.1 60.1 %collective-permute-start.89 = (bf16[256,2048]{1,0:T(8,128)(2,1)}, bf16[256,2048]{1,0:T(8,128)(2,1)}, u32[]{:S(2)}, u32[]{:S(2)}) collective-permute-start(bf16[256,2048]{1,0:T(8,128)(2,1)} %slice.299), channel_id=1, source_target_pairs={{0,8},{8,0},{16,24},{24,16},{1,9},{9,1},{17,25},{25,17},{2,10},{10... | collective-permute-start | bytes 3145736 | tf_op jit(solution)/shard_map/ppermute | solution.py:144
  455.6 44.5 %collective-permute-start.90 = (bf16[256,2048]{1,0:T(8,128)(2,1)}, bf16[256,2048]{1,0:T(8,128)(2,1)}, u32[]{:S(2)}, u32[]{:S(2)}) collective-permute-start(bf16[256,2048]{1,0:T(8,128)(2,1)} %add_convert_fusion.4), channel_id=1, source_target_pairs={{0,16},{8,24},{16,0},{24,8},{1,17},{9,25},{17,1},{25,9},{2,18},{10... | collective-permute-start | bytes 3145736 | tf_op jit(solution)/shard_map/ppermute | solution.py:144
  472.6 26.5 %collective-permute-start.81 = (bf16[2,64,2816]{2,1,0:T(8,128)(2,1)S(1)}, bf16[2,64,2816]{2,1,0:T(8,128)(2,1)S(1)}, u32[]{:S(2)}, u32[]{:S(2)}) collective-permute-start(bf16[2,64,2816]{2,1,0:T(8,128)(2,1)S(1)} %get-tuple-element.245), channel_id=1, source_target_pairs={{0,2},{2,4},{4,6},{6,7},{7,5},{5,3},{3,1},{1,0},{8,10},{10,12},{12... | collective-permute-start | bytes 2162696 | tf_op jit(solution)/shard_map/ppermute | solution.py:460
  504.8 28.0 %collective-permute-start.93 = (bf16[256,2048]{1,0:T(8,128)(2,1)S(1)}, bf16[256,2048]{1,0:T(8,128)(2,1)S(1)}, u32[]{:S(2)}, u32[]{:S(2)}) collective-permute-start(bf16[256,2048]{1,0:T(8,128)(2,1)S(1)} %fusion.38), channel_id=1, source_target_pairs={{0,16},{8,24},{16,0},{24,8},{1,17},{9,25},{17,1},{25,9},{2,18},{10... | collective-permute-start | bytes 3145736 | tf_op jit(solution)/shard_map/ppermute | solution.py:144
  506.4 25.5 %collective-permute-start.85 = (bf16[2,64,2816]{2,1,0:T(8,128)(2,1)S(1)}, bf16[2,64,2816]{2,1,0:T(8,128)(2,1)S(1)}, u32[]{:S(2)}, u32[]{:S(2)}) collective-permute-start(bf16[2,64,2816]{2,1,0:T(8,128)(2,1)S(1)} %get-tuple-element.253), channel_id=1, source_target_pairs={{0,2},{2,4},{4,6},{6,7},{7,5},{5,3},{3,1},{1,0},{8,10},{10,12},{12... | collective-permute-start | bytes 2162696 | tf_op jit(solution)/shard_map/ppermute | solution.py:460
  601.5 25.8 %collective-permute-start.99 = (bf16[2,64,2816]{2,1,0:T(8,128)(2,1)S(1)}, bf16[2,64,2816]{2,1,0:T(8,128)(2,1)S(1)}, u32[]{:S(2)}, u32[]{:S(2)}) collective-permute-start(bf16[2,64,2816]{2,1,0:T(8,128)(2,1)S(1)} %get-tuple-element.279), channel_id=1, source_target_pairs={{0,2},{2,4},{4,6},{6,7},{7,5},{5,3},{3,1},{1,0},{8,10},{10,12},{12... | collective-permute-start | bytes 2162696 | tf_op jit(solution)/shard_map/ppermute | solution.py:460
  614.1 28.1 %collective-permute-start.104 = (bf16[2,64,1664]{2,1,0:T(8,128)(2,1)}, bf16[2,64,1664]{2,1,0:T(8,128)(2,1)}, u32[]{:S(2)}, u32[]{:S(2)}) collective-permute-start(bf16[2,64,1664]{2,1,0:T(8,128)(2,1)} %get-tuple-element.276), channel_id=1, source_target_pairs={{0,2},{2,4},{4,6},{6,7},{7,5},{5,3},{3,1},{1,0},{8,10},{10,12},{12... | collective-permute-start | bytes 1277960 | tf_op jit(solution)/shard_map/ppermute | solution.py:460
  614.8 27.5 %collective-permute-start.105 = (bf16[2,64,1664]{2,1,0:T(8,128)(2,1)}, bf16[2,64,1664]{2,1,0:T(8,128)(2,1)}, u32[]{:S(2)}, u32[]{:S(2)}) collective-permute-start(bf16[2,64,1664]{2,1,0:T(8,128)(2,1)} %get-tuple-element.286), channel_id=1, source_target_pairs={{2,0},{4,2},{6,4},{7,6},{5,7},{3,5},{1,3},{0,1},{10,8},{12,10},{14... | collective-permute-start | bytes 1277960 | tf_op jit(solution)/shard_map/ppermute | solution.py:460
  629.2 31.7 %collective-permute-start.102 = (bf16[2,64,2816]{2,1,0:T(8,128)(2,1)}, bf16[2,64,2816]{2,1,0:T(8,128)(2,1)S(1)}, u32[]{:S(2)}, u32[]{:S(2)}) collective-permute-start(bf16[2,64,2816]{2,1,0:T(8,128)(2,1)} %get-tuple-element.284), channel_id=1, source_target_pairs={{0,2},{2,4},{4,6},{6,7},{7,5},{5,3},{3,1},{1,0},{8,10},{10,12},{12... | collective-permute-start | bytes 2162696 | tf_op jit(solution)/shard_map/ppermute | solution.py:460
  629.8 32.3 %collective-permute-start.103 = (bf16[2,64,2816]{2,1,0:T(8,128)(2,1)}, bf16[2,64,2816]{2,1,0:T(8,128)(2,1)S(1)}, u32[]{:S(2)}, u32[]{:S(2)}) collective-permute-start(bf16[2,64,2816]{2,1,0:T(8,128)(2,1)} %get-tuple-element.285), channel_id=1, source_target_pairs={{2,0},{4,2},{6,4},{7,6},{5,7},{3,5},{1,3},{0,1},{10,8},{12,10},{14... | collective-permute-start | bytes 2162696 | tf_op jit(solution)/shard_map/ppermute | solution.py:460
  642.3 40.0 %collective-permute-start.111 = (bf16[256,2048]{1,0:T(8,128)(2,1)}, bf16[256,2048]{1,0:T(8,128)(2,1)}, u32[]{:S(2)}, u32[]{:S(2)}) collective-permute-start(bf16[256,2048]{1,0:T(8,128)(2,1)} %slice.309), channel_id=1, source_target_pairs={{0,8},{8,0},{16,24},{24,16},{1,9},{9,1},{17,25},{25,17},{2,10},{10... | collective-permute-start | bytes 3145736 | tf_op jit(solution)/shard_map/ppermute | solution.py:144
  663.7 25.0 %collective-permute-start.134 = (bf16[64,1024]{1,0:T(8,128)(2,1)S(1)}, bf16[64,1024]{1,0:T(8,128)(2,1)S(1)}, u32[]{:S(2)}, u32[]{:S(2)}) collective-permute-start(bf16[64,1024]{1,0:T(8,128)(2,1)S(1)} %get-tuple-element.326), channel_id=1, source_target_pairs={{0,2},{2,4},{4,6},{6,7},{7,5},{5,3},{3,1},{1,0},{8,10},{10,12},{12... | collective-permute-start | bytes 393224 | tf_op jit(solution)/shard_map/ppermute | solution.py:460
  712.3 29.0 %collective-permute-start.152 = (bf16[176,1024]{1,0:T(8,128)(2,1)S(1)}, bf16[176,1024]{1,0:T(8,128)(2,1)S(1)}, u32[]{:S(2)}, u32[]{:S(2)}) collective-permute-start(bf16[176,1024]{1,0:T(8,128)(2,1)S(1)} %get-tuple-element.350), channel_id=1, source_target_pairs={{0,2},{2,4},{4,6},{6,7},{7,5},{5,3},{3,1},{1,0},{8,10},{10,12},{12... | collective-permute-start | bytes 1081352 | tf_op jit(solution)/shard_map/ppermute | solution.py:460
  719.6 25.7 %collective-permute-start.153 = (bf16[176,1024]{1,0:T(8,128)(2,1)S(1)}, bf16[176,1024]{1,0:T(8,128)(2,1)S(1)}, u32[]{:S(2)}, u32[]{:S(2)}) collective-permute-start(bf16[176,1024]{1,0:T(8,128)(2,1)S(1)} %get-tuple-element.351), channel_id=1, source_target_pairs={{2,0},{4,2},{6,4},{7,6},{5,7},{3,5},{1,3},{0,1},{10,8},{12,10},{14... | collective-permute-start | bytes 1081352 | tf_op jit(solution)/shard_map/ppermute | solution.py:460
  722.6 33.5 %collective-permute-start.122 = (bf16[2,64,1664]{2,1,0:T(8,128)(2,1)}, bf16[2,64,1664]{2,1,0:T(8,128)(2,1)S(1)}, u32[]{:S(2)}, u32[]{:S(2)}) collective-permute-start(bf16[2,64,1664]{2,1,0:T(8,128)(2,1)} %get-tuple-element.308), channel_id=1, source_target_pairs={{0,2},{2,4},{4,6},{6,7},{7,5},{5,3},{3,1},{1,0},{8,10},{10,12},{12... | collective-permute-start | bytes 1277960 | tf_op jit(solution)/shard_map/ppermute | solution.py:460
  723.2 32.9 %collective-permute-start.123 = (bf16[2,64,1664]{2,1,0:T(8,128)(2,1)}, bf16[2,64,1664]{2,1,0:T(8,128)(2,1)S(1)}, u32[]{:S(2)}, u32[]{:S(2)}) collective-permute-start(bf16[2,64,1664]{2,1,0:T(8,128)(2,1)} %get-tuple-element.309), channel_id=1, source_target_pairs={{2,0},{4,2},{6,4},{7,6},{5,7},{3,5},{1,3},{0,1},{10,8},{12,10},{14... | collective-permute-start | bytes 1277960 | tf_op jit(solution)/shard_map/ppermute | solution.py:460
  767.4 28.8 %collective-permute-start.108 = (bf16[256,2048]{1,0:T(8,128)(2,1)}, bf16[256,2048]{1,0:T(8,128)(2,1)}, u32[]{:S(2)}, u32[]{:S(2)}) collective-permute-start(bf16[256,2048]{1,0:T(8,128)(2,1)} %slice.305), channel_id=1, source_target_pairs={{0,8},{8,0},{16,24},{24,16},{1,9},{9,1},{17,25},{25,17},{2,10},{10... | collective-permute-start | bytes 3145736 | tf_op jit(solution)/shard_map/ppermute | solution.py:144
  775.6 26.3 %collective-permute-start.110 = (bf16[256,2048]{1,0:T(8,128)(2,1)}, bf16[256,2048]{1,0:T(8,128)(2,1)S(1)}, u32[]{:S(2)}, u32[]{:S(2)}) collective-permute-start(bf16[256,2048]{1,0:T(8,128)(2,1)} %add_convert_fusion.1), channel_id=1, source_target_pairs={{0,16},{8,24},{16,0},{24,8},{1,17},{9,25},{17,1},{25,9},{2,18},{10... | collective-permute-start | bytes 3145736 | tf_op jit(solution)/shard_map/ppermute | solution.py:144
  (288 other events, 3561.1 us)
